TPU v7x, 256 devices: a whole 4x4x8 slice. The times are simulated.
256 devices in a mesh: band: 8 (over z_hi, core), grid: 32 (over z_lo, y, x).
Axes of the slice: x: 4, y: 4, z: 8 (z_hi: 4, z_lo: 2; z = z_hi * 2 + z_lo), core: 2. Of those that a mesh axis runs over, the one named last changes fastest.
Arguments:
- orbitals: float32 [16, 128, 128, 128], P('band', 'grid'), may hold values from -3 to 3
- band_owner: int32 [8], replicated, may hold values from 0 to 7
- block_index: int32 [8], replicated, may hold values from 0 to 1
Outputs:
- exchange_field: float32 [16, 128, 128, 128], P('band', 'grid')
All inputs are finite; a program needn't handle non-finite values.
Results may differ from a plain program's by a relative error of at most 0.0003.
Values sent between devices are 32-bit elements; how exact they have to be, the bound alone decides.
No kernel may reach another device: no remote copies, remote signals or barrier semaphores. Data moves between devices by JAX's collectives and lax.ppermute only.
A program may use at most 128 MiB of HBM per device.

v0:
```python
import math

import jax
import jax.numpy as jnp
from jax import lax
from jax.sharding import PartitionSpec as P

BLOCK = 1


CELL_EDGE = 46.9
EINSUM_FORMS = {1: "pxyz,xk->pkyz", 2: "pxyz,yk->pxkz", 3: "pxyz,zk->pxyk"}


def from_root(array, axis, root):
    mine = lax.axis_index(axis) == root
    return lax.psum(jnp.where(mine, array, jnp.zeros_like(array)), axis)


def dft_tables(length):
    index = jnp.arange(length, dtype=jnp.int32)
    phases = index[:, None] * index[None, :] % length
    angles = 2.0 * math.pi / length * phases.astype(jnp.float32)
    return (jnp.cos(angles), jnp.sin(angles))


def product(operand, matrix, axis_number):
    return jnp.einsum(EINSUM_FORMS[axis_number], operand, matrix, precision=lax.Precision.HIGHEST)


def forward(real_part, imag_part, axis_number):
    cosine, sine_table = dft_tables(real_part.shape[axis_number])
    if imag_part is None:
        return (
            product(real_part, cosine, axis_number),
            -product(real_part, sine_table, axis_number),
        )
    new_real = product(real_part, cosine, axis_number) + product(imag_part, sine_table, axis_number)
    new_imag = product(imag_part, cosine, axis_number) - product(real_part, sine_table, axis_number)
    return (new_real, new_imag)


def inverse(real_part, imag_part, axis_number):
    length = real_part.shape[axis_number]
    cosine, sine_table = dft_tables(length)
    new_real = (
        product(real_part, cosine, axis_number) - product(imag_part, sine_table, axis_number)
    ) / length
    new_imag = (
        product(imag_part, cosine, axis_number) + product(real_part, sine_table, axis_number)
    ) / length
    return (new_real, new_imag)


def signed_frequencies(index, length):
    return jnp.where(index < length // 2, index, index - length).astype(jnp.float32)


def local_kernel(size_x, size_cy, size_z):
    whole_y = size_cy * lax.axis_size("grid")
    y_offset = lax.axis_index("grid") * size_cy
    freq_x = signed_frequencies(jnp.arange(size_x, dtype=jnp.int32), size_x)
    freq_y = signed_frequencies(y_offset + jnp.arange(size_cy, dtype=jnp.int32), whole_y)
    freq_z = signed_frequencies(jnp.arange(size_z, dtype=jnp.int32), size_z)
    unit_scale = (2.0 * math.pi / CELL_EDGE) ** 2
    squared = unit_scale * (
        freq_x[:, None, None] ** 2 + freq_y[None, :, None] ** 2 + freq_z[None, None, :] ** 2
    )
    guarded = jnp.where(squared > 0, squared, 1.0)
    return jnp.where(squared > 0, 4.0 * math.pi / guarded, 0.0)


def poisson_solve(real_part, imag_part):
    real_part, imag_part = forward(real_part, imag_part, 3)
    real_part, imag_part = forward(real_part, imag_part, 2)
    spec_real = lax.all_to_all(real_part, "grid", split_axis=2, concat_axis=1, tiled=True)
    spec_imag = lax.all_to_all(imag_part, "grid", split_axis=2, concat_axis=1, tiled=True)
    kernel = local_kernel(spec_real.shape[1], spec_real.shape[2], spec_real.shape[3])
    spec_real, spec_imag = forward(spec_real, spec_imag, 1)
    spec_real, spec_imag = inverse(kernel * spec_real, kernel * spec_imag, 1)
    real_part = lax.all_to_all(spec_real, "grid", split_axis=1, concat_axis=2, tiled=True)
    imag_part = lax.all_to_all(spec_imag, "grid", split_axis=1, concat_axis=2, tiled=True)
    real_part, imag_part = inverse(real_part, imag_part, 2)
    return inverse(real_part, imag_part, 3)


def transform_all(real_part):

    def advance(unused_state, single):
        result_pair = poisson_solve(single[None], None)
        return (unused_state, (result_pair[0][0], result_pair[1][0]))

    _, results = lax.scan(advance, jnp.int32(0), real_part)
    return results


def potentials(densities):
    potential_real, potential_imag = transform_all(densities)
    return potential_real


def shards(orbitals, band_owner, block_index):
    local_bands = orbitals.shape[0]
    accumulated = jnp.zeros_like(orbitals)
    for round_index in range(band_owner.shape[0]):
        offset = block_index[round_index] * BLOCK
        own_block = lax.dynamic_slice_in_dim(orbitals, offset, BLOCK, 0)
        chosen = from_root(own_block, "band", band_owner[round_index])
        densities = (orbitals[:, None] * chosen[None]).reshape(
            (local_bands * BLOCK,) + orbitals.shape[1:]
        )
        potential = potentials(densities).reshape((local_bands, BLOCK) + orbitals.shape[1:])
        accumulated = accumulated - jnp.sum(chosen[None] * potential, axis=1)
    return accumulated


def solution(mesh):
    return jax.shard_map(
        shards,
        mesh=mesh,
        in_specs=(P("band", "grid", None, None), P(), P()),
        out_specs=P("band", "grid", None, None),
        check_vma=False,
    )
```

profile of v0, /device:TPU:8, one launch (start us, length us, event | category | flops | bytes accessed | tf_op | source)
XLA Modules:
  0.0 1163.3 jit_solution(16201413445383740798)
XLA Ops:
  33.1 89.0 %all-reduce.3.cloned.1.call-done = (f32[4,128,128]{2,1,0:T(8,128)}, f32[4,128,128]{2,1,0:T(8,128)}, f32[4,128,128]{2,1,0:T(8,128)}, f32[4,128,128]{2,1,0:T(8,128...) async-done(((f32[4,128,128]{2,1,0:T(8,128)}, f32[4,128,128]{2,1,0:T(8,128)}, f32[4,128,128]{2,1,0:T(8,128)}, ...) | async-done | bytes 2097168 | tf_op jit(solution)/shard_map/psum | solution.py:17
  125.9 130.8 %while.104 = (s32[]{:T(128)}, f32[2,4,128,128]{3,2,1,0:T(8,128)}, f32[2,4,128,128]{3,2,1,0:T(8,128)S(1)}, s32[]{:T(128)}, u32[]{:T(128)}, /*index=5*/s32[]{:T(128)}) while((s32[]{:T(128)}, f32[2,4,128,128]{3,2,1,0:T(8,128)}, f32[2,4,128,128]{3,2,1,0:T(8,128)S(1)}, s32[]{:T(128)}, u32[]{:T(128)}, /*index=5*/s32[]{:T(128)}) %tuple.246), condition=%wide.region_2.3_spmd, body=%wide.region_1.2_spmd.sunk | while | flops 2019755136 | bytes 28582284 | solution.py:93
  129.4 7.4 all-to-all-start.1
  181.4 7.2 all-to-all-done.2
  215.0 7.1 all-to-all-done
  245.0 7.2 all-to-all-done.2
  257.9 129.5 %while.105 = (s32[]{:T(128)}, f32[2,4,128,128]{3,2,1,0:T(8,128)}, f32[2,4,128,128]{3,2,1,0:T(8,128)S(1)}, s32[]{:T(128)}, u32[]{:T(128)}, /*index=5*/s32[]{:T(128)}, f32[2,4,128,128]{3,2,1,0:T(8,128)}) while((s32[]{:T(128)}, f32[2,4,128,128]{3,2,1,0:T(8,128)}, f32[2,4,128,128]{3,2,1,0:T(8,128)S(1)}, s32[]{:T(128)}, u32[]{:T(128)}, ...), condition=%wide.region_5.6_spmd, body=%wide.region_4.5_spmd.sunk | while | flops 2019755136 | bytes 26485112 | solution.py:93
  311.4 7.2 all-to-all-done.6
  345.0 7.7 all-to-all-done.4
  375.9 7.2 all-to-all-done.6
  388.3 127.6 %while.106 = (s32[]{:T(128)}, f32[2,4,128,128]{3,2,1,0:T(8,128)}, f32[2,4,128,128]{3,2,1,0:T(8,128)S(1)}, s32[]{:T(128)}, u32[]{:T(128)}, /*index=5*/s32[]{:T(128)}) while((s32[]{:T(128)}, f32[2,4,128,128]{3,2,1,0:T(8,128)}, f32[2,4,128,128]{3,2,1,0:T(8,128)S(1)}, s32[]{:T(128)}, u32[]{:T(128)}, /*index=5*/s32[]{:T(128)}) %tuple.240), condition=%wide.region_8.9_spmd, body=%wide.region_7.8_spmd.sunk | while | flops 2019755136 | bytes 24387924 | solution.py:93
  410.5 7.1 all-to-all-done.8
  440.5 7.2 all-to-all-done.10
  504.2 7.2 all-to-all-done.10
  515.9 127.1 %while.107 = (s32[]{:T(128)}, f32[2,4,128,128]{3,2,1,0:T(8,128)S(1)}, f32[2,4,128,128]{3,2,1,0:T(8,128)S(1)}, s32[]{:T(128)}, u32[]{:T(128)}, /*index=5*/s32[]{:T(128)}) while((s32[]{:T(128)}, f32[2,4,128,128]{3,2,1,0:T(8,128)S(1)}, f32[2,4,128,128]{3,2,1,0:T(8,128)S(1)}, s32[]{:T(128)}, u32[]{:T(128)}, /*index=5*/s32[]{:T(128)}) %tuple.237), condition=%wide.region_11.12_spmd, body=%wide.region_10.11_spmd.sunk | while | flops 2019755136 | bytes 20193564 | solution.py:93
  569.8 7.2 all-to-all-done.14
  632.5 7.2 all-to-all-done.14
  643.8 126.1 %while.108 = (s32[]{:T(128)}, f32[2,4,128,128]{3,2,1,0:T(8,128)S(1)}, f32[2,4,128,128]{3,2,1,0:T(8,128)S(1)}, s32[]{:T(128)}, u32[]{:T(128)}, /*index=5*/s32[]{:T(128)}) while((s32[]{:T(128)}, f32[2,4,128,128]{3,2,1,0:T(8,128)S(1)}, f32[2,4,128,128]{3,2,1,0:T(8,128)S(1)}, s32[]{:T(128)}, u32[]{:T(128)}, /*index=5*/s32[]{:T(128)}) %tuple.234), condition=%wide.region_14.15_spmd, body=%wide.region_13.14_spmd.sunk | while | flops 2019755136 | bytes 20193564 | solution.py:93
  696.6 7.2 all-to-all-done.18
  759.4 7.3 all-to-all-done.18
  770.7 126.0 %while.109 = (s32[]{:T(128)}, f32[2,4,128,128]{3,2,1,0:T(8,128)S(1)}, f32[2,4,128,128]{3,2,1,0:T(8,128)S(1)}, s32[]{:T(128)}, u32[]{:T(128)}, /*index=5*/s32[]{:T(128)}) while((s32[]{:T(128)}, f32[2,4,128,128]{3,2,1,0:T(8,128)S(1)}, f32[2,4,128,128]{3,2,1,0:T(8,128)S(1)}, s32[]{:T(128)}, u32[]{:T(128)}, /*index=5*/s32[]{:T(128)}) %tuple.231), condition=%wide.region_17.18_spmd, body=%wide.region_16.17_spmd.sunk | while | flops 2019755136 | bytes 20193564 | solution.py:93
  823.5 7.2 all-to-all-done.22
  856.2 7.1 all-to-all-done.20
  886.2 7.2 all-to-all-done.22
  898.0 127.5 %while.110 = (s32[]{:T(128)}, f32[2,4,128,128]{3,2,1,0:T(8,128)S(1)}, f32[2,4,128,128]{3,2,1,0:T(8,128)S(1)}, s32[]{:T(128)}, u32[]{:T(128)}, /*index=5*/s32[]{:T(128)}) while((s32[]{:T(128)}, f32[2,4,128,128]{3,2,1,0:T(8,128)S(1)}, f32[2,4,128,128]{3,2,1,0:T(8,128)S(1)}, s32[]{:T(128)}, u32[]{:T(128)}, /*index=5*/s32[]{:T(128)}) %tuple.253), condition=%wide.region_20.21_spmd, body=%wide.region_19.20_spmd.sunk | while | flops 2019755136 | bytes 20193564 | solution.py:93
  920.5 8.0 all-to-all-done.24
  952.1 7.2 all-to-all-done.26
  984.7 7.1 all-to-all-done.24
  1014.8 7.2 all-to-all-done.26
  1026.8 125.7 %while.111 = (s32[]{:T(128)}, f32[2,4,128,128]{3,2,1,0:T(8,128)S(1)}, f32[2,4,128,128]{3,2,1,0:T(8,128)S(1)}, s32[]{:T(128)}, u32[]{:T(128)}, /*index=5*/s32[]{:T(128)}) while((s32[]{:T(128)}, f32[2,4,128,128]{3,2,1,0:T(8,128)S(1)}, f32[2,4,128,128]{3,2,1,0:T(8,128)S(1)}, s32[]{:T(128)}, u32[]{:T(128)}, /*index=5*/s32[]{:T(128)}) %tuple.252), condition=%wide.region_23.24_spmd, body=%wide.region_22.23_spmd.sunk | while | flops 2019755136 | bytes 20193564 | solution.py:93
  1079.2 7.2 all-to-all-done.30
  1142.0 7.2 all-to-all-done.30
  (676 shorter events, 867.3 us)
Async XLA Ops:
  6.5 115.6 %all-reduce.3.cloned.1.call-start = ((), (), s32[]{:S(2)}) async-start(), calls=%async_computation.32 | async-start | bytes 4194304 | tf_op jit(solution)/shard_map/psum | solution.py:17
  129.4 16.1 %all-to-all-start.1 = ((f32[1,4,128,128]{3,1,0,2:T(4,128)}), f32[1,4,128,128]{3,1,0,2:T(4,128)S(1)}, u32[]{:S(2)}, u32[]{:S(2)}) async-start(f32[1,4,128,128]{3,1,0,2:T(4,128)} %copy.678), calls=%async_computation.1 | async-start | bytes 524288 | tf_op jit(solution)/shard_map/while/body/eval_jaxpr/all_to_all | solution.py:77
  145.5 13.0 %all-to-all-start = ((f32[1,4,128,128]{3,1,0,2:T(4,128)}), f32[1,4,128,128]{3,1,0,2:T(4,128)S(1)}, u32[]{:S(2)}, u32[]{:S(2)}) async-start(f32[1,4,128,128]{3,1,0,2:T(4,128)} %copy.676), calls=%async_computation | async-start | bytes 524288 | tf_op jit(solution)/shard_map/while/body/eval_jaxpr/all_to_all | solution.py:76
  162.8 12.9 %all-to-all-start.3 = ((f32[1,128,4,128]{3,2,0,1:T(4,128)}), f32[1,128,4,128]{3,2,0,1:T(4,128)S(1)}, u32[]{:S(2)}, u32[]{:S(2)}) async-start(f32[1,128,4,128]{3,2,0,1:T(4,128)} %copy.682), calls=%async_computation.3 | async-start | bytes 524288 | tf_op jit(solution)/shard_map/while/body/eval_jaxpr/all_to_all | solution.py:82
  274.3 13.0 %all-to-all-start.4 = ((f32[1,4,128,128]{3,1,0,2:T(4,128)}), f32[1,4,128,128]{3,1,0,2:T(4,128)S(1)}, u32[]{:S(2)}, u32[]{:S(2)}) async-start(f32[1,4,128,128]{3,1,0,2:T(4,128)} %copy.684), calls=%async_computation.4 | async-start | bytes 524288 | tf_op jit(solution)/shard_map/while/body/eval_jaxpr/all_to_all | solution.py:76
  291.6 13.9 %all-to-all-start.7 = ((f32[1,128,4,128]{3,2,0,1:T(4,128)}), f32[1,128,4,128]{3,2,0,1:T(4,128)S(1)}, u32[]{:S(2)}, u32[]{:S(2)}) async-start(f32[1,128,4,128]{3,2,0,1:T(4,128)} %copy.690), calls=%async_computation.7 | async-start | bytes 524288 | tf_op jit(solution)/shard_map/while/body/eval_jaxpr/all_to_all | solution.py:82
  305.6 13.1 %all-to-all-start.6 = ((f32[1,128,4,128]{3,2,0,1:T(4,128)}), f32[1,128,4,128]{3,2,0,1:T(4,128)S(1)}, u32[]{:S(2)}, u32[]{:S(2)}) async-start(f32[1,128,4,128]{3,2,0,1:T(4,128)} %copy.688), calls=%async_computation.6 | async-start | bytes 524288 | tf_op jit(solution)/shard_map/while/body/eval_jaxpr/all_to_all | solution.py:81
  339.2 13.5 %all-to-all-start.4 = ((f32[1,4,128,128]{3,1,0,2:T(4,128)}), f32[1,4,128,128]{3,1,0,2:T(4,128)S(1)}, u32[]{:S(2)}, u32[]{:S(2)}) async-start(f32[1,4,128,128]{3,1,0,2:T(4,128)} %copy.684), calls=%async_computation.4 | async-start | bytes 524288 | tf_op jit(solution)/shard_map/while/body/eval_jaxpr/all_to_all | solution.py:76
  357.0 13.2 %all-to-all-start.7 = ((f32[1,128,4,128]{3,2,0,1:T(4,128)}), f32[1,128,4,128]{3,2,0,1:T(4,128)S(1)}, u32[]{:S(2)}, u32[]{:S(2)}) async-start(f32[1,128,4,128]{3,2,0,1:T(4,128)} %copy.690), calls=%async_computation.7 | async-start | bytes 524288 | tf_op jit(solution)/shard_map/while/body/eval_jaxpr/all_to_all | solution.py:82
  370.2 13.0 %all-to-all-start.6 = ((f32[1,128,4,128]{3,2,0,1:T(4,128)}), f32[1,128,4,128]{3,2,0,1:T(4,128)S(1)}, u32[]{:S(2)}, u32[]{:S(2)}) async-start(f32[1,128,4,128]{3,2,0,1:T(4,128)} %copy.688), calls=%async_computation.6 | async-start | bytes 524288 | tf_op jit(solution)/shard_map/while/body/eval_jaxpr/all_to_all | solution.py:81
  391.7 13.0 %all-to-all-start.9 = ((f32[1,4,128,128]{3,1,0,2:T(4,128)}), f32[1,4,128,128]{3,1,0,2:T(4,128)S(1)}, u32[]{:S(2)}, u32[]{:S(2)}) async-start(f32[1,4,128,128]{3,1,0,2:T(4,128)} %copy.694), calls=%async_computation.9 | async-start | bytes 524288 | tf_op jit(solution)/shard_map/while/body/eval_jaxpr/all_to_all | solution.py:77
  455.3 12.9 %all-to-all-start.9 = ((f32[1,4,128,128]{3,1,0,2:T(4,128)}), f32[1,4,128,128]{3,1,0,2:T(4,128)S(1)}, u32[]{:S(2)}, u32[]{:S(2)}) async-start(f32[1,4,128,128]{3,1,0,2:T(4,128)} %copy.694), calls=%async_computation.9 | async-start | bytes 524288 | tf_op jit(solution)/shard_map/while/body/eval_jaxpr/all_to_all | solution.py:77
  485.4 13.1 %all-to-all-start.11 = ((f32[1,128,4,128]{3,2,0,1:T(4,128)}), f32[1,128,4,128]{3,2,0,1:T(4,128)S(1)}, u32[]{:S(2)}, u32[]{:S(2)}) async-start(f32[1,128,4,128]{3,2,0,1:T(4,128)} %copy.698), calls=%async_computation.11 | async-start | bytes 524288 | tf_op jit(solution)/shard_map/while/body/eval_jaxpr/all_to_all | solution.py:82
  519.4 13.7 %all-to-all-start.13 = ((f32[1,4,128,128]{3,1,0,2:T(4,128)}), f32[1,4,128,128]{3,1,0,2:T(4,128)S(1)}, u32[]{:S(2)}, u32[]{:S(2)}) async-start(f32[1,4,128,128]{3,1,0,2:T(4,128)} %copy.702), calls=%async_computation.13 | async-start | bytes 524288 | tf_op jit(solution)/shard_map/while/body/eval_jaxpr/all_to_all | solution.py:77
  533.1 13.0 %all-to-all-start.12 = ((f32[1,4,128,128]{3,1,0,2:T(4,128)}), f32[1,4,128,128]{3,1,0,2:T(4,128)S(1)}, u32[]{:S(2)}, u32[]{:S(2)}) async-start(f32[1,4,128,128]{3,1,0,2:T(4,128)} %copy.700), calls=%async_computation.12 | async-start | bytes 524288 | tf_op jit(solution)/shard_map/while/body/eval_jaxpr/all_to_all | solution.py:76
  550.3 13.7 %all-to-all-start.15 = ((f32[1,128,4,128]{3,2,0,1:T(4,128)}), f32[1,128,4,128]{3,2,0,1:T(4,128)S(1)}, u32[]{:S(2)}, u32[]{:S(2)}) async-start(f32[1,128,4,128]{3,2,0,1:T(4,128)} %copy.706), calls=%async_computation.15 | async-start | bytes 524288 | tf_op jit(solution)/shard_map/while/body/eval_jaxpr/all_to_all | solution.py:82
  564.0 13.0 %all-to-all-start.14 = ((f32[1,128,4,128]{3,2,0,1:T(4,128)}), f32[1,128,4,128]{3,2,0,1:T(4,128)S(1)}, u32[]{:S(2)}, u32[]{:S(2)}) async-start(f32[1,128,4,128]{3,2,0,1:T(4,128)} %copy.704), calls=%async_computation.14 | async-start | bytes 524288 | tf_op jit(solution)/shard_map/while/body/eval_jaxpr/all_to_all | solution.py:81
  647.4 13.0 %all-to-all-start.17 = ((f32[1,4,128,128]{3,1,0,2:T(4,128)}), f32[1,4,128,128]{3,1,0,2:T(4,128)S(1)}, u32[]{:S(2)}, u32[]{:S(2)}) async-start(f32[1,4,128,128]{3,1,0,2:T(4,128)} %copy.710), calls=%async_computation.17 | async-start | bytes 524288 | tf_op jit(solution)/shard_map/while/body/eval_jaxpr/all_to_all | solution.py:77
  660.5 13.0 %all-to-all-start.16 = ((f32[1,4,128,128]{3,1,0,2:T(4,128)}), f32[1,4,128,128]{3,1,0,2:T(4,128)S(1)}, u32[]{:S(2)}, u32[]{:S(2)}) async-start(f32[1,4,128,128]{3,1,0,2:T(4,128)} %copy.708), calls=%async_computation.16 | async-start | bytes 524288 | tf_op jit(solution)/shard_map/while/body/eval_jaxpr/all_to_all | solution.py:76
  677.7 13.0 %all-to-all-start.19 = ((f32[1,128,4,128]{3,2,0,1:T(4,128)}), f32[1,128,4,128]{3,2,0,1:T(4,128)S(1)}, u32[]{:S(2)}, u32[]{:S(2)}) async-start(f32[1,128,4,128]{3,2,0,1:T(4,128)} %copy.714), calls=%async_computation.19 | async-start | bytes 524288 | tf_op jit(solution)/shard_map/while/body/eval_jaxpr/all_to_all | solution.py:82
  690.8 13.0 %all-to-all-start.18 = ((f32[1,128,4,128]{3,2,0,1:T(4,128)}), f32[1,128,4,128]{3,2,0,1:T(4,128)S(1)}, u32[]{:S(2)}, u32[]{:S(2)}) async-start(f32[1,128,4,128]{3,2,0,1:T(4,128)} %copy.712), calls=%async_computation.18 | async-start | bytes 524288 | tf_op jit(solution)/shard_map/while/body/eval_jaxpr/all_to_all | solution.py:81
  753.6 13.0 %all-to-all-start.18 = ((f32[1,128,4,128]{3,2,0,1:T(4,128)}), f32[1,128,4,128]{3,2,0,1:T(4,128)S(1)}, u32[]{:S(2)}, u32[]{:S(2)}) async-start(f32[1,128,4,128]{3,2,0,1:T(4,128)} %copy.712), calls=%async_computation.18 | async-start | bytes 524288 | tf_op jit(solution)/shard_map/while/body/eval_jaxpr/all_to_all | solution.py:81
  774.6 13.1 %all-to-all-start.21 = ((f32[1,4,128,128]{3,1,0,2:T(4,128)}), f32[1,4,128,128]{3,1,0,2:T(4,128)S(1)}, u32[]{:S(2)}, u32[]{:S(2)}) async-start(f32[1,4,128,128]{3,1,0,2:T(4,128)} %copy.718), calls=%async_computation.21 | async-start | bytes 524288 | tf_op jit(solution)/shard_map/while/body/eval_jaxpr/all_to_all | solution.py:77
  901.6 13.0 %all-to-all-start.25 = ((f32[1,4,128,128]{3,1,0,2:T(4,128)}), f32[1,4,128,128]{3,1,0,2:T(4,128)S(1)}, u32[]{:S(2)}, u32[]{:S(2)}) async-start(f32[1,4,128,128]{3,1,0,2:T(4,128)} %copy.726), calls=%async_computation.25 | async-start | bytes 524288 | tf_op jit(solution)/shard_map/while/body/eval_jaxpr/all_to_all | solution.py:77
  914.6 13.9 %all-to-all-start.24 = ((f32[1,4,128,128]{3,1,0,2:T(4,128)}), f32[1,4,128,128]{3,1,0,2:T(4,128)S(1)}, u32[]{:S(2)}, u32[]{:S(2)}) async-start(f32[1,4,128,128]{3,1,0,2:T(4,128)} %copy.724), calls=%async_computation.24 | async-start | bytes 524288 | tf_op jit(solution)/shard_map/while/body/eval_jaxpr/all_to_all | solution.py:76
  932.8 13.5 %all-to-all-start.27 = ((f32[1,128,4,128]{3,2,0,1:T(4,128)}), f32[1,128,4,128]{3,2,0,1:T(4,128)S(1)}, u32[]{:S(2)}, u32[]{:S(2)}) async-start(f32[1,128,4,128]{3,2,0,1:T(4,128)} %copy.730), calls=%async_computation.27 | async-start | bytes 524288 | tf_op jit(solution)/shard_map/while/body/eval_jaxpr/all_to_all | solution.py:82
  966.0 12.9 %all-to-all-start.25 = ((f32[1,4,128,128]{3,1,0,2:T(4,128)}), f32[1,4,128,128]{3,1,0,2:T(4,128)S(1)}, u32[]{:S(2)}, u32[]{:S(2)}) async-start(f32[1,4,128,128]{3,1,0,2:T(4,128)} %copy.726), calls=%async_computation.25 | async-start | bytes 524288 | tf_op jit(solution)/shard_map/while/body/eval_jaxpr/all_to_all | solution.py:77
  978.9 12.9 %all-to-all-start.24 = ((f32[1,4,128,128]{3,1,0,2:T(4,128)}), f32[1,4,128,128]{3,1,0,2:T(4,128)S(1)}, u32[]{:S(2)}, u32[]{:S(2)}) async-start(f32[1,4,128,128]{3,1,0,2:T(4,128)} %copy.724), calls=%async_computation.24 | async-start | bytes 524288 | tf_op jit(solution)/shard_map/while/body/eval_jaxpr/all_to_all | solution.py:76
  996.1 12.9 %all-to-all-start.27 = ((f32[1,128,4,128]{3,2,0,1:T(4,128)}), f32[1,128,4,128]{3,2,0,1:T(4,128)S(1)}, u32[]{:S(2)}, u32[]{:S(2)}) async-start(f32[1,128,4,128]{3,2,0,1:T(4,128)} %copy.730), calls=%async_computation.27 | async-start | bytes 524288 | tf_op jit(solution)/shard_map/while/body/eval_jaxpr/all_to_all | solution.py:82
  1030.2 13.0 %all-to-all-start.29 = ((f32[1,4,128,128]{3,1,0,2:T(4,128)}), f32[1,4,128,128]{3,1,0,2:T(4,128)S(1)}, u32[]{:S(2)}, u32[]{:S(2)}) async-start(f32[1,4,128,128]{3,1,0,2:T(4,128)} %copy.734), calls=%async_computation.29 | async-start | bytes 524288 | tf_op jit(solution)/shard_map/while/body/eval_jaxpr/all_to_all | solution.py:77
  1060.4 13.0 %all-to-all-start.31 = ((f32[1,128,4,128]{3,2,0,1:T(4,128)}), f32[1,128,4,128]{3,2,0,1:T(4,128)S(1)}, u32[]{:S(2)}, u32[]{:S(2)}) async-start(f32[1,128,4,128]{3,2,0,1:T(4,128)} %copy.738), calls=%async_computation.31 | async-start | bytes 524288 | tf_op jit(solution)/shard_map/while/body/eval_jaxpr/all_to_all | solution.py:82
  1073.3 13.1 %all-to-all-start.30 = ((f32[1,128,4,128]{3,2,0,1:T(4,128)}), f32[1,128,4,128]{3,2,0,1:T(4,128)S(1)}, u32[]{:S(2)}, u32[]{:S(2)}) async-start(f32[1,128,4,128]{3,2,0,1:T(4,128)} %copy.736), calls=%async_computation.30 | async-start | bytes 524288 | tf_op jit(solution)/shard_map/while/body/eval_jaxpr/all_to_all | solution.py:81
  (63 other events, 922.5 us)
Sparse Core Ops, SparseCore 0:
  33.2 88.8 all-reduce.2
where the time goes:
time: 1180 us; the launch traced here: 1160 us
  waiting for transfers between devices  507 us (43%)
  starting transfers between devices  325 us (28%)
  matrix products  207 us (18%)
  local copies, waits for them, and re-layouts  73.8 us (6%)
  between operations  34.3 us (3%)
    dot_general x320, matrix products, product(): jnp.einsum(EINSUM_FORMS[axis_number], operand, matrix, precision=lax.Prec...  207 us
    all_to_all x16, waiting for transfers between devices, poisson_solve(): lax.all_to_all(real_part, 'grid', split_axis=2, concat_axis=1, tiled=True)  115 us
    all_to_all x16, waiting for transfers between devices, poisson_solve(): lax.all_to_all(spec_real, 'grid', split_axis=1, concat_axis=2, tiled=True)  115 us
    all_to_all x16, waiting for transfers between devices, poisson_solve(): lax.all_to_all(spec_imag, 'grid', split_axis=1, concat_axis=2, tiled=True)  93.7 us
    all_to_all x16, waiting for transfers between devices, poisson_solve(): lax.all_to_all(imag_part, 'grid', split_axis=2, concat_axis=1, tiled=True)  93.2 us
    psum x1, waiting for transfers between devices, from_root(): return lax.psum(jnp.where(mine, array, jnp.zeros_like(array)), axis)  89 us
    all_to_all x16, starting transfers between devices, poisson_solve(): lax.all_to_all(imag_part, 'grid', split_axis=2, concat_axis=1, tiled=True)  82.7 us
    all_to_all x16, starting transfers between devices, poisson_solve(): lax.all_to_all(spec_imag, 'grid', split_axis=1, concat_axis=2, tiled=True)  80.9 us
  transfers between devices with their start and end apart: 65, of which 65 were waited for; matrix products, arithmetic and copies ran while one was open for 8% of the time, Pallas kernels for 0%

commit v1 on v0

v1 whole, which is shorter than its diff:
```python
import math

import jax
import jax.numpy as jnp
import numpy as np
from jax import lax
from jax.sharding import PartitionSpec as P

CELL_EDGE = 46.9
PREC = lax.Precision.HIGH


def basis(length):
    half = length // 2
    x = np.arange(length)
    rows = [np.full(length, 1.0 / math.sqrt(length))]
    rows += [math.sqrt(2.0 / length) * np.cos(2 * math.pi * (k * x % length) / length) for k in range(1, half)]
    rows += [(1.0 - 2.0 * (x % 2)) / math.sqrt(length)]
    rows += [math.sqrt(2.0 / length) * np.sin(2 * math.pi * (k * x % length) / length) for k in range(1, half)]
    freq = np.concatenate([np.arange(half + 1), np.arange(1, half)])
    return np.stack(rows).astype(np.float32), freq.astype(np.float32)


def shards(orbitals, band_owner, block_index):
    held, planes, ny, nz = orbitals.shape
    rounds = band_owner.shape[0]
    grid = lax.axis_size("grid")
    nx = planes * grid
    tx, fx = basis(nx)
    ty, fy = basis(ny)
    tz, fz = basis(nz)
    every = lax.all_gather(orbitals, "band", tiled=True)
    chosen = every[band_owner * held + block_index]
    psi = jnp.transpose(orbitals, (2, 0, 1, 3))
    chosen = jnp.transpose(chosen, (2, 0, 1, 3))
    rho = psi[:, :, None] * chosen[:, None]
    rows = held * rounds * planes
    rho = rho.reshape(ny, rows, nz)
    half = jnp.einsum("yrz,kz->yrk", rho, tz, precision=PREC)
    half = jnp.einsum("yrz,ky->krz", half, ty, precision=PREC)
    spec = lax.all_to_all(half, "grid", split_axis=0, concat_axis=0, tiled=True)
    own = ny // grid
    spec = spec.reshape(grid, own, held * rounds, planes, nz)
    txs = tx.reshape(nx, grid, planes)
    spec = jnp.einsum("sqnpz,msp->mqnz", spec, txs, precision=PREC)
    fy_own = lax.dynamic_slice_in_dim(jnp.asarray(fy), lax.axis_index("grid") * own, own)
    scale = (2.0 * math.pi / CELL_EDGE) ** 2
    squared = scale * (fx[:, None, None] ** 2 + fy_own[None, :, None] ** 2 + fz[None, None, :] ** 2)
    guarded = jnp.where(squared > 0, squared, 1.0)
    kernel = jnp.where(squared > 0, 4.0 * math.pi / guarded, 0.0)
    spec = spec * kernel[:, :, None, :]
    spec = jnp.einsum("mqnz,msp->sqnpz", spec, txs, precision=PREC)
    half = lax.all_to_all(spec.reshape(ny, rows, nz), "grid", split_axis=0, concat_axis=0, tiled=True)
    half = jnp.einsum("krz,ky->yrz", half, ty, precision=PREC)
    half = jnp.einsum("yrk,kz->yrz", half, tz, precision=PREC)
    pot = half.reshape(ny, held, rounds, planes, nz)
    out = -jnp.sum(chosen[:, None] * pot, axis=2)
    return jnp.transpose(out, (1, 2, 0, 3))


def solution(mesh):
    return jax.shard_map(
        shards,
        mesh=mesh,
        in_specs=(P("band", "grid", None, None), P(), P()),
        out_specs=P("band", "grid", None, None),
        check_vma=False,
    )
```

time: 1180 us -> 225 us (0.19); the launches traced: 1160 us -> 224 us
  waiting for transfers between devices: 507 us -> 111 us
  starting transfers between devices: 325 us -> 8.4 us
  matrix products: 207 us -> 18.2 us
  local copies, waits for them, and re-layouts: 73.8 us -> 10.3 us
  blocking collectives: 0 us -> 59.6 us
  between operations: 34.3 us -> 13.5 us
    all_to_all x64 -> x1, waiting for transfers between devices: 418 us -> 52.8 us  [shards(): spec = lax.all_to_all(half, 'grid', split_axis=0, concat_axis=0, tiled=True)]
    all_to_all x64 -> x1, starting transfers between devices: 325 us -> 8.39 us  [shards(): spec = lax.all_to_all(half, 'grid', split_axis=0, concat_axis=0, tiled=True)]
    dot_general x320 -> x6, matrix products: 207 us -> 18.2 us  [the longest x1 6.36 us: shards(): spec = jnp.einsum('sqnpz,msp->mqnz', spec, txs, precision=PREC)]
    psum x1 -> x0, waiting for transfers between devices: 89 us -> none  [from_root(): return lax.psum(jnp.where(mine, array, jnp.zeros_like(array)), axis)]
    all_to_all x0 -> x1, blocking collectives: none -> 59.6 us  [shards(): lax.all_to_all(spec.reshape(ny, rows, nz), 'grid', split_axis=0, concat_a...]
    all_gather x0 -> x1, waiting for transfers between devices: none -> 57.2 us  [shards(): every = lax.all_gather(orbitals, 'band', tiled=True)]
    div x32 -> x0, local copies, waits for them, and re-layouts: 28 us -> none  [the longest x16 14 us: inverse(): (product(imag_part, cosine, axis_number) + product(real_part, sine_table,...]
    sub x16 -> x0, local copies, waits for them, and re-layouts: 14 us -> none  [forward(): product(imag_part, cosine, axis_number)]
  transfers between devices with their start and end apart: 65 -> 2, of which waited for: 65 -> 2; matrix products, arithmetic and copies ran while one was open for 8% -> 0% of each run, Pallas kernels for 0% -> 0%
where the time goes in v1:
time: 225 us; the launch traced here: 224 us
  waiting for transfers between devices  111 us (49%)
  blocking collectives  59.6 us (26%)
  matrix products  18.2 us (8%)
  between operations  13.5 us (6%)
  local copies, waits for them, and re-layouts  10.3 us (5%)
  starting transfers between devices  8.4 us (4%)
  other arithmetic  3.07 us (1%)
    all_to_all x1, blocking collectives, shards(): lax.all_to_all(spec.reshape(ny, rows, nz), 'grid', split_axis=0, concat_a...  59.6 us
    all_gather x1, waiting for transfers between devices, shards(): every = lax.all_gather(orbitals, 'band', tiled=True)  57.2 us
    all_to_all x1, waiting for transfers between devices, shards(): spec = lax.all_to_all(half, 'grid', split_axis=0, concat_axis=0, tiled=True)  52.8 us
    all_to_all x1, starting transfers between devices, shards(): spec = lax.all_to_all(half, 'grid', split_axis=0, concat_axis=0, tiled=True)  8.39 us
    dot_general x1, matrix products, shards(): spec = jnp.einsum('sqnpz,msp->mqnz', spec, txs, precision=PREC)  6.36 us
  transfers between devices with their start and end apart: 2, of which 2 were waited for; matrix products, arithmetic and copies ran while one was open for 0% of the time, Pallas kernels for 0%

profile of v1, /device:TPU:8, one launch (start us, length us, event | category | flops | bytes accessed | tf_op | source)
XLA Modules:
  0.0 223.8 jit_solution(1352801500541325768)
XLA Ops:
  6.5 0.0 copy-start
  6.5 0.0 all-gather.2.cloned.1.call-start
  6.5 0.7 all-gather.2.cloned.1.call-update
  7.3 0.7 compare_select_fusion.2
  7.9 57.2 %all-gather.2.cloned.1.call-done = f32[16,4,128,128]{3,2,1,0:T(8,128)} async-done(((f32[2,4,128,128]{3,2,1,0:T(8,128)}), f32[16,4,128,128]{3,2,1,0:T(8,128)}) %all-gather.2.cloned.1.call-update) | async-done | bytes 4194320 | tf_op jit(solution)/shard_map/all_gather | solution.py:32
  65.1 2.9 %gather_fusion = f32[8,4,128,128]{3,2,1,0:T(8,128)S(1)} fusion(f32[16,4,128,128]{3,2,1,0:T(8,128)} %all-gather.2.cloned.1.call-done, s32[1024]{0:T(1024)S(1)} %pad_clamp_fusion), kind=kCustom, calls=%fused_computation | custom fusion | bytes 4194336 | tf_op jit(solution)/shard_map/gather | solution.py:33
  68.0 0.0 copy-start.1
  68.0 0.0 copy-done
  68.0 0.5 broadcast_multiply_fusion
  68.6 0.3 copy-done.1
  68.9 1.8 fusion.11
  70.7 1.9 fusion.12
  72.6 4.4 %copy.23 = f32[128,64,128]{2,1,0:T(8,128)} copy(f32[128,64,128]{2,0,1:T(8,128)S(1)} %fusion.12) | data formatting | bytes 8388608 | tf_op jit(solution)/shard_map/yrz,ky->krz/dot_general | solution.py:40
  77.0 0.0 copy-start.4
  77.0 0.0 copy-start.3
  77.0 0.0 copy-start.2
  77.0 8.4 %all-to-all-start = ((f32[128,64,128]{2,1,0:T(8,128)}), f32[128,64,128]{2,1,0:T(8,128)}, u32[]{:S(2)}, u32[]{:S(2)}) async-start(f32[128,64,128]{2,1,0:T(8,128)} %copy.23), calls=%async_computation | async-start | bytes 8388608 | tf_op jit(solution)/shard_map/all_to_all | solution.py:41
  85.4 0.0 copy-done.4
  85.4 0.1 dynamic-slice_multiply_fusion
  85.5 0.0 copy-done.3
  85.5 0.1 broadcast_add_fusion
  85.6 0.1 compare_select_fusion
  85.7 52.8 %all-to-all-done = f32[128,64,128]{2,1,0:T(8,128)} async-done(((f32[128,64,128]{2,1,0:T(8,128)}), f32[128,64,128]{2,1,0:T(8,128)}, u32[]{:S(2)}, u32[]{:S(2)}) %all-to-all-start) | async-done | bytes 4194336 | tf_op jit(solution)/shard_map/all_to_all | solution.py:41
  138.5 0.0 copy-done.2
  138.5 6.4 %fusion.4 = f32[128,4,16,128,1]{3,0,4,2,1:T(8,128)S(1)} fusion(f32[128,32,4,1,1]{0,1,2,4,3:T(8,128)S(1)} %copy-done.2, f32[32,4,16,4,128]{4,3,2,1,0:T(4,128)} %bitcast.7), kind=kOutput, calls=%fused_computation.6 | convolution fusion | flops 805306368 | bytes 8454144 | tf_op jit(solution)/shard_map/sqnpz,msp->mqnz/dot_general | solution.py:45
  144.9 2.0 fusion.6
  146.9 2.7 %copy.25 = f32[32,4,16,4,128]{4,3,2,1,0:T(4,128)S(1)} copy(f32[32,4,16,4,128]{4,0,3,2,1:T(8,128)S(1)} %fusion.6) | data formatting | bytes 8388608 | tf_op jit(solution)/shard_map/mqnz,msp->sqnpz/transpose | solution.py:52
  149.6 59.6 %all_to_all.10 = f32[128,64,128]{2,1,0:T(8,128)S(1)} all-to-all(f32[128,64,128]{2,1,0:T(8,128)S(1)} %bitcast.41), channel_id=1, replica_groups=mesh['band'=8,'grid'=32] {'grid'}, dimensions={0} | all-to-all | bytes 8388608 | tf_op jit(solution)/shard_map/all_to_all | solution.py:53
  209.2 4.2 %fusion.2 = f32[128,64,128]{2,0,1:T(8,128)S(1)} fusion(f32[128,128,1]{1,0,2:T(8,128)S(1)} %copy-done.1, f32[128,64,128]{2,1,0:T(8,128)S(1)} %all_to_all.10), kind=kOutput, calls=%fused_computation.4 | convolution fusion | flops 805306368 | bytes 8454144 | tf_op jit(solution)/shard_map/krz,ky->yrz/dot_general | solution.py:54
  213.4 1.9 fusion.13
  215.3 0.7 multiply_reduce_fusion
  216.1 0.8 negate_bitcast_fusion
  (1 shorter events, 0.0 us)
Async XLA Ops:
  6.5 61.5 %copy-start = (f32[2,4,128,128]{3,2,1,0:T(8,128)S(1)}, f32[2,4,128,128]{3,2,1,0:T(8,128)}, u32[]{:S(2)}) copy-start(f32[2,4,128,128]{3,2,1,0:T(8,128)} %param.12) | copy-start | bytes 1572868
  6.5 58.6 %all-gather.2.cloned.1.call-start = ((), (), s32[]{:S(2)}) async-start(), calls=%async_computation.2 | async-start | bytes 4718592 | tf_op jit(solution)/shard_map/all_gather | solution.py:32
  68.0 0.8 copy-start.1
  77.0 8.4 %copy-start.4 = (f32[128]{0:T(128)S(1)}, f32[128]{0:T(128)}, u32[]{:S(2)}) copy-start(f32[128]{0:T(128)} %constant.36.clone) | copy-start | bytes 1540
  77.0 8.5 %copy-start.3 = (f32[128]{0:T(128)S(1)}, f32[128]{0:T(128)}, u32[]{:S(2)}) copy-start(f32[128]{0:T(128)} %constant.40) | copy-start | bytes 1540
  77.0 61.5 %copy-start.2 = (f32[128,32,4,1,1]{0,1,2,4,3:T(8,128)S(1)}, f32[128,32,4,1,1]{0,1,2,4,3:T(8,128)}, u32[]{:S(2)}) copy-start(f32[128,32,4,1,1]{0,1,2,4,3:T(8,128)} %constant.43) | copy-start | bytes 196612
  77.0 61.5 %all-to-all-start = ((f32[128,64,128]{2,1,0:T(8,128)}), f32[128,64,128]{2,1,0:T(8,128)}, u32[]{:S(2)}, u32[]{:S(2)}) async-start(f32[128,64,128]{2,1,0:T(8,128)} %copy.23), calls=%async_computation | async-start | bytes 8388608 | tf_op jit(solution)/shard_map/all_to_all | solution.py:41
Sparse Core Ops, SparseCore 0:
  9.2 55.8 all-gather.1

commit v2 on v1

v2 whole, which is shorter than its diff:
```python
import functools
import math

import jax
import jax.numpy as jnp
import ml_dtypes
import numpy as np
from jax import lax
from jax.experimental import pallas as pl
from jax.experimental.pallas import tpu as pltpu
from jax.sharding import PartitionSpec as P

CELL_EDGE = 46.9
GRID = "grid"


def basis(length):
    half = length // 2
    x = np.arange(length)
    rows = [np.full(length, 1.0 / math.sqrt(length))]
    rows += [math.sqrt(2.0 / length) * np.cos(2 * math.pi * (k * x % length) / length) for k in range(1, half)]
    rows += [(1.0 - 2.0 * (x % 2)) / math.sqrt(length)]
    rows += [math.sqrt(2.0 / length) * np.sin(2 * math.pi * (k * x % length) / length) for k in range(1, half)]
    freq = np.concatenate([np.arange(half + 1), np.arange(1, half)])
    return np.stack(rows), freq.astype(np.float32)


def halves(table):
    table = table.astype(np.float32)
    high = table.astype(ml_dtypes.bfloat16)
    return high, (table - high.astype(np.float32)).astype(ml_dtypes.bfloat16)


def left_table(table):
    high, low = halves(table)
    return np.block([[high, high], [low, low]])


def right_table(table):
    high, low = halves(table)
    return np.block([[high, low], [high, low]])


def split(values):
    high = values.astype(jnp.bfloat16)
    return high, (values - high.astype(jnp.float32)).astype(jnp.bfloat16)


def from_left(table, values):
    product = jnp.dot(table, jnp.concatenate(split(values), axis=0), preferred_element_type=jnp.float32)
    rows = product.shape[0] // 2
    return product[:rows] + product[rows:]


def from_right(values, table):
    product = jnp.dot(jnp.concatenate(split(values), axis=1), table, preferred_element_type=jnp.float32)
    columns = product.shape[1] // 2
    return product[:, :columns] + product[:, columns:]


def picked(core_ref, mine_ref, other_ref, plane):
    same = core_ref[pl.program_id(0)] == 0
    return jnp.where(same, mine_ref[0, plane], other_ref[0, plane])


def outward(place_ref, core_ref, own_ref, mine_ref, other_ref, wz_ref, wy_ref, out_ref):
    held, planes, ny, nz = own_ref.shape
    rows = out_ref.reshape(ny * planes * held, nz)
    for p in range(planes):
        chosen = picked(core_ref, mine_ref, other_ref, p)
        rho = jnp.concatenate([own_ref[i, p] * chosen for i in range(held)], axis=0)
        rho = from_right(rho, wz_ref[...])
        rho = jnp.concatenate([rho[i * ny:(i + 1) * ny] for i in range(held)], axis=1)
        rho = from_left(wy_ref[...], rho)
        for i in range(held):
            rows[pl.ds(p * held + i, ny, stride=planes * held), :] = rho[:, i * nz:(i + 1) * nz]


def middle(kernel_ref, wx_ref, wxi_ref, in_ref, out_ref):
    slabs, own_y, width, nz = in_ref.shape
    held = 2
    planes = width // held
    rows_in = in_ref.reshape(slabs * own_y * width, nz)
    rows_out = out_ref.reshape(slabs * own_y * width, nz)
    for q in range(own_y):
        def at(p, i):
            return pl.ds(q * width + p * held + i, slabs, stride=own_y * width)

        spec = jnp.concatenate(
            [jnp.concatenate([rows_in[at(p, i), :] for p in range(planes)], axis=0) for i in range(held)], axis=1
        )
        spec = from_left(wx_ref[...], spec)
        spec = spec * jnp.concatenate([kernel_ref[q]] * held, axis=1)
        spec = from_left(wxi_ref[...], spec)
        for i in range(held):
            for p in range(planes):
                rows_out[at(p, i), :] = spec[p * slabs:(p + 1) * slabs, i * nz:(i + 1) * nz]


def inward(place_ref, core_ref, in_ref, mine_ref, other_ref, wz_ref, wy_ref, out_ref):
    held, planes, ny, nz = out_ref.shape
    rows = in_ref.reshape(ny * planes * held, nz)

    @pl.when(pl.program_id(0) == 0)
    def _():
        out_ref[...] = jnp.zeros_like(out_ref)

    for p in range(planes):
        chosen = picked(core_ref, mine_ref, other_ref, p)
        pot = jnp.concatenate(
            [rows[pl.ds(p * held + i, ny, stride=planes * held), :] for i in range(held)], axis=1
        )
        pot = from_left(wy_ref[...], pot)
        pot = jnp.concatenate([pot[:, i * nz:(i + 1) * nz] for i in range(held)], axis=0)
        pot = from_right(pot, wz_ref[...])
        for i in range(held):
            out_ref[i, p] -= chosen * pot[i * ny:(i + 1) * ny]


def rotated(array, axis, step):
    size = lax.axis_size(axis)
    return lax.ppermute(array, axis, [(i, (i + step) % size) for i in range(size)])


def every_orbital(own):
    held = own.shape[0] // 2
    below, above = lax.optimization_barrier((rotated(own, "zh", 1), rotated(own, "zh", -1)))
    far_below = rotated(below[:held], "zh", 1)
    far_above = rotated(above[held:], "zh", -1)
    mine = jnp.concatenate([own, above, far_below, far_above, below])
    return mine, rotated(mine, "core", 1)


def whole(shape):
    return pl.BlockSpec(shape, lambda *_: (0,) * len(shape))


def shards(orbitals, band_owner, block_index):
    held, planes, ny, nz = orbitals.shape
    rounds = band_owner.shape[0]
    grid = lax.axis_size(GRID)
    nx = planes * grid
    own_y = ny // grid
    width = planes * held
    tx, fx = basis(nx)
    ty, fy = basis(ny)
    tz, fz = basis(nz)
    tx = tx.reshape(nx, grid, planes).transpose(0, 2, 1).reshape(nx, nx)
    groups, cores = lax.axis_size("zh"), lax.axis_size("core")
    place = (band_owner // cores - lax.axis_index("zh")) % groups * held + block_index
    core_off = (band_owner + lax.axis_index("core")) % cores

    fy_own = lax.dynamic_slice_in_dim(jnp.asarray(fy), lax.axis_index(GRID) * own_y, own_y)
    scale = (2.0 * math.pi / CELL_EDGE) ** 2
    squared = scale * (fx[None, :, None] ** 2 + fy_own[:, None, None] ** 2 + fz[None, None, :] ** 2)
    guarded = jnp.where(squared > 0, squared, 1.0)
    kernel = jnp.where(squared > 0, 4.0 * math.pi / guarded, 0.0)

    mine, other = every_orbital(orbitals)
    block = pl.BlockSpec((1, planes, ny, nz), lambda r, place, core: (place[r], 0, 0, 0))
    part = pl.BlockSpec((ny, width, nz), lambda r, *_: (0, r, 0))
    table = whole((2 * nz, 2 * nz))
    params = pltpu.CompilerParams(vmem_limit_bytes=48 * 2**20)
    cells = rounds * held * planes * ny * nz

    def cost(transforms):
        return pl.CostEstimate(flops=transforms * 8 * nz * cells, bytes_accessed=8 * cells, transcendentals=0)

    half = pl.pallas_call(
        outward,
        grid_spec=pltpu.PrefetchScalarGridSpec(
            num_scalar_prefetch=2,
            grid=(rounds,),
            in_specs=[whole(orbitals.shape), block, block, table, table],
            out_specs=part,
        ),
        out_shape=jax.ShapeDtypeStruct((ny, rounds * width, nz), jnp.float32),
        compiler_params=params,
        cost_estimate=cost(2),
    )(place, core_off, orbitals, mine, other, right_table(tz.T), left_table(ty))
    spec = lax.all_to_all(half, GRID, split_axis=0, concat_axis=0, tiled=True)
    strip = pl.BlockSpec((grid, own_y, width, nz), lambda r: (0, 0, r, 0))
    spec = pl.pallas_call(
        middle,
        grid=(rounds,),
        in_specs=[whole(kernel.shape), table, table, strip],
        out_specs=strip,
        out_shape=jax.ShapeDtypeStruct((grid, own_y, rounds * width, nz), jnp.float32),
        compiler_params=params,
        cost_estimate=cost(2),
    )(kernel, left_table(tx), left_table(tx.T), spec.reshape(grid, own_y, rounds * width, nz))
    half = lax.all_to_all(
        spec.reshape(ny, rounds * width, nz), GRID, split_axis=0, concat_axis=0, tiled=True
    )
    return pl.pallas_call(
        inward,
        grid_spec=pltpu.PrefetchScalarGridSpec(
            num_scalar_prefetch=2,
            grid=(rounds,),
            in_specs=[part, block, block, table, table],
            out_specs=whole(orbitals.shape),
        ),
        out_shape=jax.ShapeDtypeStruct(orbitals.shape, jnp.float32),
        compiler_params=params,
        cost_estimate=cost(2),
    )(place, core_off, half, mine, other, right_table(tz), left_table(ty.T))


def solution(mesh):
    parts = jax.sharding.Mesh(mesh.devices.reshape(4, 2, 32), ("zh", "core", GRID))
    placed = P(("zh", "core"), GRID, None, None)
    return jax.shard_map(
        shards,
        mesh=parts,
        in_specs=(placed, P(), P()),
        out_specs=placed,
        check_vma=False,
    )
```

time: 225 us -> 199 us (0.88)
  Pallas kernels: 0 us -> 26.7 us
  waiting for transfers between devices: 111 us -> 90.8 us
  matrix products: 18.2 us -> 0 us
  between operations: 13.5 us -> 0.18 us
  starting transfers between devices: 8.4 us -> 18.4 us
  local copies, waits for them, and re-layouts: 10.3 us -> 1.28 us
  other arithmetic: 3.07 us -> 0.31 us
    all_gather x1 -> x0, waiting for transfers between devices: 57.2 us -> none  [shards(): every = lax.all_gather(orbitals, 'band', tiled=True)]
    ppermute x0 -> x5, waiting for transfers between devices: none -> 37.9 us  [rotated(): lax.ppermute(array, axis, [(i, (i + step) % size) for i in range(size)])]
    pallas_call x0 -> x3, Pallas kernels: none -> 26.7 us  [the longest x1 9.01 us: shards(): pl.pallas_call(outward, grid_spec=pltpu.PrefetchScalarGridSpec(num_scalar...]
    dot_general x6 -> x0, matrix products: 18.2 us -> none  [the longest x1 6.36 us: shards(): spec = jnp.einsum('sqnpz,msp->mqnz', spec, txs, precision=PREC)]
    ppermute x0 -> x5, starting transfers between devices: none -> 10.7 us  [rotated(): lax.ppermute(array, axis, [(i, (i + step) % size) for i in range(size)])]
    dot_general x1 -> x0, local copies, waits for them, and re-layouts: 4.42 us -> none  [shards(): half = jnp.einsum('yrz,ky->krz', half, ty, precision=PREC)]
    gather x1 -> x0, local copies, waits for them, and re-layouts: 2.87 us -> none  [shards(): chosen = every[band_owner * held + block_index]]
    transpose x1 -> x0, local copies, waits for them, and re-layouts: 2.7 us -> none  [shards(): spec = jnp.einsum('mqnz,msp->sqnpz', spec, txs, precision=PREC)]
  transfers between devices with their start and end apart: 2 -> 6, of which waited for: 2 -> 6; matrix products, arithmetic and copies ran while one was open for 0% -> 1% of each run, Pallas kernels for 0% -> 0%
where the time goes in v2:
time: 199 us; the launch traced here: 198 us
  waiting for transfers between devices  90.8 us (46%)
  blocking collectives  60 us (30%)
  Pallas kernels  26.7 us (13%)
  starting transfers between devices  18.4 us (9%)
    all_to_all x1, blocking collectives, shards(): lax.all_to_all(spec.reshape(ny, rounds * width, nz), GRID, split_axis=0,...  60 us
    all_to_all x1, waiting for transfers between devices, shards(): spec = lax.all_to_all(half, GRID, split_axis=0, concat_axis=0, tiled=True)  52.9 us
    ppermute x5, waiting for transfers between devices, rotated(): lax.ppermute(array, axis, [(i, (i + step) % size) for i in range(size)])  37.9 us
    ppermute x5, starting transfers between devices, rotated(): lax.ppermute(array, axis, [(i, (i + step) % size) for i in range(size)])  10.7 us
    pallas_call x1, Pallas kernels, shards(): pl.pallas_call(outward, grid_spec=pltpu.PrefetchScalarGridSpec(num_scalar...  9.01 us
    pallas_call x1, Pallas kernels, shards(): pl.pallas_call(inward, grid_spec=pltpu.PrefetchScalarGridSpec(num_scalar_...  8.96 us
    pallas_call x1, Pallas kernels, shards(): pl.pallas_call(middle, grid=(rounds,), in_specs=[whole(kernel.shape), tab...  8.76 us
    all_to_all x1, starting transfers between devices, shards(): spec = lax.all_to_all(half, GRID, split_axis=0, concat_axis=0, tiled=True)  7.73 us
  transfers between devices with their start and end apart: 6, of which 6 were waited for; matrix products, arithmetic and copies ran while one was open for 1% of the time, Pallas kernels for 0%

profile of v2, /device:TPU:8, one launch (start us, length us, event | category | flops | bytes accessed | tf_op | source)
XLA Modules:
  0.0 197.7 jit_solution(4019730165844116538)
XLA Ops:
  0.0 3.3 %collective-permute-start = (f32[2,4,128,128]{3,2,1,0:T(8,128)}, f32[2,4,128,128]{3,2,1,0:T(8,128)S(1)}, u32[]{:S(2)}, u32[]{:S(2)}) collective-permute-start(f32[2,4,128,128]{3,2,1,0:T(8,128)} %own_ref.1), channel_id=1, source_target_pairs={{0,64},{64,128},{128,192},{192,0},{1,65},{65,129},{129,193},{193,1... | collective-permute-start | bytes 1572872 | tf_op jit(solution)/shard_map/ppermute | solution.py:122
  3.3 3.0 %collective-permute-start.1 = (f32[2,4,128,128]{3,2,1,0:T(8,128)}, f32[2,4,128,128]{3,2,1,0:T(8,128)S(1)}, u32[]{:S(2)}, u32[]{:S(2)}) collective-permute-start(f32[2,4,128,128]{3,2,1,0:T(8,128)} %own_ref.1), channel_id=1, source_target_pairs={{0,192},{64,0},{128,64},{192,128},{1,193},{65,1},{129,65},{193,129... | collective-permute-start | bytes 1572872 | tf_op jit(solution)/shard_map/ppermute | solution.py:122
  6.3 16.5 %collective-permute-done = f32[2,4,128,128]{3,2,1,0:T(8,128)S(1)} collective-permute-done((f32[2,4,128,128]{3,2,1,0:T(8,128)}, f32[2,4,128,128]{3,2,1,0:T(8,128)S(1)}, u32[]{:S(2)}, u32[]{:S(2)}) %collective-permute-start) | collective-permute-done | bytes 524320 | tf_op jit(solution)/shard_map/ppermute | solution.py:122
  22.8 8.1 %collective-permute-done.1 = f32[2,4,128,128]{3,2,1,0:T(8,128)S(1)} collective-permute-done((f32[2,4,128,128]{3,2,1,0:T(8,128)}, f32[2,4,128,128]{3,2,1,0:T(8,128)S(1)}, u32[]{:S(2)}, u32[]{:S(2)}) %collective-permute-start.1) | collective-permute-done | bytes 524320 | tf_op jit(solution)/shard_map/ppermute | solution.py:122
  30.9 3.7 %collective-permute-start.2 = (f32[1,4,128,128]{3,2,1,0:T(8,128)S(1)}, f32[1,4,128,128]{3,2,1,0:T(8,128)S(1)}, u32[]{:S(2)}, u32[]{:S(2)}) collective-permute-start(f32[1,4,128,128]{3,2,1,0:T(8,128)S(1)} %slice.6), channel_id=1, source_target_pairs={{0,64},{64,128},{128,192},{192,0},{1,65},{65,129},{129,193},{193,1... | collective-permute-start | bytes 786440 | tf_op jit(solution)/shard_map/ppermute | solution.py:122
  34.6 0.0 copy-start.8
  34.7 0.0 copy-start.9
  34.7 0.0 copy-start
  34.7 0.0 copy-start.5
  34.7 0.0 copy-start.6
  34.7 0.6 collective-permute-start.3
  35.3 1.1 constant_dynamic-update-slice_fusion.4
  36.4 8.9 %collective-permute-done.2 = f32[1,4,128,128]{3,2,1,0:T(8,128)S(1)} collective-permute-done((f32[1,4,128,128]{3,2,1,0:T(8,128)S(1)}, f32[1,4,128,128]{3,2,1,0:T(8,128)S(1)}, u32[]{:S(2)}, u32[]{:S(2)}) %collective-permute-start.2) | collective-permute-done | bytes 262176 | tf_op jit(solution)/shard_map/ppermute | solution.py:122
  45.3 0.3 collective-permute-done.3
  45.6 0.1 collective-permute-start.4
  45.7 0.0 copy-done.8
  45.8 0.0 copy-done.9
  45.8 4.2 %collective-permute-done.4.other_ref = f32[8,4,128,128]{3,2,1,0:T(8,128)} collective-permute-done((f32[8,4,128,128]{3,2,1,0:T(8,128)S(1)}, f32[8,4,128,128]{3,2,1,0:T(8,128)}, u32[]{:S(2)}, u32[]{:S(2)}) %collective-permute-start.4) | collective-permute-done | bytes 2097184 | tf_op jit(solution)/shard_map/ppermute | solution.py:122
  50.0 0.0 copy-done.5
  50.0 9.0 %shard_map.118 = f32[128,64,128]{2,1,0:T(8,128)} custom-call(s32[8]{0:T(128)S(1)} %get-tuple-element.10.place_ref, s32[8]{0:T(128)S(1)} %get-tuple-element.9.core_ref, f32[2,4,128,128]{3,2,1,0:T(8,128)S(1)} %copy-done, f32[8,4,128,128]{3,2,1,0:T(8,128)S(1)} %constant_dynamic-update-slice_fusion.mine_ref, ...), custom_call_target="tpu_custom_call" | custom-call | flops 2147483648 | bytes 8388608 | tf_op jit(solution)/shard_map/pallas_call | solution.py:169
  59.0 7.7 %all-to-all-start = ((f32[128,64,128]{2,1,0:T(8,128)}), f32[128,64,128]{2,1,0:T(8,128)}, u32[]{:S(2)}, u32[]{:S(2)}) async-start(f32[128,64,128]{2,1,0:T(8,128)} %shard_map.118), calls=%async_computation | async-start | bytes 8388608 | tf_op jit(solution)/shard_map/all_to_all | solution.py:181
  66.8 0.0 copy-done.10
  66.8 0.1 dynamic-slice_multiply_fusion
  66.9 0.1 broadcast_add_fusion
  67.0 0.1 compare_select_fusion.kernel_ref
  67.1 52.9 %all-to-all-done = f32[128,64,128]{2,1,0:T(8,128)} async-done(((f32[128,64,128]{2,1,0:T(8,128)}), f32[128,64,128]{2,1,0:T(8,128)}, u32[]{:S(2)}, u32[]{:S(2)}) %all-to-all-start) | async-done | bytes 4194336 | tf_op jit(solution)/shard_map/all_to_all | solution.py:181
  120.0 0.0 copy-done.4
  120.0 8.8 %shard_map.119 = f32[32,4,64,128]{3,2,1,0:T(8,128)S(1)} custom-call(f32[4,128,128]{2,1,0:T(8,128)S(1)} %compare_select_fusion.kernel_ref, bf16[256,256]{1,0:T(8,128)(2,1)S(1)} %copy-done.3, bf16[256,256]{1,0:T(8,128)(2,1)S(1)} %copy-done.4, f32[32,4,64,128]{3,2,1,0:T(8,128)} %bitcast.in_ref), custom_call_target="tpu_custom_call" | custom-call | flops 2147483648 | bytes 8388608 | tf_op jit(solution)/shard_map/pallas_call | solution.py:183
  128.7 0.0 copy-start.1
  128.8 0.0 copy-start.2
  128.8 60.0 %all_to_all.10.in_ref = f32[128,64,128]{2,1,0:T(8,128)} all-to-all(f32[128,64,128]{2,1,0:T(8,128)S(1)} %bitcast.2), channel_id=1, replica_groups=mesh['zh'=4,'core'=2,'grid'=32] {'grid'}, dimensions={0} | all-to-all | bytes 8388608 | tf_op jit(solution)/shard_map/all_to_all | solution.py:192
  188.7 9.0 %shard_map.120 = f32[2,4,128,128]{3,2,1,0:T(8,128)} custom-call(s32[8]{0:T(128)S(1)} %get-tuple-element.10.place_ref, s32[8]{0:T(128)S(1)} %get-tuple-element.9.core_ref, f32[128,64,128]{2,1,0:T(8,128)} %all_to_all.10.in_ref, f32[8,4,128,128]{3,2,1,0:T(8,128)S(1)} %constant_dynamic-update-slice_fusion.mine_ref, ...), custom_call_target="tpu_custom_call" | custom-call | flops 2147483648 | bytes 8388608 | tf_op jit(solution)/shard_map/pallas_call | solution.py:195
  (17 shorter events, 0.2 us)
Async XLA Ops:
  0.0 22.8 %collective-permute-start = (f32[2,4,128,128]{3,2,1,0:T(8,128)}, f32[2,4,128,128]{3,2,1,0:T(8,128)S(1)}, u32[]{:S(2)}, u32[]{:S(2)}) collective-permute-start(f32[2,4,128,128]{3,2,1,0:T(8,128)} %own_ref.1), channel_id=1, source_target_pairs={{0,64},{64,128},{128,192},{192,0},{1,65},{65,129},{129,193},{193,1... | collective-permute-start | bytes 1572872 | tf_op jit(solution)/shard_map/ppermute | solution.py:122
  3.3 27.6 %collective-permute-start.1 = (f32[2,4,128,128]{3,2,1,0:T(8,128)}, f32[2,4,128,128]{3,2,1,0:T(8,128)S(1)}, u32[]{:S(2)}, u32[]{:S(2)}) collective-permute-start(f32[2,4,128,128]{3,2,1,0:T(8,128)} %own_ref.1), channel_id=1, source_target_pairs={{0,192},{64,0},{128,64},{192,128},{1,193},{65,1},{129,65},{193,129... | collective-permute-start | bytes 1572872 | tf_op jit(solution)/shard_map/ppermute | solution.py:122
  30.9 14.4 %collective-permute-start.2 = (f32[1,4,128,128]{3,2,1,0:T(8,128)S(1)}, f32[1,4,128,128]{3,2,1,0:T(8,128)S(1)}, u32[]{:S(2)}, u32[]{:S(2)}) collective-permute-start(f32[1,4,128,128]{3,2,1,0:T(8,128)S(1)} %slice.6), channel_id=1, source_target_pairs={{0,64},{64,128},{128,192},{192,0},{1,65},{65,129},{129,193},{193,1... | collective-permute-start | bytes 786440 | tf_op jit(solution)/shard_map/ppermute | solution.py:122
  34.6 11.1 %copy-start.8 = (s32[8]{0:T(128)S(1)}, s32[8]{0:T(128)}, u32[]{:S(2)}) copy-start(s32[8]{0:T(128)} %param.13) | copy-start | bytes 100
  34.7 11.1 %copy-start.9 = (s32[8]{0:T(128)S(1)}, s32[8]{0:T(128)}, u32[]{:S(2)}) copy-start(s32[8]{0:T(128)} %param.14) | copy-start | bytes 100
  34.7 15.3 %copy-start = (f32[2,4,128,128]{3,2,1,0:T(8,128)S(1)}, f32[2,4,128,128]{3,2,1,0:T(8,128)}, u32[]{:S(2)}) copy-start(f32[2,4,128,128]{3,2,1,0:T(8,128)} %own_ref.1) | copy-start | bytes 1572868
  34.7 15.3 %copy-start.5 = (bf16[256,256]{1,0:T(8,128)(2,1)S(1)}, bf16[256,256]{1,0:T(8,128)(2,1)}, u32[]{:S(2)}) copy-start(bf16[256,256]{1,0:T(8,128)(2,1)} %constant.86.clone.wz_ref) | copy-start | bytes 393220
  34.7 15.3 %copy-start.6 = (bf16[256,256]{1,0:T(8,128)(2,1)S(1)}, bf16[256,256]{1,0:T(8,128)(2,1)}, u32[]{:S(2)}) copy-start(bf16[256,256]{1,0:T(8,128)(2,1)} %constant.87.clone.wy_ref) | copy-start | bytes 393220
  34.7 10.9 %collective-permute-start.3 = (f32[1,4,128,128]{3,2,1,0:T(8,128)S(1)}, f32[1,4,128,128]{3,2,1,0:T(8,128)S(1)}, u32[]{:S(2)}, u32[]{:S(2)}) collective-permute-start(f32[1,4,128,128]{3,2,1,0:T(8,128)S(1)} %slice.7), channel_id=1, source_target_pairs={{0,192},{64,0},{128,64},{192,128},{1,193},{65,1},{129,65},{193,129... | collective-permute-start | bytes 786440 | tf_op jit(solution)/shard_map/ppermute | solution.py:122
  45.6 4.4 %collective-permute-start.4 = (f32[8,4,128,128]{3,2,1,0:T(8,128)S(1)}, f32[8,4,128,128]{3,2,1,0:T(8,128)}, u32[]{:S(2)}, u32[]{:S(2)}) collective-permute-start(f32[8,4,128,128]{3,2,1,0:T(8,128)S(1)} %constant_dynamic-update-slice_fusion.mine_ref), channel_id=1, source_target_pairs={{0,32},{32,0},{1,33},{33,1},{2,34},{34,2},{3,35},{35,3},{4,36},{36... | collective-permute-start | bytes 6291464 | tf_op jit(solution)/shard_map/ppermute | solution.py:122
  59.0 7.8 %copy-start.10 = (f32[128]{0:T(128)S(1)}, f32[128]{0:T(128)}, u32[]{:S(2)}) copy-start(f32[128]{0:T(128)} %constant.83.clone) | copy-start | bytes 1540
  59.0 7.8 %copy-start.7 = (f32[128]{0:T(128)S(1)}, f32[128]{0:T(128)}, u32[]{:S(2)}) copy-start(f32[128]{0:T(128)} %constant.93) | copy-start | bytes 1540
  59.0 60.9 %copy-start.3 = (bf16[256,256]{1,0:T(8,128)(2,1)S(1)}, bf16[256,256]{1,0:T(8,128)(2,1)}, u32[]{:S(2)}) copy-start(bf16[256,256]{1,0:T(8,128)(2,1)} %constant.88.clone.wx_ref) | copy-start | bytes 393220
  59.0 60.9 %copy-start.4 = (bf16[256,256]{1,0:T(8,128)(2,1)S(1)}, bf16[256,256]{1,0:T(8,128)(2,1)}, u32[]{:S(2)}) copy-start(bf16[256,256]{1,0:T(8,128)(2,1)} %constant.89.clone.wxi_ref) | copy-start | bytes 393220
  59.0 60.9 %all-to-all-start = ((f32[128,64,128]{2,1,0:T(8,128)}), f32[128,64,128]{2,1,0:T(8,128)}, u32[]{:S(2)}, u32[]{:S(2)}) async-start(f32[128,64,128]{2,1,0:T(8,128)} %shard_map.118), calls=%async_computation | async-start | bytes 8388608 | tf_op jit(solution)/shard_map/all_to_all | solution.py:181
  128.7 60.0 %copy-start.1 = (bf16[256,256]{1,0:T(8,128)(2,1)S(1)}, bf16[256,256]{1,0:T(8,128)(2,1)}, u32[]{:S(2)}) copy-start(bf16[256,256]{1,0:T(8,128)(2,1)} %constant.90.clone.wz_ref) | copy-start | bytes 393220
  128.8 60.0 %copy-start.2 = (bf16[256,256]{1,0:T(8,128)(2,1)S(1)}, bf16[256,256]{1,0:T(8,128)(2,1)}, u32[]{:S(2)}) copy-start(bf16[256,256]{1,0:T(8,128)(2,1)} %constant.91.clone.wy_ref) | copy-start | bytes 393220

commit v3 on v2

v3 whole, which is shorter than its diff:
```python
import math

import jax
import jax.numpy as jnp
import ml_dtypes
import numpy as np
from jax import lax
from jax.experimental import pallas as pl
from jax.experimental.pallas import tpu as pltpu
from jax.sharding import PartitionSpec as P

CELL_EDGE = 46.9
GRID = "grid"


def basis(length):
    half = length // 2
    x = np.arange(length)
    rows = [np.full(length, 1.0 / math.sqrt(length))]
    rows += [math.sqrt(2.0 / length) * np.cos(2 * math.pi * (k * x % length) / length) for k in range(1, half)]
    rows += [(1.0 - 2.0 * (x % 2)) / math.sqrt(length)]
    rows += [math.sqrt(2.0 / length) * np.sin(2 * math.pi * (k * x % length) / length) for k in range(1, half)]
    freq = np.concatenate([np.arange(half + 1), np.arange(1, half)])
    return np.stack(rows), freq.astype(np.float32)


def halves(table):
    table = table.astype(np.float32)
    high = table.astype(ml_dtypes.bfloat16)
    return high, (table - high.astype(np.float32)).astype(ml_dtypes.bfloat16)


def left_table(table):
    high, low = halves(table)
    return np.block([[high, high], [low, low]])


def right_table(table):
    high, low = halves(table)
    return np.block([[high, low], [high, low]])


def split(values):
    high = values.astype(jnp.bfloat16)
    return high, (values - high.astype(jnp.float32)).astype(jnp.bfloat16)


def from_left(table, values):
    product = jnp.dot(table, jnp.concatenate(split(values), axis=0), preferred_element_type=jnp.float32)
    rows = product.shape[0] // 2
    return product[:rows] + product[rows:]


def from_right(values, table):
    product = jnp.dot(jnp.concatenate(split(values), axis=1), table, preferred_element_type=jnp.float32)
    columns = product.shape[1] // 2
    return product[:, :columns] + product[:, columns:]


def outward(place_ref, core_ref, own_ref, mine_ref, other_ref, wz_ref, wy_ref, out_ref):
    held, planes, ny, nz = own_ref.shape
    width = planes * held

    def one(r, carry):
        same = core_ref[r] == 0
        place = place_ref[r]
        done = []
        for p in range(planes):
            chosen = jnp.where(same, mine_ref[place, p], other_ref[place, p])
            rho = jnp.concatenate([own_ref[i, p] * chosen for i in range(held)], axis=0)
            rho = from_right(rho, wz_ref[...])
            rho = jnp.concatenate([rho[i * ny:(i + 1) * ny] for i in range(held)], axis=1)
            rho = from_left(wy_ref[...], rho)
            done += [rho[:, i * nz:(i + 1) * nz] for i in range(held)]
        out_ref[:, pl.ds(pl.multiple_of(r * width, width), width), :] = jnp.swapaxes(jnp.stack(done), 0, 1)
        return carry

    lax.fori_loop(0, out_ref.shape[1] // width, one, 0)


def middle(kernel_ref, wx_ref, wxi_ref, in_ref, out_ref):
    slabs, own_y, step, nz = in_ref.shape
    held, planes = 2, kernel_ref.shape[1] // slabs
    width = planes * held

    def one(r, carry):
        at = pl.ds(pl.multiple_of(r * width, width), width)
        for q in range(own_y):
            spec = jnp.swapaxes(in_ref[:, q, at, :], 0, 1).reshape(planes, held, slabs, nz)
            spec = jnp.concatenate([spec[:, i].reshape(planes * slabs, nz) for i in range(held)], axis=1)
            spec = from_left(wx_ref[...], spec)
            spec = spec * jnp.concatenate([kernel_ref[q]] * held, axis=1)
            spec = from_left(wxi_ref[...], spec)
            spec = jnp.stack([spec[:, i * nz:(i + 1) * nz].reshape(planes, slabs, nz) for i in range(held)], axis=1)
            out_ref[:, q, at, :] = jnp.swapaxes(spec.reshape(width, slabs, nz), 0, 1)
        return carry

    lax.fori_loop(0, step // width, one, 0)


def inward(place_ref, core_ref, in_ref, mine_ref, other_ref, wz_ref, wy_ref, out_ref):
    held, planes, ny, nz = out_ref.shape
    width = planes * held
    out_ref[...] = jnp.zeros_like(out_ref)

    def one(r, carry):
        same = core_ref[r] == 0
        place = place_ref[r]
        pots = jnp.swapaxes(in_ref[:, pl.ds(pl.multiple_of(r * width, width), width), :], 0, 1)
        for p in range(planes):
            chosen = jnp.where(same, mine_ref[place, p], other_ref[place, p])
            pot = jnp.concatenate([pots[p * held + i] for i in range(held)], axis=1)
            pot = from_left(wy_ref[...], pot)
            pot = jnp.concatenate([pot[:, i * nz:(i + 1) * nz] for i in range(held)], axis=0)
            pot = from_right(pot, wz_ref[...])
            for i in range(held):
                out_ref[i, p] -= chosen * pot[i * ny:(i + 1) * ny]
        return carry

    lax.fori_loop(0, in_ref.shape[1] // width, one, 0)


def rotated(array, axis, step):
    size = lax.axis_size(axis)
    return lax.ppermute(array, axis, [(i, (i + step) % size) for i in range(size)])


def every_orbital(own):
    held = own.shape[0] // 2
    below, above = lax.optimization_barrier((rotated(own, "zh", 1), rotated(own, "zh", -1)))
    far_below = rotated(below[:held], "zh", 1)
    far_above = rotated(above[held:], "zh", -1)
    mine = jnp.concatenate([own, above, far_below, far_above, below])
    return mine, rotated(mine, "core", 1)


def shards(orbitals, band_owner, block_index):
    held, planes, ny, nz = orbitals.shape
    rounds = band_owner.shape[0]
    grid = lax.axis_size(GRID)
    nx = planes * grid
    own_y = ny // grid
    width = planes * held
    tx, fx = basis(nx)
    ty, fy = basis(ny)
    tz, fz = basis(nz)
    tx = tx.reshape(nx, grid, planes).transpose(0, 2, 1).reshape(nx, nx)
    groups, cores = lax.axis_size("zh"), lax.axis_size("core")
    place = (band_owner // cores - lax.axis_index("zh")) % groups * held + block_index
    core_off = (band_owner + lax.axis_index("core")) % cores

    fy_own = lax.dynamic_slice_in_dim(jnp.asarray(fy), lax.axis_index(GRID) * own_y, own_y)
    scale = (2.0 * math.pi / CELL_EDGE) ** 2
    squared = scale * (fx[None, :, None] ** 2 + fy_own[:, None, None] ** 2 + fz[None, None, :] ** 2)
    guarded = jnp.where(squared > 0, squared, 1.0)
    kernel = jnp.where(squared > 0, 4.0 * math.pi / guarded, 0.0)

    mine, other = every_orbital(orbitals)
    kernel, other = lax.optimization_barrier((kernel, other))
    cells = rounds * held * planes * ny * nz
    vmem, smem = pl.BlockSpec(memory_space=pltpu.VMEM), pl.BlockSpec(memory_space=pltpu.SMEM)

    def call(body, shape, scalars, operands):
        return pl.pallas_call(
            body,
            in_specs=[smem] * len(scalars) + [vmem] * len(operands),
            out_specs=vmem,
            out_shape=jax.ShapeDtypeStruct(shape, jnp.float32),
            compiler_params=pltpu.CompilerParams(vmem_limit_bytes=24 * 2**20),
            cost_estimate=pl.CostEstimate(flops=16 * nz * cells, bytes_accessed=8 * cells, transcendentals=0),
        )(*scalars, *operands)

    scalars = (place, core_off)
    half = call(
        outward, (ny, rounds * width, nz), scalars, (orbitals, mine, other, right_table(tz.T), left_table(ty))
    )
    spec = lax.all_to_all(half, GRID, split_axis=0, concat_axis=0, tiled=True)
    strips = (grid, own_y, rounds * width, nz)
    spec = call(middle, strips, (), (kernel, left_table(tx), left_table(tx.T), spec.reshape(strips)))
    half = lax.all_to_all(
        spec.reshape(ny, rounds * width, nz), GRID, split_axis=0, concat_axis=0, tiled=True
    )
    return call(inward, orbitals.shape, scalars, (half, mine, other, right_table(tz), left_table(ty.T)))


def solution(mesh):
    parts = jax.sharding.Mesh(mesh.devices.reshape(4, 2, 32), ("zh", "core", GRID))
    placed = P(("zh", "core"), GRID, None, None)
    return jax.shard_map(
        shards,
        mesh=parts,
        in_specs=(placed, P(), P()),
        out_specs=placed,
        check_vma=False,
    )
```

time: 199 us -> 185 us (0.930)
  blocking collectives: 60 us -> 113 us
  waiting for transfers between devices: 90.8 us -> 38.7 us
  starting transfers between devices: 18.4 us -> 10.7 us
  Pallas kernels: 26.7 us -> 20.2 us
    all_to_all x0 -> x1, blocking collectives: none -> 58.5 us  [shards(): spec = lax.all_to_all(half, GRID, split_axis=0, concat_axis=0, tiled=True)]
    all_to_all x1 -> x0, waiting for transfers between devices: 52.9 us -> none  [shards(): spec = lax.all_to_all(half, GRID, split_axis=0, concat_axis=0, tiled=True)]
    all_to_all x1 -> x0, starting transfers between devices: 7.73 us -> none  [shards(): spec = lax.all_to_all(half, GRID, split_axis=0, concat_axis=0, tiled=True)]
    pallas_call x3, Pallas kernels: 26.7 us -> 20.2 us  [call(): pl.pallas_call(body, in_specs=[smem] * len(scalars) + [vmem] * len(operan...]
    all_to_all x1, blocking collectives: 60 us -> 54.9 us  [shards(): lax.all_to_all(spec.reshape(ny, rounds * width, nz), GRID, split_axis=0,...]
  transfers between devices with their start and end apart: 6 -> 5, of which waited for: 6 -> 5; matrix products, arithmetic and copies ran while one was open for 1% -> 1% of each run, Pallas kernels for 0% -> 0%
where the time goes in v3:
time: 185 us
  blocking collectives  113 us (61%)
  waiting for transfers between devices  38.7 us (21%)
  Pallas kernels  20.2 us (11%)
  starting transfers between devices  10.7 us (6%)
    all_to_all x1, blocking collectives, shards(): spec = lax.all_to_all(half, GRID, split_axis=0, concat_axis=0, tiled=True)  58.5 us
    all_to_all x1, blocking collectives, shards(): lax.all_to_all(spec.reshape(ny, rounds * width, nz), GRID, split_axis=0,...  54.9 us
    ppermute x5, waiting for transfers between devices, rotated(): lax.ppermute(array, axis, [(i, (i + step) % size) for i in range(size)])  38.7 us
    pallas_call x3, Pallas kernels, call(): pl.pallas_call(body, in_specs=[smem] * len(scalars) + [vmem] * len(operan...  20.2 us
    ppermute x5, starting transfers between devices, rotated(): lax.ppermute(array, axis, [(i, (i + step) % size) for i in range(size)])  10.7 us
  transfers between devices with their start and end apart: 5, of which 5 were waited for; matrix products, arithmetic and copies ran while one was open for 1% of the time, Pallas kernels for 0%

profile of v3, /device:TPU:8, one launch (start us, length us, event | category | flops | bytes accessed | tf_op | source)
XLA Modules:
  0.0 184.8 jit_solution(15276844121684894156)
XLA Ops:
  0.0 6.3 %collective-permute-start.1 = (f32[2,4,128,128]{3,2,1,0:T(8,128)}, f32[2,4,128,128]{3,2,1,0:T(8,128)S(1)}, u32[]{:S(2)}, u32[]{:S(2)}) collective-permute-start(f32[2,4,128,128]{3,2,1,0:T(8,128)} %own_ref.1), channel_id=1, source_target_pairs={{0,192},{64,0},{128,64},{192,128},{1,193},{65,1},{129,65},{193,129... | collective-permute-start | bytes 1572872 | tf_op jit(solution)/shard_map/ppermute | solution.py:125
  6.3 0.0 collective-permute-start
  6.3 22.8 %collective-permute-done.1 = f32[2,4,128,128]{3,2,1,0:T(8,128)S(1)} collective-permute-done((f32[2,4,128,128]{3,2,1,0:T(8,128)}, f32[2,4,128,128]{3,2,1,0:T(8,128)S(1)}, u32[]{:S(2)}, u32[]{:S(2)}) %collective-permute-start.1) | collective-permute-done | bytes 524320 | tf_op jit(solution)/shard_map/ppermute | solution.py:125
  29.1 3.7 %collective-permute-done = f32[2,4,128,128]{3,2,1,0:T(8,128)S(1)} collective-permute-done((f32[2,4,128,128]{3,2,1,0:T(8,128)}, f32[2,4,128,128]{3,2,1,0:T(8,128)S(1)}, u32[]{:S(2)}, u32[]{:S(2)}) %collective-permute-start) | collective-permute-done | bytes 524320 | tf_op jit(solution)/shard_map/ppermute | solution.py:125
  32.8 0.1 collective-permute-start.2
  32.9 0.0 copy-start.10
  32.9 0.0 copy-start.8
  33.0 0.0 copy-start.9
  33.0 0.0 copy-start.7
  33.0 0.0 copy-start
  33.0 0.0 copy-start.5
  33.0 0.0 copy-start.6
  33.0 4.2 %collective-permute-start.3 = (f32[1,4,128,128]{3,2,1,0:T(8,128)S(1)}, f32[1,4,128,128]{3,2,1,0:T(8,128)S(1)}, u32[]{:S(2)}, u32[]{:S(2)}) collective-permute-start(f32[1,4,128,128]{3,2,1,0:T(8,128)S(1)} %slice.7), channel_id=1, source_target_pairs={{0,192},{64,0},{128,64},{192,128},{1,193},{65,1},{129,65},{193,129... | collective-permute-start | bytes 786440 | tf_op jit(solution)/shard_map/ppermute | solution.py:125
  37.2 1.1 constant_dynamic-update-slice_fusion.4
  38.3 3.1 %collective-permute-done.2 = f32[1,4,128,128]{3,2,1,0:T(8,128)S(1)} collective-permute-done((f32[1,4,128,128]{3,2,1,0:T(8,128)S(1)}, f32[1,4,128,128]{3,2,1,0:T(8,128)S(1)}, u32[]{:S(2)}, u32[]{:S(2)}) %collective-permute-start.2) | collective-permute-done | bytes 262176 | tf_op jit(solution)/shard_map/ppermute | solution.py:125
  41.5 5.1 %collective-permute-done.3 = f32[1,4,128,128]{3,2,1,0:T(8,128)S(1)} collective-permute-done((f32[1,4,128,128]{3,2,1,0:T(8,128)S(1)}, f32[1,4,128,128]{3,2,1,0:T(8,128)S(1)}, u32[]{:S(2)}, u32[]{:S(2)}) %collective-permute-start.3) | collective-permute-done | bytes 262176 | tf_op jit(solution)/shard_map/ppermute | solution.py:125
  46.7 0.1 collective-permute-start.4
  46.8 0.1 dynamic-slice_multiply_fusion
  46.9 0.0 copy-done.9
  46.9 0.1 broadcast_add_fusion
  47.0 0.1 compare_select_fusion.kernel_ref
  47.1 3.9 %collective-permute-done.4.other_ref = f32[8,4,128,128]{3,2,1,0:T(8,128)} collective-permute-done((f32[8,4,128,128]{3,2,1,0:T(8,128)S(1)}, f32[8,4,128,128]{3,2,1,0:T(8,128)}, u32[]{:S(2)}, u32[]{:S(2)}) %collective-permute-start.4) | collective-permute-done | bytes 2097184 | tf_op jit(solution)/shard_map/ppermute | solution.py:125
  51.1 0.0 copy-done
  51.1 7.0 %shard_map.118 = f32[128,64,128]{2,1,0:T(8,128)S(1)} custom-call(s32[8]{0:T(128)S(1)} %get-tuple-element.14.place_ref, s32[8]{0:T(128)S(1)} %get-tuple-element.13.core_ref, f32[2,4,128,128]{3,2,1,0:T(8,128)S(1)} %copy-done, f32[8,4,128,128]{3,2,1,0:T(8,128)S(1)} %constant_dynamic-update-slice_fusion.mine_ref, ...), custom_call_target="tpu_custom_call" | custom-call | flops 2147483648 | bytes 8388608 | tf_op jit(solution)/shard_map/pallas_call | solution.py:164
  58.1 0.0 copy-start.3
  58.1 0.0 copy-start.4
  58.1 58.5 %all_to_all.10 = f32[128,64,128]{2,1,0:T(8,128)S(1)} all-to-all(f32[128,64,128]{2,1,0:T(8,128)S(1)} %shard_map.118), channel_id=1, replica_groups=mesh['zh'=4,'core'=2,'grid'=32] {'grid'}, dimensions={0} | all-to-all | bytes 8388608 | tf_op jit(solution)/shard_map/all_to_all | solution.py:177
  116.7 5.5 %shard_map.119 = f32[32,4,64,128]{3,2,1,0:T(8,128)S(1)} custom-call(f32[4,128,128]{2,1,0:T(8,128)S(1)} %compare_select_fusion.kernel_ref, bf16[256,256]{1,0:T(8,128)(2,1)S(1)} %copy-done.4, bf16[256,256]{1,0:T(8,128)(2,1)S(1)} %copy-done.3, f32[32,4,64,128]{3,2,1,0:T(8,128)S(1)} %bitcast.2), custom_call_target="tpu_custom_call" | custom-call | flops 2147483648 | bytes 8388608 | tf_op jit(solution)/shard_map/pallas_call | solution.py:164
  122.2 0.0 copy-start.1
  122.2 0.0 copy-start.2
  122.2 54.9 %all_to_all.11.in_ref = f32[128,64,128]{2,1,0:T(8,128)S(1)} all-to-all(f32[128,64,128]{2,1,0:T(8,128)S(1)} %bitcast.3), channel_id=1, replica_groups=mesh['zh'=4,'core'=2,'grid'=32] {'grid'}, dimensions={0} | all-to-all | bytes 8388608 | tf_op jit(solution)/shard_map/all_to_all | solution.py:180
  177.1 7.7 %shard_map.120 = f32[2,4,128,128]{3,2,1,0:T(8,128)} custom-call(s32[8]{0:T(128)S(1)} %get-tuple-element.14.place_ref, s32[8]{0:T(128)S(1)} %get-tuple-element.13.core_ref, f32[128,64,128]{2,1,0:T(8,128)S(1)} %all_to_all.11.in_ref, f32[8,4,128,128]{3,2,1,0:T(8,128)S(1)} %constant_dynamic-update-slice_fusion.mine_ref, ...), custom_call_target="tpu_custom_call" | custom-call | flops 2147483648 | bytes 8388608 | tf_op jit(solution)/shard_map/pallas_call | solution.py:164
  (16 shorter events, 0.2 us)
Async XLA Ops:
  0.0 29.1 %collective-permute-start.1 = (f32[2,4,128,128]{3,2,1,0:T(8,128)}, f32[2,4,128,128]{3,2,1,0:T(8,128)S(1)}, u32[]{:S(2)}, u32[]{:S(2)}) collective-permute-start(f32[2,4,128,128]{3,2,1,0:T(8,128)} %own_ref.1), channel_id=1, source_target_pairs={{0,192},{64,0},{128,64},{192,128},{1,193},{65,1},{129,65},{193,129... | collective-permute-start | bytes 1572872 | tf_op jit(solution)/shard_map/ppermute | solution.py:125
  6.3 26.5 %collective-permute-start = (f32[2,4,128,128]{3,2,1,0:T(8,128)}, f32[2,4,128,128]{3,2,1,0:T(8,128)S(1)}, u32[]{:S(2)}, u32[]{:S(2)}) collective-permute-start(f32[2,4,128,128]{3,2,1,0:T(8,128)} %own_ref.1), channel_id=1, source_target_pairs={{0,64},{64,128},{128,192},{192,0},{1,65},{65,129},{129,193},{193,1... | collective-permute-start | bytes 1572872 | tf_op jit(solution)/shard_map/ppermute | solution.py:125
  32.8 8.7 %collective-permute-start.2 = (f32[1,4,128,128]{3,2,1,0:T(8,128)S(1)}, f32[1,4,128,128]{3,2,1,0:T(8,128)S(1)}, u32[]{:S(2)}, u32[]{:S(2)}) collective-permute-start(f32[1,4,128,128]{3,2,1,0:T(8,128)S(1)} %slice.6), channel_id=1, source_target_pairs={{0,64},{64,128},{128,192},{192,0},{1,65},{65,129},{129,193},{193,1... | collective-permute-start | bytes 786440 | tf_op jit(solution)/shard_map/ppermute | solution.py:125
  32.9 13.9 %copy-start.10 = (f32[128]{0:T(128)S(1)}, f32[128]{0:T(128)}, u32[]{:S(2)}) copy-start(f32[128]{0:T(128)} %constant.83.clone) | copy-start | bytes 1540
  32.9 13.9 %copy-start.8 = (s32[8]{0:T(128)S(1)}, s32[8]{0:T(128)}, u32[]{:S(2)}) copy-start(s32[8]{0:T(128)} %param.13) | copy-start | bytes 100
  33.0 13.9 %copy-start.9 = (s32[8]{0:T(128)S(1)}, s32[8]{0:T(128)}, u32[]{:S(2)}) copy-start(s32[8]{0:T(128)} %param.14) | copy-start | bytes 100
  33.0 13.9 %copy-start.7 = (f32[128]{0:T(128)S(1)}, f32[128]{0:T(128)}, u32[]{:S(2)}) copy-start(f32[128]{0:T(128)} %constant.93) | copy-start | bytes 1540
  33.0 18.1 %copy-start = (f32[2,4,128,128]{3,2,1,0:T(8,128)S(1)}, f32[2,4,128,128]{3,2,1,0:T(8,128)}, u32[]{:S(2)}) copy-start(f32[2,4,128,128]{3,2,1,0:T(8,128)} %own_ref.1) | copy-start | bytes 1572868
  33.0 18.1 %copy-start.5 = (bf16[256,256]{1,0:T(8,128)(2,1)S(1)}, bf16[256,256]{1,0:T(8,128)(2,1)}, u32[]{:S(2)}) copy-start(bf16[256,256]{1,0:T(8,128)(2,1)} %constant.87.clone.wy_ref) | copy-start | bytes 393220
  33.0 18.1 %copy-start.6 = (bf16[256,256]{1,0:T(8,128)(2,1)S(1)}, bf16[256,256]{1,0:T(8,128)(2,1)}, u32[]{:S(2)}) copy-start(bf16[256,256]{1,0:T(8,128)(2,1)} %constant.86.clone.wz_ref) | copy-start | bytes 393220
  33.0 13.6 %collective-permute-start.3 = (f32[1,4,128,128]{3,2,1,0:T(8,128)S(1)}, f32[1,4,128,128]{3,2,1,0:T(8,128)S(1)}, u32[]{:S(2)}, u32[]{:S(2)}) collective-permute-start(f32[1,4,128,128]{3,2,1,0:T(8,128)S(1)} %slice.7), channel_id=1, source_target_pairs={{0,192},{64,0},{128,64},{192,128},{1,193},{65,1},{129,65},{193,129... | collective-permute-start | bytes 786440 | tf_op jit(solution)/shard_map/ppermute | solution.py:125
  46.7 4.4 %collective-permute-start.4 = (f32[8,4,128,128]{3,2,1,0:T(8,128)S(1)}, f32[8,4,128,128]{3,2,1,0:T(8,128)}, u32[]{:S(2)}, u32[]{:S(2)}) collective-permute-start(f32[8,4,128,128]{3,2,1,0:T(8,128)S(1)} %constant_dynamic-update-slice_fusion.mine_ref), channel_id=1, source_target_pairs={{0,32},{32,0},{1,33},{33,1},{2,34},{34,2},{3,35},{35,3},{4,36},{36... | collective-permute-start | bytes 6291464 | tf_op jit(solution)/shard_map/ppermute | solution.py:125
  58.1 58.6 %copy-start.3 = (bf16[256,256]{1,0:T(8,128)(2,1)S(1)}, bf16[256,256]{1,0:T(8,128)(2,1)}, u32[]{:S(2)}) copy-start(bf16[256,256]{1,0:T(8,128)(2,1)} %constant.89.clone.wxi_ref) | copy-start | bytes 393220
  58.1 58.5 %copy-start.4 = (bf16[256,256]{1,0:T(8,128)(2,1)S(1)}, bf16[256,256]{1,0:T(8,128)(2,1)}, u32[]{:S(2)}) copy-start(bf16[256,256]{1,0:T(8,128)(2,1)} %constant.88.clone.wx_ref) | copy-start | bytes 393220
  122.2 54.9 %copy-start.1 = (bf16[256,256]{1,0:T(8,128)(2,1)S(1)}, bf16[256,256]{1,0:T(8,128)(2,1)}, u32[]{:S(2)}) copy-start(bf16[256,256]{1,0:T(8,128)(2,1)} %constant.91.clone.wy_ref) | copy-start | bytes 393220
  122.2 54.9 %copy-start.2 = (bf16[256,256]{1,0:T(8,128)(2,1)S(1)}, bf16[256,256]{1,0:T(8,128)(2,1)}, u32[]{:S(2)}) copy-start(bf16[256,256]{1,0:T(8,128)(2,1)} %constant.90.clone.wz_ref) | copy-start | bytes 393220

commit v4 on v3

--- a/solution.py
+++ b/solution.py
@@ -11,6 +11,7 @@
 
 CELL_EDGE = 46.9
 GRID = "grid"
+UNROLL = 8
 
 
 def basis(length):
@@ -57,7 +58,7 @@
     return product[:, :columns] + product[:, columns:]
 
 
-def outward(place_ref, core_ref, own_ref, mine_ref, other_ref, wz_ref, wy_ref, out_ref):
+def outward(place_ref, core_ref, own_ref, mine_ref, other_ref, wz_ref, wy_ref, out_ref, chosen_ref):
     held, planes, ny, nz = own_ref.shape
     width = planes * held
 
@@ -67,6 +68,7 @@
         done = []
         for p in range(planes):
             chosen = jnp.where(same, mine_ref[place, p], other_ref[place, p])
+            chosen_ref[r, p] = chosen
             rho = jnp.concatenate([own_ref[i, p] * chosen for i in range(held)], axis=0)
             rho = from_right(rho, wz_ref[...])
             rho = jnp.concatenate([rho[i * ny:(i + 1) * ny] for i in range(held)], axis=1)
@@ -75,7 +77,7 @@
         out_ref[:, pl.ds(pl.multiple_of(r * width, width), width), :] = jnp.swapaxes(jnp.stack(done), 0, 1)
         return carry
 
-    lax.fori_loop(0, out_ref.shape[1] // width, one, 0)
+    lax.fori_loop(0, out_ref.shape[1] // width, one, 0, unroll=UNROLL)
 
 
 def middle(kernel_ref, wx_ref, wxi_ref, in_ref, out_ref):
@@ -95,29 +97,26 @@
             out_ref[:, q, at, :] = jnp.swapaxes(spec.reshape(width, slabs, nz), 0, 1)
         return carry
 
-    lax.fori_loop(0, step // width, one, 0)
-
-
-def inward(place_ref, core_ref, in_ref, mine_ref, other_ref, wz_ref, wy_ref, out_ref):
+    lax.fori_loop(0, step // width, one, 0, unroll=UNROLL)
+
+
+def inward(in_ref, chosen_ref, wz_ref, wy_ref, out_ref):
     held, planes, ny, nz = out_ref.shape
     width = planes * held
     out_ref[...] = jnp.zeros_like(out_ref)
 
     def one(r, carry):
-        same = core_ref[r] == 0
-        place = place_ref[r]
         pots = jnp.swapaxes(in_ref[:, pl.ds(pl.multiple_of(r * width, width), width), :], 0, 1)
         for p in range(planes):
-            chosen = jnp.where(same, mine_ref[place, p], other_ref[place, p])
             pot = jnp.concatenate([pots[p * held + i] for i in range(held)], axis=1)
             pot = from_left(wy_ref[...], pot)
             pot = jnp.concatenate([pot[:, i * nz:(i + 1) * nz] for i in range(held)], axis=0)
             pot = from_right(pot, wz_ref[...])
             for i in range(held):
-                out_ref[i, p] -= chosen * pot[i * ny:(i + 1) * ny]
+                out_ref[i, p] -= chosen_ref[r, p] * pot[i * ny:(i + 1) * ny]
         return carry
 
-    lax.fori_loop(0, in_ref.shape[1] // width, one, 0)
+    lax.fori_loop(0, in_ref.shape[1] // width, one, 0, unroll=UNROLL)
 
 
 def rotated(array, axis, step):
@@ -144,12 +143,14 @@
     tx, fx = basis(nx)
     ty, fy = basis(ny)
     tz, fz = basis(nz)
-    tx = tx.reshape(nx, grid, planes).transpose(0, 2, 1).reshape(nx, nx)
+    order = np.arange(grid).reshape(-1, 4, 4).transpose(2, 1, 0).reshape(grid)
+    tx = tx.reshape(nx, grid, planes)[:, order].transpose(0, 2, 1).reshape(nx, nx)
     groups, cores = lax.axis_size("zh"), lax.axis_size("core")
     place = (band_owner // cores - lax.axis_index("zh")) % groups * held + block_index
     core_off = (band_owner + lax.axis_index("core")) % cores
 
-    fy_own = lax.dynamic_slice_in_dim(jnp.asarray(fy), lax.axis_index(GRID) * own_y, own_y)
+    spot = jnp.asarray(np.argsort(order).astype(np.int32))[lax.axis_index(GRID)]
+    fy_own = lax.dynamic_slice_in_dim(jnp.asarray(fy), spot * own_y, own_y)
     scale = (2.0 * math.pi / CELL_EDGE) ** 2
     squared = scale * (fx[None, :, None] ** 2 + fy_own[:, None, None] ** 2 + fz[None, None, :] ** 2)
     guarded = jnp.where(squared > 0, squared, 1.0)
@@ -160,27 +161,34 @@
     cells = rounds * held * planes * ny * nz
     vmem, smem = pl.BlockSpec(memory_space=pltpu.VMEM), pl.BlockSpec(memory_space=pltpu.SMEM)
 
-    def call(body, shape, scalars, operands):
+    def call(body, shapes, scalars, operands):
         return pl.pallas_call(
             body,
             in_specs=[smem] * len(scalars) + [vmem] * len(operands),
-            out_specs=vmem,
-            out_shape=jax.ShapeDtypeStruct(shape, jnp.float32),
-            compiler_params=pltpu.CompilerParams(vmem_limit_bytes=24 * 2**20),
+            out_specs=[vmem] * len(shapes),
+            out_shape=[jax.ShapeDtypeStruct(shape, jnp.float32) for shape in shapes],
+            compiler_params=pltpu.CompilerParams(vmem_limit_bytes=16 * 2**20),
             cost_estimate=pl.CostEstimate(flops=16 * nz * cells, bytes_accessed=8 * cells, transcendentals=0),
         )(*scalars, *operands)
 
-    scalars = (place, core_off)
-    half = call(
-        outward, (ny, rounds * width, nz), scalars, (orbitals, mine, other, right_table(tz.T), left_table(ty))
+    def exchange(array):
+        return lax.all_to_all(
+            array, GRID, split_axis=0, concat_axis=0, tiled=True, axis_index_groups=[order.tolist()]
+        )
+
+    sent = (ny, rounds * width, nz)
+    half, chosen = call(
+        outward,
+        [sent, (rounds, planes, ny, nz)],
+        (place, core_off),
+        (orbitals, mine, other, right_table(tz.T), left_table(ty)),
     )
-    spec = lax.all_to_all(half, GRID, split_axis=0, concat_axis=0, tiled=True)
     strips = (grid, own_y, rounds * width, nz)
-    spec = call(middle, strips, (), (kernel, left_table(tx), left_table(tx.T), spec.reshape(strips)))
-    half = lax.all_to_all(
-        spec.reshape(ny, rounds * width, nz), GRID, split_axis=0, concat_axis=0, tiled=True
-    )
-    return call(inward, orbitals.shape, scalars, (half, mine, other, right_table(tz), left_table(ty.T)))
+    spec = exchange(half).reshape(strips)
+    (spec,) = call(middle, [strips], (), (kernel, left_table(tx), left_table(tx.T), spec))
+    half = exchange(spec.reshape(sent))
+    (out,) = call(inward, [orbitals.shape], (), (half, chosen, right_table(tz), left_table(ty.T)))
+    return out
 
 
 def solution(mesh):

time: 185 us -> 177 us (0.957)
  Pallas kernels: 20.2 us -> 11.8 us
    pallas_call x3, Pallas kernels: 20.2 us -> 11.8 us  [call(): pl.pallas_call(body, in_specs=[smem] * len(scalars) + [vmem] * len(operan...]
where the time goes in v4:
time: 177 us
  blocking collectives  114 us (64%)
  waiting for transfers between devices  37.4 us (21%)
  Pallas kernels  11.8 us (7%)
  starting transfers between devices  10.7 us (6%)
  local copies, waits for them, and re-layouts  1.89 us (1%)
    all_to_all x2, blocking collectives, exchange(): lax.all_to_all(array, GRID, split_axis=0, concat_axis=0, tiled=True, axis...  114 us
    ppermute x5, waiting for transfers between devices, rotated(): lax.ppermute(array, axis, [(i, (i + step) % size) for i in range(size)])  37.4 us
    pallas_call x3, Pallas kernels, call(): pl.pallas_call(body, in_specs=[smem] * len(scalars) + [vmem] * len(operan...  11.8 us
    ppermute x5, starting transfers between devices, rotated(): lax.ppermute(array, axis, [(i, (i + step) % size) for i in range(size)])  10.7 us
  transfers between devices with their start and end apart: 5, of which 5 were waited for; matrix products, arithmetic and copies ran while one was open for 1% of the time, Pallas kernels for 0%

profile of v4, /device:TPU:8, one launch (start us, length us, event | category | flops | bytes accessed | tf_op | source)
XLA Modules:
  0.0 176.5 jit_solution(8210624648832709773)
XLA Ops:
  0.0 6.3 %collective-permute-start.1 = (f32[2,4,128,128]{3,2,1,0:T(8,128)}, f32[2,4,128,128]{3,2,1,0:T(8,128)S(1)}, u32[]{:S(2)}, u32[]{:S(2)}) collective-permute-start(f32[2,4,128,128]{3,2,1,0:T(8,128)} %own_ref.1), channel_id=1, source_target_pairs={{0,192},{64,0},{128,64},{192,128},{1,193},{65,1},{129,65},{193,129... | collective-permute-start | bytes 1572872 | tf_op jit(solution)/shard_map/ppermute | solution.py:124
  6.3 0.0 collective-permute-start
  6.3 22.8 %collective-permute-done.1 = f32[2,4,128,128]{3,2,1,0:T(8,128)S(1)} collective-permute-done((f32[2,4,128,128]{3,2,1,0:T(8,128)}, f32[2,4,128,128]{3,2,1,0:T(8,128)S(1)}, u32[]{:S(2)}, u32[]{:S(2)}) %collective-permute-start.1) | collective-permute-done | bytes 524320 | tf_op jit(solution)/shard_map/ppermute | solution.py:124
  29.1 3.7 %collective-permute-done = f32[2,4,128,128]{3,2,1,0:T(8,128)S(1)} collective-permute-done((f32[2,4,128,128]{3,2,1,0:T(8,128)}, f32[2,4,128,128]{3,2,1,0:T(8,128)S(1)}, u32[]{:S(2)}, u32[]{:S(2)}) %collective-permute-start) | collective-permute-done | bytes 524320 | tf_op jit(solution)/shard_map/ppermute | solution.py:124
  32.8 0.1 collective-permute-start.2
  32.9 0.0 copy-start.11
  32.9 0.0 copy-start.10
  33.0 0.0 copy-start.8
  33.0 0.0 copy-start.9
  33.0 0.0 copy-start.7
  33.0 0.0 copy-start
  33.0 0.0 copy-start.5
  33.0 0.0 copy-start.6
  33.0 4.2 %collective-permute-start.3 = (f32[1,4,128,128]{3,2,1,0:T(8,128)S(1)}, f32[1,4,128,128]{3,2,1,0:T(8,128)S(1)}, u32[]{:S(2)}, u32[]{:S(2)}) collective-permute-start(f32[1,4,128,128]{3,2,1,0:T(8,128)S(1)} %slice.7), channel_id=1, source_target_pairs={{0,192},{64,0},{128,64},{192,128},{1,193},{65,1},{129,65},{193,129... | collective-permute-start | bytes 786440 | tf_op jit(solution)/shard_map/ppermute | solution.py:124
  37.2 1.1 constant_dynamic-update-slice_fusion.4
  38.4 3.1 %collective-permute-done.2 = f32[1,4,128,128]{3,2,1,0:T(8,128)S(1)} collective-permute-done((f32[1,4,128,128]{3,2,1,0:T(8,128)S(1)}, f32[1,4,128,128]{3,2,1,0:T(8,128)S(1)}, u32[]{:S(2)}, u32[]{:S(2)}) %collective-permute-start.2) | collective-permute-done | bytes 262176 | tf_op jit(solution)/shard_map/ppermute | solution.py:124
  41.5 5.1 %collective-permute-done.3 = f32[1,4,128,128]{3,2,1,0:T(8,128)S(1)} collective-permute-done((f32[1,4,128,128]{3,2,1,0:T(8,128)S(1)}, f32[1,4,128,128]{3,2,1,0:T(8,128)S(1)}, u32[]{:S(2)}, u32[]{:S(2)}) %collective-permute-start.3) | collective-permute-done | bytes 262176 | tf_op jit(solution)/shard_map/ppermute | solution.py:124
  46.7 0.1 collective-permute-start.4
  46.8 0.6 dynamic_slice.6
  48.1 0.1 dynamic-slice_multiply_fusion
  48.2 0.1 broadcast_add_fusion
  48.3 0.1 compare_select_fusion.kernel_ref
  48.4 2.7 %collective-permute-done.4.other_ref = f32[8,4,128,128]{3,2,1,0:T(8,128)} collective-permute-done((f32[8,4,128,128]{3,2,1,0:T(8,128)S(1)}, f32[8,4,128,128]{3,2,1,0:T(8,128)}, u32[]{:S(2)}, u32[]{:S(2)}) %collective-permute-start.4) | collective-permute-done | bytes 2097184 | tf_op jit(solution)/shard_map/ppermute | solution.py:124
  51.1 4.7 %shard_map.127 = (f32[128,64,128]{2,1,0:T(8,128)S(1)}, f32[8,4,128,128]{3,2,1,0:T(8,128)S(1)}) custom-call(s32[8]{0:T(128)S(1)} %get-tuple-element.18.place_ref, s32[8]{0:T(128)S(1)} %get-tuple-element.17.core_ref, f32[2,4,128,128]{3,2,1,0:T(8,128)S(1)} %copy-done, f32[8,4,128,128]{3,2,1,0:T(8,128)S(1)} %constant_dynamic-update-slice_fusion.mine_ref, ...), custom_call_target="tpu_custom_call" | custom-call | flops 2147483648 | bytes 8388608 | tf_op jit(solution)/shard_map/pallas_call | solution.py:165
  55.8 0.0 copy-start.1
  55.9 0.0 copy-start.2
  55.9 59.5 %all_to_all.10 = f32[128,64,128]{2,1,0:T(8,128)S(1)} all-to-all(f32[128,64,128]{2,1,0:T(8,128)S(1)} %get-tuple-element.15), channel_id=1, replica_groups={{0,16,4,20,8,24,12,28,1,17,5,21,9,25,13,29,2,18,6,22,10,26,14,30,3,19,7..., dimensions={0} | all-to-all | bytes 8388608 | tf_op jit(solution)/shard_map/all_to_all | solution.py:175
  115.4 3.2 %shard_map.128 = f32[32,4,64,128]{3,2,1,0:T(8,128)S(1)} custom-call(f32[4,128,128]{2,1,0:T(8,128)S(1)} %compare_select_fusion.kernel_ref, bf16[256,256]{1,0:T(8,128)(2,1)S(1)} %copy-done.2, bf16[256,256]{1,0:T(8,128)(2,1)S(1)} %copy-done.1, f32[32,4,64,128]{3,2,1,0:T(8,128)S(1)} %bitcast.3), custom_call_target="tpu_custom_call" | custom-call | flops 2147483648 | bytes 8388608 | tf_op jit(solution)/shard_map/pallas_call | solution.py:165
  118.6 0.0 copy-start.3
  118.6 0.0 copy-start.4
  118.6 54.0 %all_to_all.11.in_ref = f32[128,64,128]{2,1,0:T(8,128)S(1)} all-to-all(f32[128,64,128]{2,1,0:T(8,128)S(1)} %bitcast.4), channel_id=1, replica_groups={{0,16,4,20,8,24,12,28,1,17,5,21,9,25,13,29,2,18,6,22,10,26,14,30,3,19,7..., dimensions={0} | all-to-all | bytes 8388608 | tf_op jit(solution)/shard_map/all_to_all | solution.py:175
  172.7 3.9 %shard_map.129 = f32[2,4,128,128]{3,2,1,0:T(8,128)} custom-call(f32[128,64,128]{2,1,0:T(8,128)S(1)} %all_to_all.11.in_ref, f32[8,4,128,128]{3,2,1,0:T(8,128)S(1)} %get-tuple-element.16.chosen_ref, bf16[256,256]{1,0:T(8,128)(2,1)S(1)} %copy-done.4, bf16[256,256]{1,0:T(8,128)(2,1)S(1)} %copy-done.3), custom_call_target="tpu_custom_call" | custom-call | flops 2147483648 | bytes 8388608 | tf_op jit(solution)/shard_map/pallas_call | solution.py:165
  (19 shorter events, 0.2 us)
Async XLA Ops:
  0.0 29.1 %collective-permute-start.1 = (f32[2,4,128,128]{3,2,1,0:T(8,128)}, f32[2,4,128,128]{3,2,1,0:T(8,128)S(1)}, u32[]{:S(2)}, u32[]{:S(2)}) collective-permute-start(f32[2,4,128,128]{3,2,1,0:T(8,128)} %own_ref.1), channel_id=1, source_target_pairs={{0,192},{64,0},{128,64},{192,128},{1,193},{65,1},{129,65},{193,129... | collective-permute-start | bytes 1572872 | tf_op jit(solution)/shard_map/ppermute | solution.py:124
  6.3 26.5 %collective-permute-start = (f32[2,4,128,128]{3,2,1,0:T(8,128)}, f32[2,4,128,128]{3,2,1,0:T(8,128)S(1)}, u32[]{:S(2)}, u32[]{:S(2)}) collective-permute-start(f32[2,4,128,128]{3,2,1,0:T(8,128)} %own_ref.1), channel_id=1, source_target_pairs={{0,64},{64,128},{128,192},{192,0},{1,65},{65,129},{129,193},{193,1... | collective-permute-start | bytes 1572872 | tf_op jit(solution)/shard_map/ppermute | solution.py:124
  32.8 8.7 %collective-permute-start.2 = (f32[1,4,128,128]{3,2,1,0:T(8,128)S(1)}, f32[1,4,128,128]{3,2,1,0:T(8,128)S(1)}, u32[]{:S(2)}, u32[]{:S(2)}) collective-permute-start(f32[1,4,128,128]{3,2,1,0:T(8,128)S(1)} %slice.6), channel_id=1, source_target_pairs={{0,64},{64,128},{128,192},{192,0},{1,65},{65,129},{129,193},{193,1... | collective-permute-start | bytes 786440 | tf_op jit(solution)/shard_map/ppermute | solution.py:124
  32.9 13.9 %copy-start.11 = (s32[32]{0:T(128)S(1)}, s32[32]{0:T(128)}, u32[]{:S(2)}) copy-start(s32[32]{0:T(128)} %constant.89.clone) | copy-start | bytes 388
  32.9 15.1 %copy-start.10 = (f32[128]{0:T(128)S(1)}, f32[128]{0:T(128)}, u32[]{:S(2)}) copy-start(f32[128]{0:T(128)} %constant.90.clone) | copy-start | bytes 1540
  33.0 15.2 %copy-start.8 = (s32[8]{0:T(128)S(1)}, s32[8]{0:T(128)}, u32[]{:S(2)}) copy-start(s32[8]{0:T(128)} %param.14) | copy-start | bytes 100
  33.0 15.2 %copy-start.9 = (s32[8]{0:T(128)S(1)}, s32[8]{0:T(128)}, u32[]{:S(2)}) copy-start(s32[8]{0:T(128)} %param.15) | copy-start | bytes 100
  33.0 15.2 %copy-start.7 = (f32[128]{0:T(128)S(1)}, f32[128]{0:T(128)}, u32[]{:S(2)}) copy-start(f32[128]{0:T(128)} %constant.100) | copy-start | bytes 1540
  33.0 18.1 %copy-start = (f32[2,4,128,128]{3,2,1,0:T(8,128)S(1)}, f32[2,4,128,128]{3,2,1,0:T(8,128)}, u32[]{:S(2)}) copy-start(f32[2,4,128,128]{3,2,1,0:T(8,128)} %own_ref.1) | copy-start | bytes 1572868
  33.0 18.1 %copy-start.5 = (bf16[256,256]{1,0:T(8,128)(2,1)S(1)}, bf16[256,256]{1,0:T(8,128)(2,1)}, u32[]{:S(2)}) copy-start(bf16[256,256]{1,0:T(8,128)(2,1)} %constant.94.clone.wy_ref) | copy-start | bytes 393220
  33.0 18.1 %copy-start.6 = (bf16[256,256]{1,0:T(8,128)(2,1)S(1)}, bf16[256,256]{1,0:T(8,128)(2,1)}, u32[]{:S(2)}) copy-start(bf16[256,256]{1,0:T(8,128)(2,1)} %constant.93.clone.wz_ref) | copy-start | bytes 393220
  33.0 13.6 %collective-permute-start.3 = (f32[1,4,128,128]{3,2,1,0:T(8,128)S(1)}, f32[1,4,128,128]{3,2,1,0:T(8,128)S(1)}, u32[]{:S(2)}, u32[]{:S(2)}) collective-permute-start(f32[1,4,128,128]{3,2,1,0:T(8,128)S(1)} %slice.7), channel_id=1, source_target_pairs={{0,192},{64,0},{128,64},{192,128},{1,193},{65,1},{129,65},{193,129... | collective-permute-start | bytes 786440 | tf_op jit(solution)/shard_map/ppermute | solution.py:124
  46.7 4.4 %collective-permute-start.4 = (f32[8,4,128,128]{3,2,1,0:T(8,128)S(1)}, f32[8,4,128,128]{3,2,1,0:T(8,128)}, u32[]{:S(2)}, u32[]{:S(2)}) collective-permute-start(f32[8,4,128,128]{3,2,1,0:T(8,128)S(1)} %constant_dynamic-update-slice_fusion.mine_ref), channel_id=1, source_target_pairs={{0,32},{32,0},{1,33},{33,1},{2,34},{34,2},{3,35},{35,3},{4,36},{36... | collective-permute-start | bytes 6291464 | tf_op jit(solution)/shard_map/ppermute | solution.py:124
  55.8 59.5 %copy-start.1 = (bf16[256,256]{1,0:T(8,128)(2,1)S(1)}, bf16[256,256]{1,0:T(8,128)(2,1)}, u32[]{:S(2)}) copy-start(bf16[256,256]{1,0:T(8,128)(2,1)} %constant.96.clone.wxi_ref) | copy-start | bytes 393220
  55.9 59.5 %copy-start.2 = (bf16[256,256]{1,0:T(8,128)(2,1)S(1)}, bf16[256,256]{1,0:T(8,128)(2,1)}, u32[]{:S(2)}) copy-start(bf16[256,256]{1,0:T(8,128)(2,1)} %constant.95.clone.wx_ref) | copy-start | bytes 393220
  118.6 54.0 %copy-start.3 = (bf16[256,256]{1,0:T(8,128)(2,1)S(1)}, bf16[256,256]{1,0:T(8,128)(2,1)}, u32[]{:S(2)}) copy-start(bf16[256,256]{1,0:T(8,128)(2,1)} %constant.98.clone.wy_ref) | copy-start | bytes 393220
  118.6 54.0 %copy-start.4 = (bf16[256,256]{1,0:T(8,128)(2,1)S(1)}, bf16[256,256]{1,0:T(8,128)(2,1)}, u32[]{:S(2)}) copy-start(bf16[256,256]{1,0:T(8,128)(2,1)} %constant.97.clone.wz_ref) | copy-start | bytes 393220

commit v5 on v4

--- a/solution.py
+++ b/solution.py
@@ -126,10 +126,13 @@
 
 def every_orbital(own):
     held = own.shape[0] // 2
-    below, above = lax.optimization_barrier((rotated(own, "zh", 1), rotated(own, "zh", -1)))
-    far_below = rotated(below[:held], "zh", 1)
-    far_above = rotated(above[held:], "zh", -1)
-    mine = jnp.concatenate([own, above, far_below, far_above, below])
+    first, last = own[:held], own[held:]
+    below_first, above_last = rotated(first, "zh", 1), rotated(last, "zh", -1)
+    below_last, above_first = rotated(last, "zh", 1), rotated(first, "zh", -1)
+    far_first, far_last = rotated(below_first, "zh", 1), rotated(above_last, "zh", -1)
+    mine = jnp.concatenate(
+        [own, above_first, above_last, far_first, far_last, below_first, below_last]
+    )
     return mine, rotated(mine, "core", 1)
 
 

time: 177 us -> 175 us (0.989)
  waiting for transfers between devices: 37.4 us -> 25.1 us
  blocking collectives: 114 us -> 121 us
  starting transfers between devices: 10.7 us -> 13.1 us
    ppermute x5 -> x7, waiting for transfers between devices: 37.4 us -> 25.1 us  [rotated(): lax.ppermute(array, axis, [(i, (i + step) % size) for i in range(size)])]
    all_to_all x2, blocking collectives: 114 us -> 121 us  [exchange(): lax.all_to_all(array, GRID, split_axis=0, concat_axis=0, tiled=True, axis...]
    ppermute x5 -> x7, starting transfers between devices: 10.7 us -> 13.1 us  [rotated(): lax.ppermute(array, axis, [(i, (i + step) % size) for i in range(size)])]
  transfers between devices with their start and end apart: 5 -> 7, of which waited for: 5 -> 5; matrix products, arithmetic and copies ran while one was open for 1% -> 1% of each run, Pallas kernels for 0% -> 0%
where the time goes in v5:
time: 175 us
  blocking collectives  121 us (69%)
  waiting for transfers between devices  25.1 us (14%)
  starting transfers between devices  13.1 us (7%)
  Pallas kernels  11.8 us (7%)
  local copies, waits for them, and re-layouts  2.91 us (2%)
    all_to_all x2, blocking collectives, exchange(): lax.all_to_all(array, GRID, split_axis=0, concat_axis=0, tiled=True, axis...  121 us
    ppermute x7, waiting for transfers between devices, rotated(): lax.ppermute(array, axis, [(i, (i + step) % size) for i in range(size)])  25.1 us
    ppermute x7, starting transfers between devices, rotated(): lax.ppermute(array, axis, [(i, (i + step) % size) for i in range(size)])  13.1 us
    pallas_call x3, Pallas kernels, call(): pl.pallas_call(body, in_specs=[smem] * len(scalars) + [vmem] * len(operan...  11.8 us
  transfers between devices with their start and end apart: 7, of which 5 were waited for; matrix products, arithmetic and copies ran while one was open for 1% of the time, Pallas kernels for 0%

profile of v5, /device:TPU:8, one launch (start us, length us, event | category | flops | bytes accessed | tf_op | source)
XLA Modules:
  0.0 174.7 jit_solution(17265728287342532227)
XLA Ops:
  0.0 1.1 fusion.5
  1.1 3.3 %collective-permute-start.2 = (f32[1,4,128,128]{3,2,1,0:T(8,128)S(1)}, f32[1,4,128,128]{3,2,1,0:T(8,128)S(1)}, u32[]{:S(2)}, u32[]{:S(2)}) collective-permute-start(f32[1,4,128,128]{3,2,1,0:T(8,128)S(1)} %get-tuple-element.14), channel_id=1, source_target_pairs={{0,64},{64,128},{128,192},{192,0},{1,65},{65,129},{129,193},{193,1... | collective-permute-start | bytes 786440 | tf_op jit(solution)/shard_map/ppermute | solution.py:124
  4.4 0.0 copy-start.7
  4.4 0.0 copy-start
  4.5 0.0 copy-start.5
  4.5 0.0 copy-start.6
  4.5 3.2 %collective-permute-start.1 = (f32[1,4,128,128]{3,2,1,0:T(8,128)S(1)}, f32[1,4,128,128]{3,2,1,0:T(8,128)S(1)}, u32[]{:S(2)}, u32[]{:S(2)}) collective-permute-start(f32[1,4,128,128]{3,2,1,0:T(8,128)S(1)} %get-tuple-element.13), channel_id=1, source_target_pairs={{0,192},{64,0},{128,64},{192,128},{1,193},{65,1},{129,65},{193,129... | collective-permute-start | bytes 786440 | tf_op jit(solution)/shard_map/ppermute | solution.py:124
  7.6 2.9 %collective-permute-start = (f32[1,4,128,128]{3,2,1,0:T(8,128)S(1)}, f32[1,4,128,128]{3,2,1,0:T(8,128)S(1)}, u32[]{:S(2)}, u32[]{:S(2)}) collective-permute-start(f32[1,4,128,128]{3,2,1,0:T(8,128)S(1)} %get-tuple-element.14), channel_id=1, source_target_pairs={{0,192},{64,0},{128,64},{192,128},{1,193},{65,1},{129,65},{193,129... | collective-permute-start | bytes 786440 | tf_op jit(solution)/shard_map/ppermute | solution.py:124
  10.5 0.1 collective-permute-start.5
  10.6 6.0 %collective-permute-done.2 = f32[1,4,128,128]{3,2,1,0:T(8,128)S(1)} collective-permute-done((f32[1,4,128,128]{3,2,1,0:T(8,128)S(1)}, f32[1,4,128,128]{3,2,1,0:T(8,128)S(1)}, u32[]{:S(2)}, u32[]{:S(2)}) %collective-permute-start.2) | collective-permute-done | bytes 262176 | tf_op jit(solution)/shard_map/ppermute | solution.py:124
  16.6 0.7 collective-permute-start.3
  17.3 1.1 constant_dynamic-update-slice_fusion.6
  18.4 8.5 %collective-permute-done.1 = f32[1,4,128,128]{3,2,1,0:T(8,128)S(1)} collective-permute-done((f32[1,4,128,128]{3,2,1,0:T(8,128)S(1)}, f32[1,4,128,128]{3,2,1,0:T(8,128)S(1)}, u32[]{:S(2)}, u32[]{:S(2)}) %collective-permute-start.1) | collective-permute-done | bytes 262176 | tf_op jit(solution)/shard_map/ppermute | solution.py:124
  26.9 2.8 %collective-permute-start.4 = (f32[1,4,128,128]{3,2,1,0:T(8,128)S(1)}, f32[1,4,128,128]{3,2,1,0:T(8,128)S(1)}, u32[]{:S(2)}, u32[]{:S(2)}) collective-permute-start(f32[1,4,128,128]{3,2,1,0:T(8,128)S(1)} %collective-permute-done.1), channel_id=1, source_target_pairs={{0,192},{64,0},{128,64},{192,128},{1,193},{65,1},{129,65},{193,129... | collective-permute-start | bytes 786440 | tf_op jit(solution)/shard_map/ppermute | solution.py:124
  29.7 2.8 %collective-permute-done = f32[1,4,128,128]{3,2,1,0:T(8,128)S(1)} collective-permute-done((f32[1,4,128,128]{3,2,1,0:T(8,128)S(1)}, f32[1,4,128,128]{3,2,1,0:T(8,128)S(1)}, u32[]{:S(2)}, u32[]{:S(2)}) %collective-permute-start) | collective-permute-done | bytes 262176 | tf_op jit(solution)/shard_map/ppermute | solution.py:124
  32.5 0.0 collective-permute-done.3
  32.6 5.1 %collective-permute-done.4 = f32[1,4,128,128]{3,2,1,0:T(8,128)S(1)} collective-permute-done((f32[1,4,128,128]{3,2,1,0:T(8,128)S(1)}, f32[1,4,128,128]{3,2,1,0:T(8,128)S(1)}, u32[]{:S(2)}, u32[]{:S(2)}) %collective-permute-start.4) | collective-permute-done | bytes 262176 | tf_op jit(solution)/shard_map/ppermute | solution.py:124
  37.8 0.1 collective-permute-start.6
  37.9 0.6 dynamic_slice.6
  39.1 0.1 dynamic-slice_multiply_fusion
  39.2 0.1 broadcast_add_fusion
  39.3 0.1 compare_select_fusion.kernel_ref
  39.5 2.7 %collective-permute-done.6.other_ref = f32[8,4,128,128]{3,2,1,0:T(8,128)} collective-permute-done((f32[8,4,128,128]{3,2,1,0:T(8,128)S(1)}, f32[8,4,128,128]{3,2,1,0:T(8,128)}, u32[]{:S(2)}, u32[]{:S(2)}) %collective-permute-start.6) | collective-permute-done | bytes 2097184 | tf_op jit(solution)/shard_map/ppermute | solution.py:124
  42.2 4.7 %shard_map.127 = (f32[128,64,128]{2,1,0:T(8,128)S(1)}, f32[8,4,128,128]{3,2,1,0:T(8,128)S(1)}) custom-call(s32[8]{0:T(128)S(1)} %get-tuple-element.16.place_ref, s32[8]{0:T(128)S(1)} %get-tuple-element.15.core_ref, f32[2,4,128,128]{3,2,1,0:T(8,128)S(1)} %copy-done, f32[8,4,128,128]{3,2,1,0:T(8,128)S(1)} %constant_dynamic-update-slice_fusion.mine_ref, ...), custom_call_target="tpu_custom_call" | custom-call | flops 2147483648 | bytes 8388608 | tf_op jit(solution)/shard_map/pallas_call | solution.py:168
  46.9 0.0 copy-start.1
  46.9 0.0 copy-start.2
  46.9 66.7 %all_to_all.10 = f32[128,64,128]{2,1,0:T(8,128)S(1)} all-to-all(f32[128,64,128]{2,1,0:T(8,128)S(1)} %get-tuple-element.11), channel_id=1, replica_groups={{0,16,4,20,8,24,12,28,1,17,5,21,9,25,13,29,2,18,6,22,10,26,14,30,3,19,7..., dimensions={0} | all-to-all | bytes 8388608 | tf_op jit(solution)/shard_map/all_to_all | solution.py:178
  113.6 3.2 %shard_map.128 = f32[32,4,64,128]{3,2,1,0:T(8,128)S(1)} custom-call(f32[4,128,128]{2,1,0:T(8,128)S(1)} %compare_select_fusion.kernel_ref, bf16[256,256]{1,0:T(8,128)(2,1)S(1)} %copy-done.2, bf16[256,256]{1,0:T(8,128)(2,1)S(1)} %copy-done.1, f32[32,4,64,128]{3,2,1,0:T(8,128)S(1)} %bitcast.3), custom_call_target="tpu_custom_call" | custom-call | flops 2147483648 | bytes 8388608 | tf_op jit(solution)/shard_map/pallas_call | solution.py:168
  116.8 0.0 copy-start.3
  116.8 0.0 copy-start.4
  116.8 54.0 %all_to_all.11.in_ref = f32[128,64,128]{2,1,0:T(8,128)S(1)} all-to-all(f32[128,64,128]{2,1,0:T(8,128)S(1)} %bitcast.4), channel_id=1, replica_groups={{0,16,4,20,8,24,12,28,1,17,5,21,9,25,13,29,2,18,6,22,10,26,14,30,3,19,7..., dimensions={0} | all-to-all | bytes 8388608 | tf_op jit(solution)/shard_map/all_to_all | solution.py:178
  170.9 3.9 %shard_map.129 = f32[2,4,128,128]{3,2,1,0:T(8,128)} custom-call(f32[128,64,128]{2,1,0:T(8,128)S(1)} %all_to_all.11.in_ref, f32[8,4,128,128]{3,2,1,0:T(8,128)S(1)} %get-tuple-element.12.chosen_ref, bf16[256,256]{1,0:T(8,128)(2,1)S(1)} %copy-done.4, bf16[256,256]{1,0:T(8,128)(2,1)S(1)} %copy-done.3), custom_call_target="tpu_custom_call" | custom-call | flops 2147483648 | bytes 8388608 | tf_op jit(solution)/shard_map/pallas_call | solution.py:168
  (24 shorter events, 0.2 us)
Async XLA Ops:
  1.1 15.5 %collective-permute-start.2 = (f32[1,4,128,128]{3,2,1,0:T(8,128)S(1)}, f32[1,4,128,128]{3,2,1,0:T(8,128)S(1)}, u32[]{:S(2)}, u32[]{:S(2)}) collective-permute-start(f32[1,4,128,128]{3,2,1,0:T(8,128)S(1)} %get-tuple-element.14), channel_id=1, source_target_pairs={{0,64},{64,128},{128,192},{192,0},{1,65},{65,129},{129,193},{193,1... | collective-permute-start | bytes 786440 | tf_op jit(solution)/shard_map/ppermute | solution.py:124
  4.4 33.5 %copy-start.11 = (s32[32]{0:T(128)S(1)}, s32[32]{0:T(128)}, u32[]{:S(2)}) copy-start(s32[32]{0:T(128)} %constant.89.clone) | copy-start | bytes 388
  4.4 34.7 %copy-start.10 = (f32[128]{0:T(128)S(1)}, f32[128]{0:T(128)}, u32[]{:S(2)}) copy-start(f32[128]{0:T(128)} %constant.90.clone) | copy-start | bytes 1540
  4.4 34.8 %copy-start.8 = (s32[8]{0:T(128)S(1)}, s32[8]{0:T(128)}, u32[]{:S(2)}) copy-start(s32[8]{0:T(128)} %param.14) | copy-start | bytes 100
  4.4 34.8 %copy-start.9 = (s32[8]{0:T(128)S(1)}, s32[8]{0:T(128)}, u32[]{:S(2)}) copy-start(s32[8]{0:T(128)} %param.15) | copy-start | bytes 100
  4.4 34.8 %copy-start.7 = (f32[128]{0:T(128)S(1)}, f32[128]{0:T(128)}, u32[]{:S(2)}) copy-start(f32[128]{0:T(128)} %constant.100) | copy-start | bytes 1540
  4.4 37.7 %copy-start = (f32[2,4,128,128]{3,2,1,0:T(8,128)S(1)}, f32[2,4,128,128]{3,2,1,0:T(8,128)}, u32[]{:S(2)}) copy-start(f32[2,4,128,128]{3,2,1,0:T(8,128)} %own_ref.1) | copy-start | bytes 1572868
  4.5 37.7 %copy-start.5 = (bf16[256,256]{1,0:T(8,128)(2,1)S(1)}, bf16[256,256]{1,0:T(8,128)(2,1)}, u32[]{:S(2)}) copy-start(bf16[256,256]{1,0:T(8,128)(2,1)} %constant.94.clone.wy_ref) | copy-start | bytes 393220
  4.5 37.7 %copy-start.6 = (bf16[256,256]{1,0:T(8,128)(2,1)S(1)}, bf16[256,256]{1,0:T(8,128)(2,1)}, u32[]{:S(2)}) copy-start(bf16[256,256]{1,0:T(8,128)(2,1)} %constant.93.clone.wz_ref) | copy-start | bytes 393220
  4.5 22.4 %collective-permute-start.1 = (f32[1,4,128,128]{3,2,1,0:T(8,128)S(1)}, f32[1,4,128,128]{3,2,1,0:T(8,128)S(1)}, u32[]{:S(2)}, u32[]{:S(2)}) collective-permute-start(f32[1,4,128,128]{3,2,1,0:T(8,128)S(1)} %get-tuple-element.13), channel_id=1, source_target_pairs={{0,192},{64,0},{128,64},{192,128},{1,193},{65,1},{129,65},{193,129... | collective-permute-start | bytes 786440 | tf_op jit(solution)/shard_map/ppermute | solution.py:124
  7.6 24.8 %collective-permute-start = (f32[1,4,128,128]{3,2,1,0:T(8,128)S(1)}, f32[1,4,128,128]{3,2,1,0:T(8,128)S(1)}, u32[]{:S(2)}, u32[]{:S(2)}) collective-permute-start(f32[1,4,128,128]{3,2,1,0:T(8,128)S(1)} %get-tuple-element.14), channel_id=1, source_target_pairs={{0,192},{64,0},{128,64},{192,128},{1,193},{65,1},{129,65},{193,129... | collective-permute-start | bytes 786440 | tf_op jit(solution)/shard_map/ppermute | solution.py:124
  10.5 27.2 %collective-permute-start.5 = (f32[1,4,128,128]{3,2,1,0:T(8,128)S(1)}, f32[1,4,128,128]{3,2,1,0:T(8,128)S(1)}, u32[]{:S(2)}, u32[]{:S(2)}) collective-permute-start(f32[1,4,128,128]{3,2,1,0:T(8,128)S(1)} %get-tuple-element.13), channel_id=1, source_target_pairs={{0,64},{64,128},{128,192},{192,0},{1,65},{65,129},{129,193},{193,1... | collective-permute-start | bytes 786440 | tf_op jit(solution)/shard_map/ppermute | solution.py:124
  16.6 16.0 %collective-permute-start.3 = (f32[1,4,128,128]{3,2,1,0:T(8,128)S(1)}, f32[1,4,128,128]{3,2,1,0:T(8,128)S(1)}, u32[]{:S(2)}, u32[]{:S(2)}) collective-permute-start(f32[1,4,128,128]{3,2,1,0:T(8,128)S(1)} %collective-permute-done.2), channel_id=1, source_target_pairs={{0,64},{64,128},{128,192},{192,0},{1,65},{65,129},{129,193},{193,1... | collective-permute-start | bytes 786440 | tf_op jit(solution)/shard_map/ppermute | solution.py:124
  26.9 10.8 %collective-permute-start.4 = (f32[1,4,128,128]{3,2,1,0:T(8,128)S(1)}, f32[1,4,128,128]{3,2,1,0:T(8,128)S(1)}, u32[]{:S(2)}, u32[]{:S(2)}) collective-permute-start(f32[1,4,128,128]{3,2,1,0:T(8,128)S(1)} %collective-permute-done.1), channel_id=1, source_target_pairs={{0,192},{64,0},{128,64},{192,128},{1,193},{65,1},{129,65},{193,129... | collective-permute-start | bytes 786440 | tf_op jit(solution)/shard_map/ppermute | solution.py:124
  37.8 4.4 %collective-permute-start.6 = (f32[8,4,128,128]{3,2,1,0:T(8,128)S(1)}, f32[8,4,128,128]{3,2,1,0:T(8,128)}, u32[]{:S(2)}, u32[]{:S(2)}) collective-permute-start(f32[8,4,128,128]{3,2,1,0:T(8,128)S(1)} %constant_dynamic-update-slice_fusion.mine_ref), channel_id=1, source_target_pairs={{0,32},{32,0},{1,33},{33,1},{2,34},{34,2},{3,35},{35,3},{4,36},{36... | collective-permute-start | bytes 6291464 | tf_op jit(solution)/shard_map/ppermute | solution.py:124
  46.9 66.7 %copy-start.1 = (bf16[256,256]{1,0:T(8,128)(2,1)S(1)}, bf16[256,256]{1,0:T(8,128)(2,1)}, u32[]{:S(2)}) copy-start(bf16[256,256]{1,0:T(8,128)(2,1)} %constant.96.clone.wxi_ref) | copy-start | bytes 393220
  46.9 66.7 %copy-start.2 = (bf16[256,256]{1,0:T(8,128)(2,1)S(1)}, bf16[256,256]{1,0:T(8,128)(2,1)}, u32[]{:S(2)}) copy-start(bf16[256,256]{1,0:T(8,128)(2,1)} %constant.95.clone.wx_ref) | copy-start | bytes 393220
  116.8 54.0 %copy-start.3 = (bf16[256,256]{1,0:T(8,128)(2,1)S(1)}, bf16[256,256]{1,0:T(8,128)(2,1)}, u32[]{:S(2)}) copy-start(bf16[256,256]{1,0:T(8,128)(2,1)} %constant.98.clone.wy_ref) | copy-start | bytes 393220
  116.8 54.0 %copy-start.4 = (bf16[256,256]{1,0:T(8,128)(2,1)S(1)}, bf16[256,256]{1,0:T(8,128)(2,1)}, u32[]{:S(2)}) copy-start(bf16[256,256]{1,0:T(8,128)(2,1)} %constant.97.clone.wz_ref) | copy-start | bytes 393220

commit v6 on v5

--- a/solution.py
+++ b/solution.py
@@ -130,10 +130,9 @@
     below_first, above_last = rotated(first, "zh", 1), rotated(last, "zh", -1)
     below_last, above_first = rotated(last, "zh", 1), rotated(first, "zh", -1)
     far_first, far_last = rotated(below_first, "zh", 1), rotated(above_last, "zh", -1)
-    mine = jnp.concatenate(
-        [own, above_first, above_last, far_first, far_last, below_first, below_last]
-    )
-    return mine, rotated(mine, "core", 1)
+    blocks = [below_first, below_last, above_first, above_last]
+    blocks.append(jnp.concatenate([far_first, far_last, own]))
+    return jnp.concatenate(blocks), jnp.concatenate([rotated(block, "core", 1) for block in blocks])
 
 
 def shards(orbitals, band_owner, block_index):
@@ -149,7 +148,8 @@
     order = np.arange(grid).reshape(-1, 4, 4).transpose(2, 1, 0).reshape(grid)
     tx = tx.reshape(nx, grid, planes)[:, order].transpose(0, 2, 1).reshape(nx, nx)
     groups, cores = lax.axis_size("zh"), lax.axis_size("core")
-    place = (band_owner // cores - lax.axis_index("zh")) % groups * held + block_index
+    offset = (band_owner // cores - lax.axis_index("zh")) % groups
+    place = jnp.where(offset == 0, groups - 1, jnp.where(offset == groups - 1, 0, offset)) * held + block_index
     core_off = (band_owner + lax.axis_index("core")) % cores
 
     spot = jnp.asarray(np.argsort(order).astype(np.int32))[lax.axis_index(GRID)]

time: 175 us -> 174 us (level)
  blocking collectives: 121 us -> 112 us
  starting transfers between devices: 13.1 us -> 16.1 us
  waiting for transfers between devices: 25.1 us -> 28 us
  other arithmetic: 0.31 us -> 3.02 us
    all_to_all x2, blocking collectives: 121 us -> 112 us  [exchange(): lax.all_to_all(array, GRID, split_axis=0, concat_axis=0, tiled=True, axis...]
    ppermute x7 -> x11, starting transfers between devices: 13.1 us -> 16.1 us  [rotated(): lax.ppermute(array, axis, [(i, (i + step) % size) for i in range(size)])]
    ppermute x7 -> x11, waiting for transfers between devices: 25.1 us -> 28 us  [rotated(): lax.ppermute(array, axis, [(i, (i + step) % size) for i in range(size)])]
  transfers between devices with their start and end apart: 7 -> 11, of which waited for: 5 -> 5; matrix products, arithmetic and copies ran while one was open for 1% -> 3% of each run, Pallas kernels for 0% -> 0%
where the time goes in v6:
time: 174 us
  blocking collectives  112 us (64%)
  waiting for transfers between devices  28 us (16%)
  starting transfers between devices  16.1 us (9%)
  Pallas kernels  11.1 us (6%)
  other arithmetic  3.02 us (2%)
  local copies, waits for them, and re-layouts  2.71 us (2%)
    all_to_all x2, blocking collectives, exchange(): lax.all_to_all(array, GRID, split_axis=0, concat_axis=0, tiled=True, axis...  112 us
    ppermute x11, waiting for transfers between devices, rotated(): lax.ppermute(array, axis, [(i, (i + step) % size) for i in range(size)])  28 us
    ppermute x11, starting transfers between devices, rotated(): lax.ppermute(array, axis, [(i, (i + step) % size) for i in range(size)])  16.1 us
    pallas_call x3, Pallas kernels, call(): pl.pallas_call(body, in_specs=[smem] * len(scalars) + [vmem] * len(operan...  11.1 us
  transfers between devices with their start and end apart: 11, of which 5 were waited for; matrix products, arithmetic and copies ran while one was open for 3% of the time, Pallas kernels for 0%

profile of v6, /device:TPU:8, one launch (start us, length us, event | category | flops | bytes accessed | tf_op | source)
XLA Modules:
  0.0 174.0 jit_solution(1980691827900393181)
XLA Ops:
  0.0 1.1 fusion.5
  1.1 6.4 %collective-permute-start.6 = (f32[1,4,128,128]{3,2,1,0:T(8,128)S(1)}, f32[1,4,128,128]{3,2,1,0:T(8,128)S(1)}, u32[]{:S(2)}, u32[]{:S(2)}) collective-permute-start(f32[1,4,128,128]{3,2,1,0:T(8,128)S(1)} %get-tuple-element.13), channel_id=1, source_target_pairs={{0,192},{64,0},{128,64},{192,128},{1,193},{65,1},{129,65},{193,129... | collective-permute-start | bytes 786440 | tf_op jit(solution)/shard_map/ppermute | solution.py:124
  7.5 4.1 %collective-permute-start.4 = (f32[1,4,128,128]{3,2,1,0:T(8,128)S(1)}, f32[1,4,128,128]{3,2,1,0:T(8,128)S(1)}, u32[]{:S(2)}, u32[]{:S(2)}) collective-permute-start(f32[1,4,128,128]{3,2,1,0:T(8,128)S(1)} %get-tuple-element.14), channel_id=1, source_target_pairs={{0,192},{64,0},{128,64},{192,128},{1,193},{65,1},{129,65},{193,129... | collective-permute-start | bytes 786440 | tf_op jit(solution)/shard_map/ppermute | solution.py:124
  11.6 1.2 dynamic_slice.6
  13.5 0.7 dynamic-slice_multiply_fusion
  14.3 0.7 broadcast_add_fusion
  15.0 0.8 compare_select_fusion.kernel_ref
  15.8 7.6 %collective-permute-done.6 = f32[1,4,128,128]{3,2,1,0:T(8,128)S(1)} collective-permute-done((f32[1,4,128,128]{3,2,1,0:T(8,128)S(1)}, f32[1,4,128,128]{3,2,1,0:T(8,128)S(1)}, u32[]{:S(2)}, u32[]{:S(2)}) %collective-permute-start.6) | collective-permute-done | bytes 262176 | tf_op jit(solution)/shard_map/ppermute | solution.py:124
  23.4 4.7 %collective-permute-start.9 = (f32[1,4,128,128]{3,2,1,0:T(8,128)S(1)}, f32[1,4,128,128]{3,2,1,0:T(8,128)S(1)}, u32[]{:S(2)}, u32[]{:S(2)}) collective-permute-start(f32[1,4,128,128]{3,2,1,0:T(8,128)S(1)} %collective-permute-done.6), channel_id=1, source_target_pairs={{0,192},{64,0},{128,64},{192,128},{1,193},{65,1},{129,65},{193,129... | collective-permute-start | bytes 786440 | tf_op jit(solution)/shard_map/ppermute | solution.py:124
  28.1 5.7 %collective-permute-done = f32[1,4,128,128]{3,2,1,0:T(8,128)S(1)} collective-permute-done((f32[1,4,128,128]{3,2,1,0:T(8,128)S(1)}, f32[1,4,128,128]{3,2,1,0:T(8,128)S(1)}, u32[]{:S(2)}, u32[]{:S(2)}) %collective-permute-start) | collective-permute-done | bytes 262176 | tf_op jit(solution)/shard_map/ppermute | solution.py:124
  33.8 0.7 and_select_fusion
  34.5 0.1 collective-permute-start.7
  34.6 0.0 collective-permute-done.2
  34.6 0.5 collective-permute-start.3
  35.1 0.2 collective-permute-start.1
  35.3 5.9 %collective-permute-done.9 = f32[1,4,128,128]{3,2,1,0:T(8,128)S(1)} collective-permute-done((f32[1,4,128,128]{3,2,1,0:T(8,128)S(1)}, f32[1,4,128,128]{3,2,1,0:T(8,128)S(1)}, u32[]{:S(2)}, u32[]{:S(2)}) %collective-permute-start.9) | collective-permute-done | bytes 262176 | tf_op jit(solution)/shard_map/ppermute | solution.py:124
  41.2 6.6 %collective-permute-done.8 = f32[1,4,128,128]{3,2,1,0:T(8,128)S(1)} collective-permute-done((f32[1,4,128,128]{3,2,1,0:T(8,128)S(1)}, f32[1,4,128,128]{3,2,1,0:T(8,128)S(1)}, u32[]{:S(2)}, u32[]{:S(2)}) %collective-permute-start.8) | collective-permute-done | bytes 262176 | tf_op jit(solution)/shard_map/ppermute | solution.py:124
  47.8 0.1 pad_maximum_fusion
  47.9 0.1 collective-permute-start.10
  48.1 0.0 copy-start.5
  48.2 0.0 copy-start.6
  48.3 2.3 %collective-permute-done.10 = f32[4,4,128,128]{3,2,1,0:T(8,128)S(1)} collective-permute-done((f32[4,4,128,128]{3,2,1,0:T(8,128)S(1)}, f32[4,4,128,128]{3,2,1,0:T(8,128)S(1)}, u32[]{:S(2)}, u32[]{:S(2)}) %collective-permute-start.10) | collective-permute-done | bytes 1048608 | tf_op jit(solution)/shard_map/ppermute | solution.py:124
  50.6 0.1 constant_dynamic-update-slice_fusion.other_ref
  50.7 3.9 %shard_map.127 = (f32[128,64,128]{2,1,0:T(8,128)S(1)}, f32[8,4,128,128]{3,2,1,0:T(8,128)S(1)}) custom-call(s32[8]{0:T(128)S(1)} %get-tuple-element.16.place_ref, s32[8]{0:T(128)S(1)} %get-tuple-element.15.core_ref, f32[2,4,128,128]{3,2,1,0:T(8,128)S(1)} %copy-done, f32[8,4,128,128]{3,2,1,0:T(8,128)S(1)} %constant_dynamic-update-slice_fusion.5.mine_ref, ...), custom_call_target="tpu_custom_call" | custom-call | flops 2147483648 | bytes 8388608 | tf_op jit(solution)/shard_map/pallas_call | solution.py:168
  54.6 0.0 copy-start.1
  54.7 0.0 copy-start.2
  54.7 58.1 %all_to_all.10 = f32[128,64,128]{2,1,0:T(8,128)S(1)} all-to-all(f32[128,64,128]{2,1,0:T(8,128)S(1)} %get-tuple-element.11), channel_id=1, replica_groups={{0,16,4,20,8,24,12,28,1,17,5,21,9,25,13,29,2,18,6,22,10,26,14,30,3,19,7..., dimensions={0} | all-to-all | bytes 8388608 | tf_op jit(solution)/shard_map/all_to_all | solution.py:178
  112.8 3.2 %shard_map.128 = f32[32,4,64,128]{3,2,1,0:T(8,128)S(1)} custom-call(f32[4,128,128]{2,1,0:T(8,128)S(1)} %compare_select_fusion.kernel_ref, bf16[256,256]{1,0:T(8,128)(2,1)S(1)} %copy-done.2, bf16[256,256]{1,0:T(8,128)(2,1)S(1)} %copy-done.1, f32[32,4,64,128]{3,2,1,0:T(8,128)S(1)} %bitcast.3), custom_call_target="tpu_custom_call" | custom-call | flops 2147483648 | bytes 8388608 | tf_op jit(solution)/shard_map/pallas_call | solution.py:168
  115.9 0.0 copy-start.3
  116.0 0.0 copy-start.4
  116.0 54.0 %all_to_all.11.in_ref = f32[128,64,128]{2,1,0:T(8,128)S(1)} all-to-all(f32[128,64,128]{2,1,0:T(8,128)S(1)} %bitcast.4), channel_id=1, replica_groups={{0,16,4,20,8,24,12,28,1,17,5,21,9,25,13,29,2,18,6,22,10,26,14,30,3,19,7..., dimensions={0} | all-to-all | bytes 8388608 | tf_op jit(solution)/shard_map/all_to_all | solution.py:178
  170.0 4.0 %shard_map.129 = f32[2,4,128,128]{3,2,1,0:T(8,128)} custom-call(f32[128,64,128]{2,1,0:T(8,128)S(1)} %all_to_all.11.in_ref, f32[8,4,128,128]{3,2,1,0:T(8,128)S(1)} %get-tuple-element.12.chosen_ref, bf16[256,256]{1,0:T(8,128)(2,1)S(1)} %copy-done.4, bf16[256,256]{1,0:T(8,128)(2,1)S(1)} %copy-done.3), custom_call_target="tpu_custom_call" | custom-call | flops 2147483648 | bytes 8388608 | tf_op jit(solution)/shard_map/pallas_call | solution.py:168
  (28 shorter events, 0.3 us)
Async XLA Ops:
  0.0 47.8 %copy-start = (f32[2,4,128,128]{3,2,1,0:T(8,128)S(1)}, f32[2,4,128,128]{3,2,1,0:T(8,128)}, u32[]{:S(2)}) copy-start(f32[2,4,128,128]{3,2,1,0:T(8,128)} %own_ref.1) | copy-start | bytes 1572868
  1.1 22.2 %collective-permute-start.6 = (f32[1,4,128,128]{3,2,1,0:T(8,128)S(1)}, f32[1,4,128,128]{3,2,1,0:T(8,128)S(1)}, u32[]{:S(2)}, u32[]{:S(2)}) collective-permute-start(f32[1,4,128,128]{3,2,1,0:T(8,128)S(1)} %get-tuple-element.13), channel_id=1, source_target_pairs={{0,192},{64,0},{128,64},{192,128},{1,193},{65,1},{129,65},{193,129... | collective-permute-start | bytes 786440 | tf_op jit(solution)/shard_map/ppermute | solution.py:124
  7.5 27.1 %collective-permute-start.2 = (f32[1,4,128,128]{3,2,1,0:T(8,128)S(1)}, f32[1,4,128,128]{3,2,1,0:T(8,128)S(1)}, u32[]{:S(2)}, u32[]{:S(2)}) collective-permute-start(f32[1,4,128,128]{3,2,1,0:T(8,128)S(1)} %get-tuple-element.13), channel_id=1, source_target_pairs={{0,64},{64,128},{128,192},{192,0},{1,65},{65,129},{129,193},{193,1... | collective-permute-start | bytes 786440 | tf_op jit(solution)/shard_map/ppermute | solution.py:124
  7.5 27.6 %collective-permute-start.4 = (f32[1,4,128,128]{3,2,1,0:T(8,128)S(1)}, f32[1,4,128,128]{3,2,1,0:T(8,128)S(1)}, u32[]{:S(2)}, u32[]{:S(2)}) collective-permute-start(f32[1,4,128,128]{3,2,1,0:T(8,128)S(1)} %get-tuple-element.14), channel_id=1, source_target_pairs={{0,192},{64,0},{128,64},{192,128},{1,193},{65,1},{129,65},{193,129... | collective-permute-start | bytes 786440 | tf_op jit(solution)/shard_map/ppermute | solution.py:124
  11.6 22.1 %collective-permute-start = (f32[1,4,128,128]{3,2,1,0:T(8,128)S(1)}, f32[1,4,128,128]{3,2,1,0:T(8,128)S(1)}, u32[]{:S(2)}, u32[]{:S(2)}) collective-permute-start(f32[1,4,128,128]{3,2,1,0:T(8,128)S(1)} %get-tuple-element.14), channel_id=1, source_target_pairs={{0,64},{64,128},{128,192},{192,0},{1,65},{65,129},{129,193},{193,1... | collective-permute-start | bytes 786440 | tf_op jit(solution)/shard_map/ppermute | solution.py:124
  23.4 17.8 %collective-permute-start.9 = (f32[1,4,128,128]{3,2,1,0:T(8,128)S(1)}, f32[1,4,128,128]{3,2,1,0:T(8,128)S(1)}, u32[]{:S(2)}, u32[]{:S(2)}) collective-permute-start(f32[1,4,128,128]{3,2,1,0:T(8,128)S(1)} %collective-permute-done.6), channel_id=1, source_target_pairs={{0,192},{64,0},{128,64},{192,128},{1,193},{65,1},{129,65},{193,129... | collective-permute-start | bytes 786440 | tf_op jit(solution)/shard_map/ppermute | solution.py:124
  33.8 14.0 %collective-permute-start.8 = (f32[1,4,128,128]{3,2,1,0:T(8,128)S(1)}, f32[1,4,128,128]{3,2,1,0:T(8,128)S(1)}, u32[]{:S(2)}, u32[]{:S(2)}) collective-permute-start(f32[1,4,128,128]{3,2,1,0:T(8,128)S(1)} %collective-permute-done), channel_id=1, source_target_pairs={{0,64},{64,128},{128,192},{192,0},{1,65},{65,129},{129,193},{193,1... | collective-permute-start | bytes 786440 | tf_op jit(solution)/shard_map/ppermute | solution.py:124
  34.5 13.7 %collective-permute-start.7 = (f32[1,4,128,128]{3,2,1,0:T(8,128)S(1)}, f32[1,4,128,128]{3,2,1,0:T(8,128)S(1)}, u32[]{:S(2)}, u32[]{:S(2)}) collective-permute-start(f32[1,4,128,128]{3,2,1,0:T(8,128)S(1)} %collective-permute-done.6), channel_id=1, source_target_pairs={{0,32},{32,0},{1,33},{33,1},{2,34},{34,2},{3,35},{35,3},{4,36},{36... | collective-permute-start | bytes 786440 | tf_op jit(solution)/shard_map/ppermute | solution.py:124
  34.6 13.5 %collective-permute-start.3 = (f32[1,4,128,128]{3,2,1,0:T(8,128)S(1)}, f32[1,4,128,128]{3,2,1,0:T(8,128)S(1)}, u32[]{:S(2)}, u32[]{:S(2)}) collective-permute-start(f32[1,4,128,128]{3,2,1,0:T(8,128)S(1)} %collective-permute-done.2), channel_id=1, source_target_pairs={{0,32},{32,0},{1,33},{33,1},{2,34},{34,2},{3,35},{35,3},{4,36},{36... | collective-permute-start | bytes 786440 | tf_op jit(solution)/shard_map/ppermute | solution.py:124
  35.1 12.9 %collective-permute-start.1 = (f32[1,4,128,128]{3,2,1,0:T(8,128)S(1)}, f32[1,4,128,128]{3,2,1,0:T(8,128)S(1)}, u32[]{:S(2)}, u32[]{:S(2)}) collective-permute-start(f32[1,4,128,128]{3,2,1,0:T(8,128)S(1)} %collective-permute-done), channel_id=1, source_target_pairs={{0,32},{32,0},{1,33},{33,1},{2,34},{34,2},{3,35},{35,3},{4,36},{36... | collective-permute-start | bytes 786440 | tf_op jit(solution)/shard_map/ppermute | solution.py:124
  41.2 7.0 %collective-permute-start.5 = (f32[1,4,128,128]{3,2,1,0:T(8,128)S(1)}, f32[1,4,128,128]{3,2,1,0:T(8,128)S(1)}, u32[]{:S(2)}, u32[]{:S(2)}) collective-permute-start(f32[1,4,128,128]{3,2,1,0:T(8,128)S(1)} %collective-permute-done.4), channel_id=1, source_target_pairs={{0,32},{32,0},{1,33},{33,1},{2,34},{34,2},{3,35},{35,3},{4,36},{36... | collective-permute-start | bytes 786440 | tf_op jit(solution)/shard_map/ppermute | solution.py:124
  47.9 2.7 %collective-permute-start.10 = (f32[4,4,128,128]{3,2,1,0:T(8,128)S(1)}, f32[4,4,128,128]{3,2,1,0:T(8,128)S(1)}, u32[]{:S(2)}, u32[]{:S(2)}) collective-permute-start(f32[4,4,128,128]{3,2,1,0:T(8,128)S(1)} %pad_maximum_fusion), channel_id=1, source_target_pairs={{0,32},{32,0},{1,33},{33,1},{2,34},{34,2},{3,35},{35,3},{4,36},{36... | collective-permute-start | bytes 3145736 | tf_op jit(solution)/shard_map/ppermute | solution.py:124
  48.1 2.5 %copy-start.5 = (bf16[256,256]{1,0:T(8,128)(2,1)S(1)}, bf16[256,256]{1,0:T(8,128)(2,1)}, u32[]{:S(2)}) copy-start(bf16[256,256]{1,0:T(8,128)(2,1)} %constant.97.clone.wy_ref) | copy-start | bytes 393220
  48.2 2.5 %copy-start.6 = (bf16[256,256]{1,0:T(8,128)(2,1)S(1)}, bf16[256,256]{1,0:T(8,128)(2,1)}, u32[]{:S(2)}) copy-start(bf16[256,256]{1,0:T(8,128)(2,1)} %constant.96.clone.wz_ref) | copy-start | bytes 393220
  54.6 58.1 %copy-start.1 = (bf16[256,256]{1,0:T(8,128)(2,1)S(1)}, bf16[256,256]{1,0:T(8,128)(2,1)}, u32[]{:S(2)}) copy-start(bf16[256,256]{1,0:T(8,128)(2,1)} %constant.99.clone.wxi_ref) | copy-start | bytes 393220
  54.7 58.1 %copy-start.2 = (bf16[256,256]{1,0:T(8,128)(2,1)S(1)}, bf16[256,256]{1,0:T(8,128)(2,1)}, u32[]{:S(2)}) copy-start(bf16[256,256]{1,0:T(8,128)(2,1)} %constant.98.clone.wx_ref) | copy-start | bytes 393220
  115.9 54.0 %copy-start.3 = (bf16[256,256]{1,0:T(8,128)(2,1)S(1)}, bf16[256,256]{1,0:T(8,128)(2,1)}, u32[]{:S(2)}) copy-start(bf16[256,256]{1,0:T(8,128)(2,1)} %constant.101.clone.wy_ref) | copy-start | bytes 393220
  116.0 54.0 %copy-start.4 = (bf16[256,256]{1,0:T(8,128)(2,1)S(1)}, bf16[256,256]{1,0:T(8,128)(2,1)}, u32[]{:S(2)}) copy-start(bf16[256,256]{1,0:T(8,128)(2,1)} %constant.100.clone.wz_ref) | copy-start | bytes 393220

commit v7 on v6

--- a/solution.py
+++ b/solution.py
@@ -21,8 +21,7 @@
     rows += [math.sqrt(2.0 / length) * np.cos(2 * math.pi * (k * x % length) / length) for k in range(1, half)]
     rows += [(1.0 - 2.0 * (x % 2)) / math.sqrt(length)]
     rows += [math.sqrt(2.0 / length) * np.sin(2 * math.pi * (k * x % length) / length) for k in range(1, half)]
-    freq = np.concatenate([np.arange(half + 1), np.arange(1, half)])
-    return np.stack(rows), freq.astype(np.float32)
+    return np.stack(rows)
 
 
 def halves(table):
@@ -80,10 +79,23 @@
     lax.fori_loop(0, out_ref.shape[1] // width, one, 0, unroll=UNROLL)
 
 
-def middle(kernel_ref, wx_ref, wxi_ref, in_ref, out_ref):
+def frequency(row, length):
+    return jnp.where(row > length // 2, row - length // 2, row).astype(jnp.float32)
+
+
+def middle(spot_ref, wx_ref, wxi_ref, in_ref, out_ref, kernel_ref):
     slabs, own_y, step, nz = in_ref.shape
-    held, planes = 2, kernel_ref.shape[1] // slabs
-    width = planes * held
+    _, nx, _ = kernel_ref.shape
+    held, planes = 2, nx // slabs
+    width = planes * held
+    scale = (2.0 * math.pi / CELL_EDGE) ** 2
+    freq_x = frequency(lax.broadcasted_iota(jnp.int32, (nx, nz), 0), nx)
+    freq_z = frequency(lax.broadcasted_iota(jnp.int32, (nx, nz), 1), nz)
+    for q in range(own_y):
+        freq_y = frequency(jnp.full((nx, nz), spot_ref[0] * own_y + q, jnp.int32), slabs * own_y)
+        squared = scale * (freq_x**2 + freq_y**2 + freq_z**2)
+        guarded = jnp.where(squared > 0, squared, 1.0)
+        kernel_ref[q] = jnp.where(squared > 0, 4.0 * math.pi / guarded, 0.0)
 
     def one(r, carry):
         at = pl.ds(pl.multiple_of(r * width, width), width)
@@ -142,9 +154,7 @@
     nx = planes * grid
     own_y = ny // grid
     width = planes * held
-    tx, fx = basis(nx)
-    ty, fy = basis(ny)
-    tz, fz = basis(nz)
+    tx, ty, tz = basis(nx), basis(ny), basis(nz)
     order = np.arange(grid).reshape(-1, 4, 4).transpose(2, 1, 0).reshape(grid)
     tx = tx.reshape(nx, grid, planes)[:, order].transpose(0, 2, 1).reshape(nx, nx)
     groups, cores = lax.axis_size("zh"), lax.axis_size("core")
@@ -152,24 +162,21 @@
     place = jnp.where(offset == 0, groups - 1, jnp.where(offset == groups - 1, 0, offset)) * held + block_index
     core_off = (band_owner + lax.axis_index("core")) % cores
 
-    spot = jnp.asarray(np.argsort(order).astype(np.int32))[lax.axis_index(GRID)]
-    fy_own = lax.dynamic_slice_in_dim(jnp.asarray(fy), spot * own_y, own_y)
-    scale = (2.0 * math.pi / CELL_EDGE) ** 2
-    squared = scale * (fx[None, :, None] ** 2 + fy_own[:, None, None] ** 2 + fz[None, None, :] ** 2)
-    guarded = jnp.where(squared > 0, squared, 1.0)
-    kernel = jnp.where(squared > 0, 4.0 * math.pi / guarded, 0.0)
+    here = lax.axis_index(GRID)
+    spot = here % 4 * (grid // 4) + here // 4 % 4 * (grid // 16) + here // 16
 
     mine, other = every_orbital(orbitals)
-    kernel, other = lax.optimization_barrier((kernel, other))
+    spot, other = lax.optimization_barrier((jnp.full((1,), spot, jnp.int32), other))
     cells = rounds * held * planes * ny * nz
     vmem, smem = pl.BlockSpec(memory_space=pltpu.VMEM), pl.BlockSpec(memory_space=pltpu.SMEM)
 
-    def call(body, shapes, scalars, operands):
+    def call(body, shapes, scalars, operands, scratch=()):
         return pl.pallas_call(
             body,
             in_specs=[smem] * len(scalars) + [vmem] * len(operands),
             out_specs=[vmem] * len(shapes),
             out_shape=[jax.ShapeDtypeStruct(shape, jnp.float32) for shape in shapes],
+            scratch_shapes=scratch,
             compiler_params=pltpu.CompilerParams(vmem_limit_bytes=16 * 2**20),
             cost_estimate=pl.CostEstimate(flops=16 * nz * cells, bytes_accessed=8 * cells, transcendentals=0),
         )(*scalars, *operands)
@@ -188,7 +195,13 @@
     )
     strips = (grid, own_y, rounds * width, nz)
     spec = exchange(half).reshape(strips)
-    (spec,) = call(middle, [strips], (), (kernel, left_table(tx), left_table(tx.T), spec))
+    (spec,) = call(
+        middle,
+        [strips],
+        (spot,),
+        (left_table(tx), left_table(tx.T), spec),
+        [pltpu.VMEM((own_y, nx, nz), jnp.float32)],
+    )
     half = exchange(spec.reshape(sent))
     (out,) = call(inward, [orbitals.shape], (), (half, chosen, right_table(tz), left_table(ty.T)))
     return out

time: 174 us -> 173 us (level)
  other arithmetic: 3.02 us -> 0.76 us
  waiting for transfers between devices: 28 us -> 30.1 us
    ppermute x11, waiting for transfers between devices: 28 us -> 30.1 us  [rotated(): lax.ppermute(array, axis, [(i, (i + step) % size) for i in range(size)])]
  transfers between devices with their start and end apart: 11 -> 11, of which waited for: 5 -> 6; matrix products, arithmetic and copies ran while one was open for 3% -> 1% of each run, Pallas kernels for 0% -> 0%
where the time goes in v7:
time: 173 us; the launch traced here: 172 us
  blocking collectives  113 us (65%)
  waiting for transfers between devices  30.1 us (17%)
  starting transfers between devices  15.4 us (9%)
  Pallas kernels  11.4 us (7%)
    all_to_all x2, blocking collectives, exchange(): lax.all_to_all(array, GRID, split_axis=0, concat_axis=0, tiled=True, axis...  113 us
    ppermute x11, waiting for transfers between devices, rotated(): lax.ppermute(array, axis, [(i, (i + step) % size) for i in range(size)])  30.1 us
    ppermute x11, starting transfers between devices, rotated(): lax.ppermute(array, axis, [(i, (i + step) % size) for i in range(size)])  15.4 us
    pallas_call x3, Pallas kernels, call(): pl.pallas_call(body, in_specs=[smem] * len(scalars) + [vmem] * len(operan...  11.4 us
  transfers between devices with their start and end apart: 11, of which 6 were waited for; matrix products, arithmetic and copies ran while one was open for 1% of the time, Pallas kernels for 0%

profile of v7, /device:TPU:8, one launch (start us, length us, event | category | flops | bytes accessed | tf_op | source)
XLA Modules:
  0.0 172.5 jit_solution(5966474024140732591)
XLA Ops:
  0.0 1.1 fusion.4
  1.1 6.4 %collective-permute-start.6 = (f32[1,4,128,128]{3,2,1,0:T(8,128)S(1)}, f32[1,4,128,128]{3,2,1,0:T(8,128)S(1)}, u32[]{:S(2)}, u32[]{:S(2)}) collective-permute-start(f32[1,4,128,128]{3,2,1,0:T(8,128)S(1)} %get-tuple-element.13), channel_id=1, source_target_pairs={{0,192},{64,0},{128,64},{192,128},{1,193},{65,1},{129,65},{193,129... | collective-permute-start | bytes 786440 | tf_op jit(solution)/shard_map/ppermute | solution.py:136
  7.5 0.0 collective-permute-start
  7.5 1.5 collective-permute-start.2
  9.1 2.6 %collective-permute-start.4 = (f32[1,4,128,128]{3,2,1,0:T(8,128)S(1)}, f32[1,4,128,128]{3,2,1,0:T(8,128)S(1)}, u32[]{:S(2)}, u32[]{:S(2)}) collective-permute-start(f32[1,4,128,128]{3,2,1,0:T(8,128)S(1)} %get-tuple-element.14), channel_id=1, source_target_pairs={{0,192},{64,0},{128,64},{192,128},{1,193},{65,1},{129,65},{193,129... | collective-permute-start | bytes 786440 | tf_op jit(solution)/shard_map/ppermute | solution.py:136
  11.7 11.7 %collective-permute-done.6 = f32[1,4,128,128]{3,2,1,0:T(8,128)S(1)} collective-permute-done((f32[1,4,128,128]{3,2,1,0:T(8,128)S(1)}, f32[1,4,128,128]{3,2,1,0:T(8,128)S(1)}, u32[]{:S(2)}, u32[]{:S(2)}) %collective-permute-start.6) | collective-permute-done | bytes 262176 | tf_op jit(solution)/shard_map/ppermute | solution.py:136
  23.4 4.7 %collective-permute-start.9 = (f32[1,4,128,128]{3,2,1,0:T(8,128)S(1)}, f32[1,4,128,128]{3,2,1,0:T(8,128)S(1)}, u32[]{:S(2)}, u32[]{:S(2)}) collective-permute-start(f32[1,4,128,128]{3,2,1,0:T(8,128)S(1)} %collective-permute-done.6), channel_id=1, source_target_pairs={{0,192},{64,0},{128,64},{192,128},{1,193},{65,1},{129,65},{193,129... | collective-permute-start | bytes 786440 | tf_op jit(solution)/shard_map/ppermute | solution.py:136
  28.1 0.0 collective-permute-done
  28.1 0.0 collective-permute-start.8
  28.1 0.7 and_select_fusion
  28.8 0.1 collective-permute-start.7
  28.9 1.4 collective-permute-done.2
  30.3 3.8 %collective-permute-done.4 = f32[1,4,128,128]{3,2,1,0:T(8,128)S(1)} collective-permute-done((f32[1,4,128,128]{3,2,1,0:T(8,128)S(1)}, f32[1,4,128,128]{3,2,1,0:T(8,128)S(1)}, u32[]{:S(2)}, u32[]{:S(2)}) %collective-permute-start.4) | collective-permute-done | bytes 262176 | tf_op jit(solution)/shard_map/ppermute | solution.py:136
  34.1 0.0 collective-permute-start.1
  34.1 7.1 %collective-permute-done.9 = f32[1,4,128,128]{3,2,1,0:T(8,128)S(1)} collective-permute-done((f32[1,4,128,128]{3,2,1,0:T(8,128)S(1)}, f32[1,4,128,128]{3,2,1,0:T(8,128)S(1)}, u32[]{:S(2)}, u32[]{:S(2)}) %collective-permute-start.9) | collective-permute-done | bytes 262176 | tf_op jit(solution)/shard_map/ppermute | solution.py:136
  41.2 0.0 collective-permute-start.5
  41.2 3.8 %collective-permute-done.8 = f32[1,4,128,128]{3,2,1,0:T(8,128)S(1)} collective-permute-done((f32[1,4,128,128]{3,2,1,0:T(8,128)S(1)}, f32[1,4,128,128]{3,2,1,0:T(8,128)S(1)}, u32[]{:S(2)}, u32[]{:S(2)}) %collective-permute-start.8) | collective-permute-done | bytes 262176 | tf_op jit(solution)/shard_map/ppermute | solution.py:136
  45.0 0.1 pad_maximum_fusion
  45.1 0.1 collective-permute-start.10
  45.4 0.0 copy-start.5
  45.4 0.0 copy-start.6
  45.5 2.3 %collective-permute-done.10 = f32[4,4,128,128]{3,2,1,0:T(8,128)S(1)} collective-permute-done((f32[4,4,128,128]{3,2,1,0:T(8,128)S(1)}, f32[4,4,128,128]{3,2,1,0:T(8,128)S(1)}, u32[]{:S(2)}, u32[]{:S(2)}) %collective-permute-start.10) | collective-permute-done | bytes 1048608 | tf_op jit(solution)/shard_map/ppermute | solution.py:136
  47.8 0.1 constant_dynamic-update-slice_fusion.other_ref
  47.9 3.9 %shard_map.91 = (f32[128,64,128]{2,1,0:T(8,128)S(1)}, f32[8,4,128,128]{3,2,1,0:T(8,128)S(1)}) custom-call(s32[8]{0:T(128)S(1)} %get-tuple-element.16.place_ref, s32[8]{0:T(128)S(1)} %get-tuple-element.15.core_ref, f32[2,4,128,128]{3,2,1,0:T(8,128)S(1)} %copy-done, f32[8,4,128,128]{3,2,1,0:T(8,128)S(1)} %constant_dynamic-update-slice_fusion.5.mine_ref, ...), custom_call_target="tpu_custom_call" | custom-call | flops 2147483648 | bytes 8388608 | tf_op jit(solution)/shard_map/pallas_call | solution.py:174
  51.9 0.0 copy-start.1
  51.9 0.0 copy-start.2
  51.9 59.1 %all_to_all.10 = f32[128,64,128]{2,1,0:T(8,128)S(1)} all-to-all(f32[128,64,128]{2,1,0:T(8,128)S(1)} %get-tuple-element.11), channel_id=1, replica_groups={{0,16,4,20,8,24,12,28,1,17,5,21,9,25,13,29,2,18,6,22,10,26,14,30,3,19,7..., dimensions={0} | all-to-all | bytes 8388608 | tf_op jit(solution)/shard_map/all_to_all | solution.py:185
  111.0 3.3 %shard_map.92 = f32[32,4,64,128]{3,2,1,0:T(8,128)S(1)} custom-call(s32[1]{0:T(128)} %bitcast.spot_ref, bf16[256,256]{1,0:T(8,128)(2,1)S(1)} %copy-done.2, bf16[256,256]{1,0:T(8,128)(2,1)S(1)} %copy-done.1, f32[32,4,64,128]{3,2,1,0:T(8,128)S(1)} %bitcast.3), custom_call_target="tpu_custom_call" | custom-call | flops 2147483648 | bytes 8388608 | tf_op jit(solution)/shard_map/pallas_call | solution.py:174
  114.3 0.0 copy-start.3
  114.3 0.0 copy-start.4
  114.3 54.0 %all_to_all.11.in_ref = f32[128,64,128]{2,1,0:T(8,128)S(1)} all-to-all(f32[128,64,128]{2,1,0:T(8,128)S(1)} %bitcast.4), channel_id=1, replica_groups={{0,16,4,20,8,24,12,28,1,17,5,21,9,25,13,29,2,18,6,22,10,26,14,30,3,19,7..., dimensions={0} | all-to-all | bytes 8388608 | tf_op jit(solution)/shard_map/all_to_all | solution.py:185
  168.3 4.1 %shard_map.93 = f32[2,4,128,128]{3,2,1,0:T(8,128)} custom-call(f32[128,64,128]{2,1,0:T(8,128)S(1)} %all_to_all.11.in_ref, f32[8,4,128,128]{3,2,1,0:T(8,128)S(1)} %get-tuple-element.12.chosen_ref, bf16[256,256]{1,0:T(8,128)(2,1)S(1)} %copy-done.4, bf16[256,256]{1,0:T(8,128)(2,1)S(1)} %copy-done.3), custom_call_target="tpu_custom_call" | custom-call | flops 2147483648 | bytes 8388608 | tf_op jit(solution)/shard_map/pallas_call | solution.py:174
  (24 shorter events, 0.3 us)
Async XLA Ops:
  0.0 45.0 %copy-start = (f32[2,4,128,128]{3,2,1,0:T(8,128)S(1)}, f32[2,4,128,128]{3,2,1,0:T(8,128)}, u32[]{:S(2)}) copy-start(f32[2,4,128,128]{3,2,1,0:T(8,128)} %own_ref.1) | copy-start | bytes 1572868
  1.1 22.2 %collective-permute-start.6 = (f32[1,4,128,128]{3,2,1,0:T(8,128)S(1)}, f32[1,4,128,128]{3,2,1,0:T(8,128)S(1)}, u32[]{:S(2)}, u32[]{:S(2)}) collective-permute-start(f32[1,4,128,128]{3,2,1,0:T(8,128)S(1)} %get-tuple-element.13), channel_id=1, source_target_pairs={{0,192},{64,0},{128,64},{192,128},{1,193},{65,1},{129,65},{193,129... | collective-permute-start | bytes 786440 | tf_op jit(solution)/shard_map/ppermute | solution.py:136
  7.5 20.6 %collective-permute-start = (f32[1,4,128,128]{3,2,1,0:T(8,128)S(1)}, f32[1,4,128,128]{3,2,1,0:T(8,128)S(1)}, u32[]{:S(2)}, u32[]{:S(2)}) collective-permute-start(f32[1,4,128,128]{3,2,1,0:T(8,128)S(1)} %get-tuple-element.14), channel_id=1, source_target_pairs={{0,64},{64,128},{128,192},{192,0},{1,65},{65,129},{129,193},{193,1... | collective-permute-start | bytes 786440 | tf_op jit(solution)/shard_map/ppermute | solution.py:136
  7.5 22.8 %collective-permute-start.2 = (f32[1,4,128,128]{3,2,1,0:T(8,128)S(1)}, f32[1,4,128,128]{3,2,1,0:T(8,128)S(1)}, u32[]{:S(2)}, u32[]{:S(2)}) collective-permute-start(f32[1,4,128,128]{3,2,1,0:T(8,128)S(1)} %get-tuple-element.13), channel_id=1, source_target_pairs={{0,64},{64,128},{128,192},{192,0},{1,65},{65,129},{129,193},{193,1... | collective-permute-start | bytes 786440 | tf_op jit(solution)/shard_map/ppermute | solution.py:136
  9.1 25.0 %collective-permute-start.4 = (f32[1,4,128,128]{3,2,1,0:T(8,128)S(1)}, f32[1,4,128,128]{3,2,1,0:T(8,128)S(1)}, u32[]{:S(2)}, u32[]{:S(2)}) collective-permute-start(f32[1,4,128,128]{3,2,1,0:T(8,128)S(1)} %get-tuple-element.14), channel_id=1, source_target_pairs={{0,192},{64,0},{128,64},{192,128},{1,193},{65,1},{129,65},{193,129... | collective-permute-start | bytes 786440 | tf_op jit(solution)/shard_map/ppermute | solution.py:136
  23.4 17.8 %collective-permute-start.9 = (f32[1,4,128,128]{3,2,1,0:T(8,128)S(1)}, f32[1,4,128,128]{3,2,1,0:T(8,128)S(1)}, u32[]{:S(2)}, u32[]{:S(2)}) collective-permute-start(f32[1,4,128,128]{3,2,1,0:T(8,128)S(1)} %collective-permute-done.6), channel_id=1, source_target_pairs={{0,192},{64,0},{128,64},{192,128},{1,193},{65,1},{129,65},{193,129... | collective-permute-start | bytes 786440 | tf_op jit(solution)/shard_map/ppermute | solution.py:136
  28.1 16.9 %collective-permute-start.8 = (f32[1,4,128,128]{3,2,1,0:T(8,128)S(1)}, f32[1,4,128,128]{3,2,1,0:T(8,128)S(1)}, u32[]{:S(2)}, u32[]{:S(2)}) collective-permute-start(f32[1,4,128,128]{3,2,1,0:T(8,128)S(1)} %collective-permute-done), channel_id=1, source_target_pairs={{0,64},{64,128},{128,192},{192,0},{1,65},{65,129},{129,193},{193,1... | collective-permute-start | bytes 786440 | tf_op jit(solution)/shard_map/ppermute | solution.py:136
  28.8 16.6 %collective-permute-start.7 = (f32[1,4,128,128]{3,2,1,0:T(8,128)S(1)}, f32[1,4,128,128]{3,2,1,0:T(8,128)S(1)}, u32[]{:S(2)}, u32[]{:S(2)}) collective-permute-start(f32[1,4,128,128]{3,2,1,0:T(8,128)S(1)} %collective-permute-done.6), channel_id=1, source_target_pairs={{0,32},{32,0},{1,33},{33,1},{2,34},{34,2},{3,35},{35,3},{4,36},{36... | collective-permute-start | bytes 786440 | tf_op jit(solution)/shard_map/ppermute | solution.py:136
  30.3 15.1 %collective-permute-start.3 = (f32[1,4,128,128]{3,2,1,0:T(8,128)S(1)}, f32[1,4,128,128]{3,2,1,0:T(8,128)S(1)}, u32[]{:S(2)}, u32[]{:S(2)}) collective-permute-start(f32[1,4,128,128]{3,2,1,0:T(8,128)S(1)} %collective-permute-done.2), channel_id=1, source_target_pairs={{0,32},{32,0},{1,33},{33,1},{2,34},{34,2},{3,35},{35,3},{4,36},{36... | collective-permute-start | bytes 786440 | tf_op jit(solution)/shard_map/ppermute | solution.py:136
  34.1 11.2 %collective-permute-start.1 = (f32[1,4,128,128]{3,2,1,0:T(8,128)S(1)}, f32[1,4,128,128]{3,2,1,0:T(8,128)S(1)}, u32[]{:S(2)}, u32[]{:S(2)}) collective-permute-start(f32[1,4,128,128]{3,2,1,0:T(8,128)S(1)} %collective-permute-done), channel_id=1, source_target_pairs={{0,32},{32,0},{1,33},{33,1},{2,34},{34,2},{3,35},{35,3},{4,36},{36... | collective-permute-start | bytes 786440 | tf_op jit(solution)/shard_map/ppermute | solution.py:136
  41.2 4.2 %collective-permute-start.5 = (f32[1,4,128,128]{3,2,1,0:T(8,128)S(1)}, f32[1,4,128,128]{3,2,1,0:T(8,128)S(1)}, u32[]{:S(2)}, u32[]{:S(2)}) collective-permute-start(f32[1,4,128,128]{3,2,1,0:T(8,128)S(1)} %collective-permute-done.4), channel_id=1, source_target_pairs={{0,32},{32,0},{1,33},{33,1},{2,34},{34,2},{3,35},{35,3},{4,36},{36... | collective-permute-start | bytes 786440 | tf_op jit(solution)/shard_map/ppermute | solution.py:136
  45.1 2.7 %collective-permute-start.10 = (f32[4,4,128,128]{3,2,1,0:T(8,128)S(1)}, f32[4,4,128,128]{3,2,1,0:T(8,128)S(1)}, u32[]{:S(2)}, u32[]{:S(2)}) collective-permute-start(f32[4,4,128,128]{3,2,1,0:T(8,128)S(1)} %pad_maximum_fusion), channel_id=1, source_target_pairs={{0,32},{32,0},{1,33},{33,1},{2,34},{34,2},{3,35},{35,3},{4,36},{36... | collective-permute-start | bytes 3145736 | tf_op jit(solution)/shard_map/ppermute | solution.py:136
  45.4 2.5 %copy-start.5 = (bf16[256,256]{1,0:T(8,128)(2,1)S(1)}, bf16[256,256]{1,0:T(8,128)(2,1)}, u32[]{:S(2)}) copy-start(bf16[256,256]{1,0:T(8,128)(2,1)} %constant.102.clone.wy_ref) | copy-start | bytes 393220
  45.4 2.5 %copy-start.6 = (bf16[256,256]{1,0:T(8,128)(2,1)S(1)}, bf16[256,256]{1,0:T(8,128)(2,1)}, u32[]{:S(2)}) copy-start(bf16[256,256]{1,0:T(8,128)(2,1)} %constant.101.clone.wz_ref) | copy-start | bytes 393220
  51.9 59.1 %copy-start.1 = (bf16[256,256]{1,0:T(8,128)(2,1)S(1)}, bf16[256,256]{1,0:T(8,128)(2,1)}, u32[]{:S(2)}) copy-start(bf16[256,256]{1,0:T(8,128)(2,1)} %constant.104.clone.wxi_ref) | copy-start | bytes 393220
  51.9 59.1 %copy-start.2 = (bf16[256,256]{1,0:T(8,128)(2,1)S(1)}, bf16[256,256]{1,0:T(8,128)(2,1)}, u32[]{:S(2)}) copy-start(bf16[256,256]{1,0:T(8,128)(2,1)} %constant.103.clone.wx_ref) | copy-start | bytes 393220
  114.3 54.1 %copy-start.3 = (bf16[256,256]{1,0:T(8,128)(2,1)S(1)}, bf16[256,256]{1,0:T(8,128)(2,1)}, u32[]{:S(2)}) copy-start(bf16[256,256]{1,0:T(8,128)(2,1)} %constant.106.clone.wy_ref) | copy-start | bytes 393220
  114.3 54.0 %copy-start.4 = (bf16[256,256]{1,0:T(8,128)(2,1)S(1)}, bf16[256,256]{1,0:T(8,128)(2,1)}, u32[]{:S(2)}) copy-start(bf16[256,256]{1,0:T(8,128)(2,1)} %constant.105.clone.wz_ref) | copy-start | bytes 393220

commit v8 on v7

--- a/solution.py
+++ b/solution.py
@@ -57,13 +57,15 @@
     return product[:, :columns] + product[:, columns:]
 
 
-def outward(place_ref, core_ref, own_ref, mine_ref, other_ref, wz_ref, wy_ref, out_ref, chosen_ref):
+def outward(groups, cores, owner_ref, index_ref, own_ref, mine_ref, other_ref, wz_ref, wy_ref, out_ref, chosen_ref):
     held, planes, ny, nz = own_ref.shape
     width = planes * held
 
     def one(r, carry):
-        same = core_ref[r] == 0
-        place = place_ref[r]
+        owner = owner_ref[r]
+        same = lax.rem(owner + lax.axis_index("core"), cores) == 0
+        offset = lax.rem(lax.div(owner, cores) + groups - lax.axis_index("zh"), groups)
+        place = jnp.where(offset == 0, groups - 1, jnp.where(offset == groups - 1, 0, offset)) * held + index_ref[r]
         done = []
         for p in range(planes):
             chosen = jnp.where(same, mine_ref[place, p], other_ref[place, p])
@@ -83,16 +85,18 @@
     return jnp.where(row > length // 2, row - length // 2, row).astype(jnp.float32)
 
 
-def middle(spot_ref, wx_ref, wxi_ref, in_ref, out_ref, kernel_ref):
+def middle(wx_ref, wxi_ref, in_ref, out_ref, kernel_ref):
     slabs, own_y, step, nz = in_ref.shape
     _, nx, _ = kernel_ref.shape
     held, planes = 2, nx // slabs
     width = planes * held
+    here = lax.axis_index(GRID)
+    spot = lax.rem(here, 4) * (slabs // 4) + lax.rem(lax.div(here, 4), 4) * (slabs // 16) + lax.div(here, 16)
     scale = (2.0 * math.pi / CELL_EDGE) ** 2
     freq_x = frequency(lax.broadcasted_iota(jnp.int32, (nx, nz), 0), nx)
     freq_z = frequency(lax.broadcasted_iota(jnp.int32, (nx, nz), 1), nz)
     for q in range(own_y):
-        freq_y = frequency(jnp.full((nx, nz), spot_ref[0] * own_y + q, jnp.int32), slabs * own_y)
+        freq_y = frequency(jnp.full((nx, nz), spot * own_y + q, jnp.int32), slabs * own_y)
         squared = scale * (freq_x**2 + freq_y**2 + freq_z**2)
         guarded = jnp.where(squared > 0, squared, 1.0)
         kernel_ref[q] = jnp.where(squared > 0, 4.0 * math.pi / guarded, 0.0)
@@ -158,15 +162,7 @@
     order = np.arange(grid).reshape(-1, 4, 4).transpose(2, 1, 0).reshape(grid)
     tx = tx.reshape(nx, grid, planes)[:, order].transpose(0, 2, 1).reshape(nx, nx)
     groups, cores = lax.axis_size("zh"), lax.axis_size("core")
-    offset = (band_owner // cores - lax.axis_index("zh")) % groups
-    place = jnp.where(offset == 0, groups - 1, jnp.where(offset == groups - 1, 0, offset)) * held + block_index
-    core_off = (band_owner + lax.axis_index("core")) % cores
-
-    here = lax.axis_index(GRID)
-    spot = here % 4 * (grid // 4) + here // 4 % 4 * (grid // 16) + here // 16
-
     mine, other = every_orbital(orbitals)
-    spot, other = lax.optimization_barrier((jnp.full((1,), spot, jnp.int32), other))
     cells = rounds * held * planes * ny * nz
     vmem, smem = pl.BlockSpec(memory_space=pltpu.VMEM), pl.BlockSpec(memory_space=pltpu.SMEM)
 
@@ -188,9 +184,9 @@
 
     sent = (ny, rounds * width, nz)
     half, chosen = call(
-        outward,
+        lambda *refs: outward(groups, cores, *refs),
         [sent, (rounds, planes, ny, nz)],
-        (place, core_off),
+        (band_owner, block_index),
         (orbitals, mine, other, right_table(tz.T), left_table(ty)),
     )
     strips = (grid, own_y, rounds * width, nz)
@@ -198,7 +194,7 @@
     (spec,) = call(
         middle,
         [strips],
-        (spot,),
+        (),
         (left_table(tx), left_table(tx.T), spec),
         [pltpu.VMEM((own_y, nx, nz), jnp.float32)],
     )

time: 173 us -> 172 us (level)
  transfers between devices with their start and end apart: 11 -> 11, of which waited for: 6 -> 6; matrix products, arithmetic and copies ran while one was open for 1% -> 0% of each run, Pallas kernels for 0% -> 0%
where the time goes in v8:
time: 172 us
  blocking collectives  113 us (66%)
  waiting for transfers between devices  30.9 us (18%)
  starting transfers between devices  15.3 us (9%)
  Pallas kernels  11.1 us (6%)
    all_to_all x2, blocking collectives, exchange(): lax.all_to_all(array, GRID, split_axis=0, concat_axis=0, tiled=True, axis...  113 us
    ppermute x11, waiting for transfers between devices, rotated(): lax.ppermute(array, axis, [(i, (i + step) % size) for i in range(size)])  30.9 us
    ppermute x11, starting transfers between devices, rotated(): lax.ppermute(array, axis, [(i, (i + step) % size) for i in range(size)])  15.3 us
    pallas_call x3, Pallas kernels, call(): pl.pallas_call(body, in_specs=[smem] * len(scalars) + [vmem] * len(operan...  11.1 us
  transfers between devices with their start and end apart: 11, of which 6 were waited for; matrix products, arithmetic and copies ran while one was open for 0% of the time, Pallas kernels for 0%

profile of v8, /device:TPU:8, one launch (start us, length us, event | category | flops | bytes accessed | tf_op | source)
XLA Modules:
  0.0 172.2 jit_solution(11432541603950090771)
XLA Ops:
  0.0 1.1 fusion
  1.1 6.4 %collective-permute-start.3 = (f32[1,4,128,128]{3,2,1,0:T(8,128)S(1)}, f32[1,4,128,128]{3,2,1,0:T(8,128)S(1)}, u32[]{:S(2)}, u32[]{:S(2)}) collective-permute-start(f32[1,4,128,128]{3,2,1,0:T(8,128)S(1)} %get-tuple-element.9), channel_id=1, source_target_pairs={{0,192},{64,0},{128,64},{192,128},{1,193},{65,1},{129,65},{193,129... | collective-permute-start | bytes 786440 | tf_op jit(solution)/shard_map/ppermute | solution.py:140
  7.5 0.0 collective-permute-start
  7.5 1.5 collective-permute-start.1
  9.1 2.6 %collective-permute-start.2 = (f32[1,4,128,128]{3,2,1,0:T(8,128)S(1)}, f32[1,4,128,128]{3,2,1,0:T(8,128)S(1)}, u32[]{:S(2)}, u32[]{:S(2)}) collective-permute-start(f32[1,4,128,128]{3,2,1,0:T(8,128)S(1)} %get-tuple-element.10), channel_id=1, source_target_pairs={{0,192},{64,0},{128,64},{192,128},{1,193},{65,1},{129,65},{193,129... | collective-permute-start | bytes 786440 | tf_op jit(solution)/shard_map/ppermute | solution.py:140
  11.7 11.7 %collective-permute-done.3 = f32[1,4,128,128]{3,2,1,0:T(8,128)S(1)} collective-permute-done((f32[1,4,128,128]{3,2,1,0:T(8,128)S(1)}, f32[1,4,128,128]{3,2,1,0:T(8,128)S(1)}, u32[]{:S(2)}, u32[]{:S(2)}) %collective-permute-start.3) | collective-permute-done | bytes 262176 | tf_op jit(solution)/shard_map/ppermute | solution.py:140
  23.4 4.7 %collective-permute-start.5 = (f32[1,4,128,128]{3,2,1,0:T(8,128)S(1)}, f32[1,4,128,128]{3,2,1,0:T(8,128)S(1)}, u32[]{:S(2)}, u32[]{:S(2)}) collective-permute-start(f32[1,4,128,128]{3,2,1,0:T(8,128)S(1)} %collective-permute-done.3), channel_id=1, source_target_pairs={{0,192},{64,0},{128,64},{192,128},{1,193},{65,1},{129,65},{193,129... | collective-permute-start | bytes 786440 | tf_op jit(solution)/shard_map/ppermute | solution.py:140
  28.1 0.0 collective-permute-done
  28.1 2.2 %collective-permute-done.1 = f32[1,4,128,128]{3,2,1,0:T(8,128)S(1)} collective-permute-done((f32[1,4,128,128]{3,2,1,0:T(8,128)S(1)}, f32[1,4,128,128]{3,2,1,0:T(8,128)S(1)}, u32[]{:S(2)}, u32[]{:S(2)}) %collective-permute-start.1) | collective-permute-done | bytes 262176 | tf_op jit(solution)/shard_map/ppermute | solution.py:140
  30.3 0.0 collective-permute-start.7
  30.3 3.8 %collective-permute-done.2 = f32[1,4,128,128]{3,2,1,0:T(8,128)S(1)} collective-permute-done((f32[1,4,128,128]{3,2,1,0:T(8,128)S(1)}, f32[1,4,128,128]{3,2,1,0:T(8,128)S(1)}, u32[]{:S(2)}, u32[]{:S(2)}) %collective-permute-start.2) | collective-permute-done | bytes 262176 | tf_op jit(solution)/shard_map/ppermute | solution.py:140
  34.1 7.1 %collective-permute-done.5 = f32[1,4,128,128]{3,2,1,0:T(8,128)S(1)} collective-permute-done((f32[1,4,128,128]{3,2,1,0:T(8,128)S(1)}, f32[1,4,128,128]{3,2,1,0:T(8,128)S(1)}, u32[]{:S(2)}, u32[]{:S(2)}) %collective-permute-start.5) | collective-permute-done | bytes 262176 | tf_op jit(solution)/shard_map/ppermute | solution.py:140
  41.2 3.8 %collective-permute-done.4 = f32[1,4,128,128]{3,2,1,0:T(8,128)S(1)} collective-permute-done((f32[1,4,128,128]{3,2,1,0:T(8,128)S(1)}, f32[1,4,128,128]{3,2,1,0:T(8,128)S(1)}, u32[]{:S(2)}, u32[]{:S(2)}) %collective-permute-start.4) | collective-permute-done | bytes 262176 | tf_op jit(solution)/shard_map/ppermute | solution.py:140
  45.0 0.1 pad_maximum_fusion
  45.1 0.1 collective-permute-start.10
  45.2 0.0 collective-permute-done.6
  45.3 0.0 collective-permute-done.7
  45.4 0.0 copy-start.3
  45.4 0.0 copy-start.4
  45.4 0.0 copy-start.7
  45.4 0.0 copy-start.8
  45.5 2.3 %collective-permute-done.10 = f32[4,4,128,128]{3,2,1,0:T(8,128)S(1)} collective-permute-done((f32[4,4,128,128]{3,2,1,0:T(8,128)S(1)}, f32[4,4,128,128]{3,2,1,0:T(8,128)S(1)}, u32[]{:S(2)}, u32[]{:S(2)}) %collective-permute-start.10) | collective-permute-done | bytes 1048608 | tf_op jit(solution)/shard_map/ppermute | solution.py:140
  47.8 0.1 constant_dynamic-update-slice_fusion.7.refs_4_
  48.0 3.9 %shard_map.91 = (f32[128,64,128]{2,1,0:T(8,128)S(1)}, f32[8,4,128,128]{3,2,1,0:T(8,128)S(1)}) custom-call(s32[8]{0:T(128)S(1)} %copy-done.3, s32[8]{0:T(128)S(1)} %copy-done.4, f32[2,4,128,128]{3,2,1,0:T(8,128)S(1)} %copy-done, f32[8,4,128,128]{3,2,1,0:T(8,128)S(1)} %constant_dynamic-update-slice_fusion.refs_3_, ...), custom_call_target="tpu_custom_call" | custom-call | flops 2147483648 | bytes 8388608 | tf_op jit(solution)/shard_map/pallas_call | solution.py:170
  51.9 0.0 copy-start.1
  51.9 0.0 copy-start.2
  51.9 59.1 %all_to_all.10 = f32[128,64,128]{2,1,0:T(8,128)S(1)} all-to-all(f32[128,64,128]{2,1,0:T(8,128)S(1)} %get-tuple-element.7), channel_id=1, replica_groups={{0,16,4,20,8,24,12,28,1,17,5,21,9,25,13,29,2,18,6,22,10,26,14,30,3,19,7..., dimensions={0} | all-to-all | bytes 8388608 | tf_op jit(solution)/shard_map/all_to_all | solution.py:181
  111.0 3.2 %shard_map.92 = f32[32,4,64,128]{3,2,1,0:T(8,128)S(1)} custom-call(bf16[256,256]{1,0:T(8,128)(2,1)S(1)} %copy-done.2, bf16[256,256]{1,0:T(8,128)(2,1)S(1)} %copy-done.1, f32[32,4,64,128]{3,2,1,0:T(8,128)S(1)} %bitcast.2), custom_call_target="tpu_custom_call" | custom-call | flops 2147483648 | bytes 8388608 | tf_op jit(solution)/shard_map/pallas_call | solution.py:170
  114.1 0.0 copy-start.5
  114.2 0.0 copy-start.6
  114.2 54.0 %all_to_all.11.in_ref = f32[128,64,128]{2,1,0:T(8,128)S(1)} all-to-all(f32[128,64,128]{2,1,0:T(8,128)S(1)} %bitcast.3), channel_id=1, replica_groups={{0,16,4,20,8,24,12,28,1,17,5,21,9,25,13,29,2,18,6,22,10,26,14,30,3,19,7..., dimensions={0} | all-to-all | bytes 8388608 | tf_op jit(solution)/shard_map/all_to_all | solution.py:181
  168.2 4.0 %shard_map.93 = f32[2,4,128,128]{3,2,1,0:T(8,128)} custom-call(f32[128,64,128]{2,1,0:T(8,128)S(1)} %all_to_all.11.in_ref, f32[8,4,128,128]{3,2,1,0:T(8,128)S(1)} %get-tuple-element.8.chosen_ref, bf16[256,256]{1,0:T(8,128)(2,1)S(1)} %copy-done.6, bf16[256,256]{1,0:T(8,128)(2,1)S(1)} %copy-done.5), custom_call_target="tpu_custom_call" | custom-call | flops 2147483648 | bytes 8388608 | tf_op jit(solution)/shard_map/pallas_call | solution.py:170
  (27 shorter events, 0.3 us)
Async XLA Ops:
  0.0 45.0 %copy-start = (f32[2,4,128,128]{3,2,1,0:T(8,128)S(1)}, f32[2,4,128,128]{3,2,1,0:T(8,128)}, u32[]{:S(2)}) copy-start(f32[2,4,128,128]{3,2,1,0:T(8,128)} %refs_2_.1) | copy-start | bytes 1572868
  1.1 22.2 %collective-permute-start.3 = (f32[1,4,128,128]{3,2,1,0:T(8,128)S(1)}, f32[1,4,128,128]{3,2,1,0:T(8,128)S(1)}, u32[]{:S(2)}, u32[]{:S(2)}) collective-permute-start(f32[1,4,128,128]{3,2,1,0:T(8,128)S(1)} %get-tuple-element.9), channel_id=1, source_target_pairs={{0,192},{64,0},{128,64},{192,128},{1,193},{65,1},{129,65},{193,129... | collective-permute-start | bytes 786440 | tf_op jit(solution)/shard_map/ppermute | solution.py:140
  7.5 20.6 %collective-permute-start = (f32[1,4,128,128]{3,2,1,0:T(8,128)S(1)}, f32[1,4,128,128]{3,2,1,0:T(8,128)S(1)}, u32[]{:S(2)}, u32[]{:S(2)}) collective-permute-start(f32[1,4,128,128]{3,2,1,0:T(8,128)S(1)} %get-tuple-element.10), channel_id=1, source_target_pairs={{0,64},{64,128},{128,192},{192,0},{1,65},{65,129},{129,193},{193,1... | collective-permute-start | bytes 786440 | tf_op jit(solution)/shard_map/ppermute | solution.py:140
  7.5 22.8 %collective-permute-start.1 = (f32[1,4,128,128]{3,2,1,0:T(8,128)S(1)}, f32[1,4,128,128]{3,2,1,0:T(8,128)S(1)}, u32[]{:S(2)}, u32[]{:S(2)}) collective-permute-start(f32[1,4,128,128]{3,2,1,0:T(8,128)S(1)} %get-tuple-element.9), channel_id=1, source_target_pairs={{0,64},{64,128},{128,192},{192,0},{1,65},{65,129},{129,193},{193,1... | collective-permute-start | bytes 786440 | tf_op jit(solution)/shard_map/ppermute | solution.py:140
  9.1 25.0 %collective-permute-start.2 = (f32[1,4,128,128]{3,2,1,0:T(8,128)S(1)}, f32[1,4,128,128]{3,2,1,0:T(8,128)S(1)}, u32[]{:S(2)}, u32[]{:S(2)}) collective-permute-start(f32[1,4,128,128]{3,2,1,0:T(8,128)S(1)} %get-tuple-element.10), channel_id=1, source_target_pairs={{0,192},{64,0},{128,64},{192,128},{1,193},{65,1},{129,65},{193,129... | collective-permute-start | bytes 786440 | tf_op jit(solution)/shard_map/ppermute | solution.py:140
  23.4 17.8 %collective-permute-start.5 = (f32[1,4,128,128]{3,2,1,0:T(8,128)S(1)}, f32[1,4,128,128]{3,2,1,0:T(8,128)S(1)}, u32[]{:S(2)}, u32[]{:S(2)}) collective-permute-start(f32[1,4,128,128]{3,2,1,0:T(8,128)S(1)} %collective-permute-done.3), channel_id=1, source_target_pairs={{0,192},{64,0},{128,64},{192,128},{1,193},{65,1},{129,65},{193,129... | collective-permute-start | bytes 786440 | tf_op jit(solution)/shard_map/ppermute | solution.py:140
  28.1 16.9 %collective-permute-start.4 = (f32[1,4,128,128]{3,2,1,0:T(8,128)S(1)}, f32[1,4,128,128]{3,2,1,0:T(8,128)S(1)}, u32[]{:S(2)}, u32[]{:S(2)}) collective-permute-start(f32[1,4,128,128]{3,2,1,0:T(8,128)S(1)} %collective-permute-done), channel_id=1, source_target_pairs={{0,64},{64,128},{128,192},{192,0},{1,65},{65,129},{129,193},{193,1... | collective-permute-start | bytes 786440 | tf_op jit(solution)/shard_map/ppermute | solution.py:140
  28.1 17.4 %collective-permute-start.9 = (f32[1,4,128,128]{3,2,1,0:T(8,128)S(1)}, f32[1,4,128,128]{3,2,1,0:T(8,128)S(1)}, u32[]{:S(2)}, u32[]{:S(2)}) collective-permute-start(f32[1,4,128,128]{3,2,1,0:T(8,128)S(1)} %collective-permute-done.3), channel_id=1, source_target_pairs={{0,32},{32,0},{1,33},{33,1},{2,34},{34,2},{3,35},{35,3},{4,36},{36... | collective-permute-start | bytes 786440 | tf_op jit(solution)/shard_map/ppermute | solution.py:140
  30.3 15.1 %collective-permute-start.7 = (f32[1,4,128,128]{3,2,1,0:T(8,128)S(1)}, f32[1,4,128,128]{3,2,1,0:T(8,128)S(1)}, u32[]{:S(2)}, u32[]{:S(2)}) collective-permute-start(f32[1,4,128,128]{3,2,1,0:T(8,128)S(1)} %collective-permute-done.1), channel_id=1, source_target_pairs={{0,32},{32,0},{1,33},{33,1},{2,34},{34,2},{3,35},{35,3},{4,36},{36... | collective-permute-start | bytes 786440 | tf_op jit(solution)/shard_map/ppermute | solution.py:140
  34.1 11.2 %collective-permute-start.6 = (f32[1,4,128,128]{3,2,1,0:T(8,128)S(1)}, f32[1,4,128,128]{3,2,1,0:T(8,128)S(1)}, u32[]{:S(2)}, u32[]{:S(2)}) collective-permute-start(f32[1,4,128,128]{3,2,1,0:T(8,128)S(1)} %collective-permute-done), channel_id=1, source_target_pairs={{0,32},{32,0},{1,33},{33,1},{2,34},{34,2},{3,35},{35,3},{4,36},{36... | collective-permute-start | bytes 786440 | tf_op jit(solution)/shard_map/ppermute | solution.py:140
  41.2 4.2 %collective-permute-start.8 = (f32[1,4,128,128]{3,2,1,0:T(8,128)S(1)}, f32[1,4,128,128]{3,2,1,0:T(8,128)S(1)}, u32[]{:S(2)}, u32[]{:S(2)}) collective-permute-start(f32[1,4,128,128]{3,2,1,0:T(8,128)S(1)} %collective-permute-done.2), channel_id=1, source_target_pairs={{0,32},{32,0},{1,33},{33,1},{2,34},{34,2},{3,35},{35,3},{4,36},{36... | collective-permute-start | bytes 786440 | tf_op jit(solution)/shard_map/ppermute | solution.py:140
  45.1 2.7 %collective-permute-start.10 = (f32[4,4,128,128]{3,2,1,0:T(8,128)S(1)}, f32[4,4,128,128]{3,2,1,0:T(8,128)S(1)}, u32[]{:S(2)}, u32[]{:S(2)}) collective-permute-start(f32[4,4,128,128]{3,2,1,0:T(8,128)S(1)} %pad_maximum_fusion), channel_id=1, source_target_pairs={{0,32},{32,0},{1,33},{33,1},{2,34},{34,2},{3,35},{35,3},{4,36},{36... | collective-permute-start | bytes 3145736 | tf_op jit(solution)/shard_map/ppermute | solution.py:140
  45.4 2.5 %copy-start.3 = (s32[8]{0:T(128)S(1)}, s32[8]{0:T(128)}, u32[]{:S(2)}) copy-start(s32[8]{0:T(128)} %refs_0_.1) | copy-start | bytes 100
  45.4 2.5 %copy-start.4 = (s32[8]{0:T(128)S(1)}, s32[8]{0:T(128)}, u32[]{:S(2)}) copy-start(s32[8]{0:T(128)} %refs_1_.1) | copy-start | bytes 100
  45.4 2.5 %copy-start.7 = (bf16[256,256]{1,0:T(8,128)(2,1)S(1)}, bf16[256,256]{1,0:T(8,128)(2,1)}, u32[]{:S(2)}) copy-start(bf16[256,256]{1,0:T(8,128)(2,1)} %constant.13.clone.refs_6_) | copy-start | bytes 393220
  45.4 2.5 %copy-start.8 = (bf16[256,256]{1,0:T(8,128)(2,1)S(1)}, bf16[256,256]{1,0:T(8,128)(2,1)}, u32[]{:S(2)}) copy-start(bf16[256,256]{1,0:T(8,128)(2,1)} %constant.12.clone.refs_5_) | copy-start | bytes 393220
  51.9 59.1 %copy-start.1 = (bf16[256,256]{1,0:T(8,128)(2,1)S(1)}, bf16[256,256]{1,0:T(8,128)(2,1)}, u32[]{:S(2)}) copy-start(bf16[256,256]{1,0:T(8,128)(2,1)} %constant.15.clone.wxi_ref) | copy-start | bytes 393220
  51.9 59.1 %copy-start.2 = (bf16[256,256]{1,0:T(8,128)(2,1)S(1)}, bf16[256,256]{1,0:T(8,128)(2,1)}, u32[]{:S(2)}) copy-start(bf16[256,256]{1,0:T(8,128)(2,1)} %constant.14.clone.wx_ref) | copy-start | bytes 393220
  114.1 54.0 %copy-start.5 = (bf16[256,256]{1,0:T(8,128)(2,1)S(1)}, bf16[256,256]{1,0:T(8,128)(2,1)}, u32[]{:S(2)}) copy-start(bf16[256,256]{1,0:T(8,128)(2,1)} %constant.17.clone.wy_ref) | copy-start | bytes 393220
  114.2 54.0 %copy-start.6 = (bf16[256,256]{1,0:T(8,128)(2,1)S(1)}, bf16[256,256]{1,0:T(8,128)(2,1)}, u32[]{:S(2)}) copy-start(bf16[256,256]{1,0:T(8,128)(2,1)} %constant.16.clone.wz_ref) | copy-start | bytes 393220
